TPU v7x, 32 devices: a whole 2x2x4 slice. The times are simulated.
32 devices in a mesh: rep: 4 (over x, core), shard: 8 (over z, y).
Axes of the slice: x: 2, y: 2, z: 4, core: 2. Of those that a mesh axis runs over, the one named last changes fastest.
Arguments:
- tokens: bfloat16 [32768, 1024], P(('rep', 'shard')), may hold values from -6 to 6
- w_query: bfloat16 [1024, 1024], P('shard'), may hold values from -0.1875 to 0.1875
- w_key: bfloat16 [1024, 1024], P('shard'), may hold values from -0.1875 to 0.1875
- w_value: bfloat16 [1024, 1024], P('shard'), may hold values from -0.1875 to 0.1875
- b_query: bfloat16 [1024], P('shard'), may hold values from -3 to 3
- b_value: bfloat16 [1024], P('shard'), may hold values from -3 to 3
- w_out: bfloat16 [1024, 1024], P('shard'), may hold values from -3 to 3
- b_out: bfloat16 [1024], P('shard'), may hold values from -3 to 3
- gain_one: bfloat16 [1024], P('shard'), may hold values from 0.5 to 1.5
- shift_one: bfloat16 [1024], P('shard'), may hold values from -3 to 3
- w_inner: bfloat16 [1024, 4096], P('shard'), may hold values from -0.1875 to 0.1875
- b_inner: bfloat16 [4096], P('shard'), may hold values from -3 to 3
- w_outer: bfloat16 [4096, 1024], P('shard'), may hold values from -0.09375 to 0.09375
- b_outer: bfloat16 [1024], P('shard'), may hold values from -3 to 3
- gain_two: bfloat16 [1024], P('shard'), may hold values from 0.5 to 1.5
- shift_two: bfloat16 [1024], P('shard'), may hold values from -3 to 3
- cotangent: bfloat16 [32768, 1024], P(('rep', 'shard')), may hold values from -6 to 6
Outputs:
- output: bfloat16 [32768, 1024], P(('rep', 'shard'))
- d_tokens: bfloat16 [32768, 1024], P(('rep', 'shard'))
- grad_w_query: float32 [1024, 1024], P('shard')
- grad_w_key: float32 [1024, 1024], P('shard')
- grad_w_value: float32 [1024, 1024], P('shard')
- grad_b_query: float32 [1024], P('shard')
- grad_b_value: float32 [1024], P('shard')
- grad_w_out: float32 [1024, 1024], P('shard')
- grad_b_out: float32 [1024], P('shard')
- grad_gain_one: float32 [1024], P('shard')
- grad_shift_one: float32 [1024], P('shard')
- grad_w_inner: float32 [1024, 4096], P('shard')
- grad_b_inner: float32 [4096], P('shard')
- grad_w_outer: float32 [4096, 1024], P('shard')
- grad_b_outer: float32 [1024], P('shard')
- grad_gain_two: float32 [1024], P('shard')
- grad_shift_two: float32 [1024], P('shard')
All inputs are finite; a program needn't handle non-finite values.
Results may differ from a plain program's by a relative error of at most 0.017.
Values may be sent and summed in bfloat16 or wider, within the bound.
No kernel may reach another device: no remote copies, remote signals or barrier semaphores. Data moves between devices by JAX's collectives and lax.ppermute only.
A program may use at most 192 MiB of HBM per device.

v0:
```python
import jax
import jax.numpy as jnp
from jax import lax
from jax.sharding import PartitionSpec as P

D = 1024
H = 16
DH = 64
SEQ = 512


def project(left, right):
    return jnp.dot(left, right, preferred_element_type=jnp.float32)


def gram(left, right):
    return lax.dot_general(
        left, right, (((0,), (0,)), ((), ())), preferred_element_type=jnp.float32
    )


def against(left, right):
    return lax.dot_general(
        left, right, (((1,), (1,)), ((), ())), preferred_element_type=jnp.float32
    )


def layer_norm(values, gain, shift):
    centre = values - jnp.mean(values, axis=-1, keepdims=True)
    spread = jnp.mean(centre * centre, axis=-1, keepdims=True)
    return centre * lax.rsqrt(spread + 1e-12) * gain + shift


def smooth(values):
    return jax.nn.gelu(values, approximate=False)


def column_sum(values):
    return jnp.sum(values.astype(jnp.float32), axis=0)


def attend_block(block):
    query, key, value = block
    scores = jnp.einsum("qhd,khd->hqk", query, key, preferred_element_type=jnp.float32) * 0.125
    top = jnp.max(scores, axis=-1, keepdims=True)
    expo = jnp.exp(scores - top)
    total = jnp.sum(expo, axis=-1, keepdims=True)
    probs_low = (expo / total).astype(jnp.bfloat16)
    attended = jnp.einsum("hqk,khd->qhd", probs_low, value, preferred_element_type=jnp.float32)
    return (attended, (top + jnp.log(total))[..., 0])


def attend_back(block):
    query, key, value, d_attended, log_total = block
    scores = jnp.einsum("qhd,khd->hqk", query, key, preferred_element_type=jnp.float32) * 0.125
    probs = jnp.exp(scores - log_total[..., None])
    probs_low = probs.astype(jnp.bfloat16)
    d_value = jnp.einsum("hqk,qhd->khd", probs_low, d_attended, preferred_element_type=jnp.float32)
    d_probs = jnp.einsum("qhd,khd->hqk", d_attended, value, preferred_element_type=jnp.float32)
    inner = jnp.sum(probs * d_probs, axis=-1, keepdims=True)
    d_scores = (probs * (d_probs - inner)).astype(jnp.bfloat16)
    d_query = jnp.einsum("hqk,khd->qhd", d_scores, key, preferred_element_type=jnp.float32) * 0.125
    d_key = jnp.einsum("hqk,qhd->khd", d_scores, query, preferred_element_type=jnp.float32) * 0.125
    return (d_query.astype(jnp.bfloat16), d_key.astype(jnp.bfloat16), d_value.astype(jnp.bfloat16))


def shards(
    tokens,
    w_query,
    w_key,
    w_value,
    b_query,
    b_value,
    w_out,
    b_out,
    gain_one,
    shift_one,
    w_inner,
    b_inner,
    w_outer,
    b_outer,
    gain_two,
    shift_two,
    cotangent,
):
    count = tokens.shape[0]
    layout = (count // SEQ, SEQ, H, DH)
    (
        whole_query,
        whole_key,
        whole_value,
        bias_query,
        bias_value,
        whole_out,
        bias_out,
        gain_first,
        shift_first,
    ) = (
        lax.all_gather(w_query, "shard", axis=0, tiled=True),
        lax.all_gather(w_key, "shard", axis=0, tiled=True),
        lax.all_gather(w_value, "shard", axis=0, tiled=True),
        lax.all_gather(b_query, "shard", axis=0, tiled=True),
        lax.all_gather(b_value, "shard", axis=0, tiled=True),
        lax.all_gather(w_out, "shard", axis=0, tiled=True),
        lax.all_gather(b_out, "shard", axis=0, tiled=True),
        lax.all_gather(gain_one, "shard", axis=0, tiled=True),
        lax.all_gather(shift_one, "shard", axis=0, tiled=True),
    )
    query_low = (
        (project(tokens, whole_query) + bias_query.astype(jnp.float32))
        .astype(jnp.bfloat16)
        .reshape(layout)
    )
    key_low = project(tokens, whole_key).astype(jnp.bfloat16).reshape(layout)
    value_low = (
        (project(tokens, whole_value) + bias_value.astype(jnp.float32))
        .astype(jnp.bfloat16)
        .reshape(layout)
    )
    attended, log_total = lax.map(attend_block, (query_low, key_low, value_low))
    attended_low = attended.reshape(count, D).astype(jnp.bfloat16)
    branch = project(attended_low, whole_out) + bias_out.astype(jnp.float32)
    first, first_pull = jax.vjp(
        layer_norm,
        tokens.astype(jnp.float32) + branch,
        gain_first.astype(jnp.float32),
        shift_first.astype(jnp.float32),
    )
    first_low = first.astype(jnp.bfloat16)
    whole_inner, bias_inner, whole_outer, bias_outer, gain_second, shift_second = (
        lax.all_gather(w_inner, "shard", axis=0, tiled=True),
        lax.all_gather(b_inner, "shard", axis=0, tiled=True),
        lax.all_gather(w_outer, "shard", axis=0, tiled=True),
        lax.all_gather(b_outer, "shard", axis=0, tiled=True),
        lax.all_gather(gain_two, "shard", axis=0, tiled=True),
        lax.all_gather(shift_two, "shard", axis=0, tiled=True),
    )
    pre = project(first_low, whole_inner) + bias_inner.astype(jnp.float32)
    active, gelu_pull = jax.vjp(smooth, pre)
    active_low = active.astype(jnp.bfloat16)
    second = first + project(active_low, whole_outer) + bias_outer.astype(jnp.float32)
    output, second_pull = jax.vjp(
        layer_norm, second, gain_second.astype(jnp.float32), shift_second.astype(jnp.float32)
    )
    whole_inner, whole_outer = (
        lax.all_gather(w_inner, "shard", axis=0, tiled=True),
        lax.all_gather(w_outer, "shard", axis=0, tiled=True),
    )
    d_second, grad_gain_two, grad_shift_two = second_pull(cotangent.astype(jnp.float32))
    d_mid = d_second.astype(jnp.bfloat16)
    grad_w_outer = gram(active_low, d_mid)
    grad_b_outer = column_sum(d_mid)
    (d_pre,) = gelu_pull(against(d_mid, whole_outer))
    d_pre_low = d_pre.astype(jnp.bfloat16)
    grad_w_inner = gram(first_low, d_pre_low)
    grad_b_inner = column_sum(d_pre_low)
    d_first = d_second + against(d_pre_low, whole_inner)
    own_inner, own_bias_inner, own_outer, own_bias_outer, own_gain_two, own_shift_two = (
        lax.psum_scatter(grad_w_inner, "shard", scatter_dimension=0, tiled=True),
        lax.psum_scatter(grad_b_inner, "shard", scatter_dimension=0, tiled=True),
        lax.psum_scatter(grad_w_outer, "shard", scatter_dimension=0, tiled=True),
        lax.psum_scatter(grad_b_outer, "shard", scatter_dimension=0, tiled=True),
        lax.psum_scatter(grad_gain_two, "shard", scatter_dimension=0, tiled=True),
        lax.psum_scatter(grad_shift_two, "shard", scatter_dimension=0, tiled=True),
    )
    whole_query, whole_key, whole_value, whole_out = (
        lax.all_gather(w_query, "shard", axis=0, tiled=True),
        lax.all_gather(w_key, "shard", axis=0, tiled=True),
        lax.all_gather(w_value, "shard", axis=0, tiled=True),
        lax.all_gather(w_out, "shard", axis=0, tiled=True),
    )
    d_inner, grad_gain_one, grad_shift_one = first_pull(d_first)
    d_branch = d_inner.astype(jnp.bfloat16)
    grad_w_out = gram(attended_low, d_branch)
    grad_b_out = column_sum(d_branch)
    d_attended = against(d_branch, whole_out).astype(jnp.bfloat16).reshape(layout)
    d_query, d_key, d_value = lax.map(
        attend_back, (query_low, key_low, value_low, d_attended, log_total)
    )
    d_query = d_query.reshape(count, D)
    d_key = d_key.reshape(count, D)
    d_value = d_value.reshape(count, D)
    grad_w_query = gram(tokens, d_query)
    grad_w_key = gram(tokens, d_key)
    grad_w_value = gram(tokens, d_value)
    grad_b_query = column_sum(d_query)
    grad_b_value = column_sum(d_value)
    d_tokens = (
        d_inner
        + against(d_query, whole_query)
        + against(d_key, whole_key)
        + against(d_value, whole_value)
    )
    (
        own_query,
        own_key,
        own_value,
        own_bias_query,
        own_bias_value,
        own_out,
        own_bias_out,
        own_gain_one,
        own_shift_one,
    ) = (
        lax.psum_scatter(grad_w_query, "shard", scatter_dimension=0, tiled=True),
        lax.psum_scatter(grad_w_key, "shard", scatter_dimension=0, tiled=True),
        lax.psum_scatter(grad_w_value, "shard", scatter_dimension=0, tiled=True),
        lax.psum_scatter(grad_b_query, "shard", scatter_dimension=0, tiled=True),
        lax.psum_scatter(grad_b_value, "shard", scatter_dimension=0, tiled=True),
        lax.psum_scatter(grad_w_out, "shard", scatter_dimension=0, tiled=True),
        lax.psum_scatter(grad_b_out, "shard", scatter_dimension=0, tiled=True),
        lax.psum_scatter(grad_gain_one, "shard", scatter_dimension=0, tiled=True),
        lax.psum_scatter(grad_shift_one, "shard", scatter_dimension=0, tiled=True),
    )
    (
        own_query,
        own_key,
        own_value,
        own_bias_query,
        own_bias_value,
        own_out,
        own_bias_out,
        own_gain_one,
        own_shift_one,
        own_inner,
        own_bias_inner,
        own_outer,
        own_bias_outer,
        own_gain_two,
        own_shift_two,
    ) = (
        lax.psum(own_query.astype(jnp.bfloat16), "rep").astype(jnp.float32),
        lax.psum(own_key.astype(jnp.bfloat16), "rep").astype(jnp.float32),
        lax.psum(own_value.astype(jnp.bfloat16), "rep").astype(jnp.float32),
        lax.psum(own_bias_query.astype(jnp.bfloat16), "rep").astype(jnp.float32),
        lax.psum(own_bias_value.astype(jnp.bfloat16), "rep").astype(jnp.float32),
        lax.psum(own_out.astype(jnp.bfloat16), "rep").astype(jnp.float32),
        lax.psum(own_bias_out.astype(jnp.bfloat16), "rep").astype(jnp.float32),
        lax.psum(own_gain_one.astype(jnp.bfloat16), "rep").astype(jnp.float32),
        lax.psum(own_shift_one.astype(jnp.bfloat16), "rep").astype(jnp.float32),
        lax.psum(own_inner.astype(jnp.bfloat16), "rep").astype(jnp.float32),
        lax.psum(own_bias_inner.astype(jnp.bfloat16), "rep").astype(jnp.float32),
        lax.psum(own_outer.astype(jnp.bfloat16), "rep").astype(jnp.float32),
        lax.psum(own_bias_outer.astype(jnp.bfloat16), "rep").astype(jnp.float32),
        lax.psum(own_gain_two.astype(jnp.bfloat16), "rep").astype(jnp.float32),
        lax.psum(own_shift_two.astype(jnp.bfloat16), "rep").astype(jnp.float32),
    )
    return (
        output.astype(jnp.bfloat16),
        d_tokens.astype(jnp.bfloat16),
        own_query,
        own_key,
        own_value,
        own_bias_query,
        own_bias_value,
        own_out,
        own_bias_out,
        own_gain_one,
        own_shift_one,
        own_inner,
        own_bias_inner,
        own_outer,
        own_bias_outer,
        own_gain_two,
        own_shift_two,
    )


def solution(mesh):
    return jax.shard_map(
        shards,
        mesh=mesh,
        in_specs=(
            P(("rep", "shard"), None),
            P("shard", None),
            P("shard", None),
            P("shard", None),
            P("shard"),
            P("shard"),
            P("shard", None),
            P("shard"),
            P("shard"),
            P("shard"),
            P("shard", None),
            P("shard"),
            P("shard", None),
            P("shard"),
            P("shard"),
            P("shard"),
            P(("rep", "shard"), None),
        ),
        out_specs=(
            P(("rep", "shard"), None),
            P(("rep", "shard"), None),
            P("shard", None),
            P("shard", None),
            P("shard", None),
            P("shard"),
            P("shard"),
            P("shard", None),
            P("shard"),
            P("shard"),
            P("shard"),
            P("shard", None),
            P("shard"),
            P("shard", None),
            P("shard"),
            P("shard"),
            P("shard"),
        ),
        check_vma=False,
    )
```

profile of v0, /device:TPU:0, one launch (start us, length us, event | category | flops | bytes accessed | tf_op | source)
XLA Modules:
  0.0 1679.9 jit_solution(16207832645588316354)
XLA Ops:
  13.9 22.1 %all-gather.6 = bf16[8,1,128]{2,1,0:T(2,128)(2,1)S(1)} all-gather(bf16[1,1,128]{2,1,0:T(2,128)(2,1)S(1)} %bitcast.210), channel_id=1, replica_groups=mesh['rep'=4,'shard'=8] {'shard'}, dimensions={0}, use_global_device_ids=true | all-gather | bytes 2304 | tf_op jit(solution)/shard_map/all_gather | solution.py:134
  36.7 26.3 %all-gather.5 = bf16[8,1,512]{2,1,0:T(2,128)(2,1)S(1)} all-gather(bf16[1,1,512]{2,1,0:T(2,128)(2,1)S(1)} %reshape.171), channel_id=1, replica_groups=mesh['rep'=4,'shard'=8] {'shard'}, dimensions={0}, use_global_device_ids=true | all-gather | bytes 9216 | tf_op jit(solution)/shard_map/all_gather | solution.py:132
  63.6 16.3 all-gather.2
  80.5 18.2 %all-gather = bf16[8,1,128]{2,1,0:T(2,128)(2,1)S(1)} all-gather(bf16[1,1,128]{2,1,0:T(2,128)(2,1)S(1)} %bitcast.212), channel_id=1, replica_groups=mesh['rep'=4,'shard'=8] {'shard'}, dimensions={0}, use_global_device_ids=true | all-gather | bytes 2304 | tf_op jit(solution)/shard_map/all_gather | solution.py:103
  98.7 16.4 all-gather.1
  119.1 18.0 %all-gather.4 = bf16[8,1,128]{2,1,0:T(2,128)(2,1)S(1)} all-gather(bf16[1,1,128]{2,1,0:T(2,128)(2,1)S(1)} %bitcast.214), channel_id=1, replica_groups=mesh['rep'=4,'shard'=8] {'shard'}, dimensions={0}, use_global_device_ids=true | all-gather | bytes 2304 | tf_op jit(solution)/shard_map/all_gather | solution.py:107
  137.7 16.6 all-gather.3
  154.9 18.0 %all-gather.7 = bf16[8,1,128]{2,1,0:T(2,128)(2,1)S(1)} all-gather(bf16[1,1,128]{2,1,0:T(2,128)(2,1)S(1)} %bitcast.216), channel_id=1, replica_groups=mesh['rep'=4,'shard'=8] {'shard'}, dimensions={0}, use_global_device_ids=true | all-gather | bytes 2304 | tf_op jit(solution)/shard_map/all_gather | solution.py:135
  173.5 16.3 all-gather.8
  231.7 54.8 %while.26 = (s32[]{:T(128)}, bf16[2,512,16,64]{1,3,2,0:T(8,128)(2,1)}, f32[2,16,512]{2,1,0:T(8,128)S(1)}, bf16[2,512,16,64]{1,3,2,0:T(8,128)(2,1)}, bf16[2,512,1...) while((s32[]{:T(128)}, bf16[2,512,16,64]{1,3,2,0:T(8,128)(2,1)}, ...), condition=%wide.region_3.4_spmd, body=%wide.region_0.3_spmd.sunk | while | flops 1111482368 | bytes 55838808 | solution.py:120
  231.9 9.4 multiply_reduce_fusion.8
  258.7 10.2 multiply_reduce_fusion.8
  277.6 8.9 bitcast_dynamic-update-slice_fusion.4
  301.2 36.5 %all-gather.24.cloned.1.call-done = bf16[1024,4096]{1,0:T(8,128)(2,1)} async-done(((bf16[128,4096]{1,0:T(8,128)(2,1)}), bf16[1024,4096]{1,0:T(8,128)(2,1)}) %all-gather.24.cloned.1.call-update) | async-done | bytes 8388624 | tf_op jit(solution)/shard_map/all_gather | solution.py:131
  337.7 48.1 %multiply_convert_fusion.3 = (bf16[1024,4096]{1,0:T(8,128)(2,1)}, f32[1024,4096]{1,0:T(8,128)}, f32[1024,4096]{1,0:T(8,128)}) fusion(f32[4096]{0:T(1024)S(1)} %bitcast.204, bf16[1024,4096]{1,0:T(8,128)(2,1)} %all-gather.24.cloned.1.call-done, bf16[1024,1024]{0,1:T(8,128)(2,1)S(1)} %fusion.68.clone.4), kind=kOutput, calls=%fused_computation.60 | convolution fusion | flops 8866758656 | bytes 52445184 | tf_op jit(solution)/shard_map/dot_general | solution.py:13
  385.8 77.1 %all-gather.26.cloned.1.call-done = bf16[4096,1024]{1,0:T(8,128)(2,1)} async-done(((bf16[512,1024]{1,0:T(8,128)(2,1)}), bf16[4096,1024]{1,0:T(8,128)(2,1)}) %all-gather.26.cloned.1.call-update) | async-done | bytes 8388624 | tf_op jit(solution)/shard_map/all_gather | solution.py:133
  462.8 14.9 fusion.73
  490.9 24.3 %convert_reduce_fusion = (f32[4096]{0:T(1024)}, bf16[1024,4096]{1,0:T(8,128)(2,1)}) fusion(f32[1024,4096]{1,0:T(8,128)} %get-tuple-element.271, f32[1024,4096]{1,0:T(8,128)} %get-tuple-element.281, f32[4096]{0:T(1024)S(1)} %bitcast.205, bf16[1024,1024]{0,1:T(8,128)(2,1)} %get-tuple-element.263, bf16[4096,1024]{1,0:T(8,128)(2,1)} %all-gather.26.cloned.1.call-done), kind=kOutput, calls=%fused_computation.58 | convolution fusion | flops 8661233664 | bytes 52461568 | tf_op jit(solution)/shard_map/dot_general | solution.py:23
  515.2 17.4 %multiply_reduce_fusion.2 = (f32[1024]{0:T(1024)}, f32[1024]{0:T(1024)S(1)}, f32[1024]{0:T(1024)}, f32[1024,1024]{0,1:T(8,128)S(1)}) fusion(f32[1024,1024]{0,1:T(8,128)S(1)} %copy-done.7, f32[1024]{0:T(1024)S(1)} %fusion.63, f32[1024]{0:T(1024)S(1)} %broadcast_multiply_fusion.1, f32[1024]{0:T(1024)S(1)} %bitcast.197, ...), kind=kOutput, calls=%fused_computation.84 | convolution fusion | flops 8607757312 | bytes 31502336 | tf_op jit(solution)/shard_map/dot_general | solution.py:23
  550.0 90.4 %while.27 = (s32[]{:T(128)}, bf16[2,512,16,64]{1,3,2,0:T(8,128)(2,1)}, bf16[2,512,16,64]{1,3,2,0:T(8,128)(2,1)}, bf16[2,512,16,64]{1,3,2,0:T(8,128)(2,1)}, bf16[...) while((s32[]{:T(128)}, ...), condition=%wide.region_14.15_spmd, body=%wide.region_12.14_spmd.sunk | while | flops 2737299456 | bytes 312710592 | solution.py:177
  554.2 10.9 multiply_reduce_fusion.9
  599.0 10.9 multiply_reduce_fusion.9
  678.8 16.7 fusion.65
  697.1 14.6 fusion.75
  720.2 17.1 %reduce-scatter.7.cloned.1.call-done = f32[128,1024]{0,1:T(8,128)} async-done(((f32[1024,1024]{0,1:T(8,128)}), f32[128,1024]{0,1:T(8,128)}) %reduce-scatter.7.cloned.1.call-update) | async-done | bytes 524304 | tf_op jit(solution)/shard_map/reduce_scatter | solution.py:205
  739.1 90.5 %reduce-scatter.9.cloned.1.call-done = f32[128,1024]{0,1:T(8,128)} async-done(((f32[1024,1024]{0,1:T(8,128)}), f32[128,1024]{0,1:T(8,128)}) %reduce-scatter.9.cloned.1.call-update) | async-done | bytes 524304 | tf_op jit(solution)/shard_map/reduce_scatter | solution.py:206
  831.4 90.1 %reduce-scatter.11.cloned.1.call-done = f32[128,1024]{0,1:T(8,128)} async-done(((f32[1024,1024]{0,1:T(8,128)}), f32[128,1024]{0,1:T(8,128)}) %reduce-scatter.11.cloned.1.call-update) | async-done | bytes 524304 | tf_op jit(solution)/shard_map/reduce_scatter | solution.py:207
  923.3 90.0 %reduce-scatter.13.cloned.1.call-done = f32[128,1024]{1,0:T(8,128)} async-done(((f32[1024,1024]{1,0:T(8,128)}), f32[128,1024]{1,0:T(8,128)}) %reduce-scatter.13.cloned.1.call-update) | async-done | bytes 524304 | tf_op jit(solution)/shard_map/reduce_scatter | solution.py:210
  1015.1 284.5 %reduce-scatter.15.cloned.1.call-done = f32[128,4096]{1,0:T(8,128)} async-done(((f32[1024,4096]{1,0:T(8,128)}), f32[128,4096]{1,0:T(8,128)}) %reduce-scatter.15.cloned.1.call-update) | async-done | bytes 2097168 | tf_op jit(solution)/shard_map/reduce_scatter | solution.py:159
  1302.3 283.2 %reduce-scatter.17.cloned.1.call-done = f32[512,1024]{1,0:T(8,128)} async-done(((f32[4096,1024]{1,0:T(8,128)}), f32[512,1024]{1,0:T(8,128)}) %reduce-scatter.17.cloned.1.call-update) | async-done | bytes 2097168 | tf_op jit(solution)/shard_map/reduce_scatter | solution.py:161
  1597.5 9.7 add_convert_fusion.1
  1613.9 35.6 %all-reduce.9 = (bf16[1024]{0:T(1024)(128)(2,1)S(1)}, bf16[1024]{0:T(1024)(128)(2,1)S(1)}, bf16[1024]{0:T(1024)(128)(2,1)S(1)}, bf16[1024]{0:T(1024)(128)(2,1)S(...) all-reduce(f32[1024]{0:T(1024)S(1)} %reduce_sum.216, ...), channel_id=5, replica_groups=mesh['rep'=4,'shard'=8] {'shard'}, use_global_device_ids=true, to_apply=%region_22.23.clone | all-reduce | flops 12288 | bytes 73728
  (303 shorter events, 293.6 us)
Async XLA Ops:
  7.2 29.5 %copy-start.58 = (bf16[512]{0:T(512)(128)(2,1)S(1)}, bf16[512]{0:T(512)(128)(2,1)}, u32[]{:S(2)}) copy-start(bf16[512]{0:T(512)(128)(2,1)} %param.32) | copy-start | bytes 3076
  7.2 56.4 %copy-start.60 = (bf16[128]{0:T(256)(128)(2,1)S(1)}, bf16[128]{0:T(256)(128)(2,1)}, u32[]{:S(2)}) copy-start(bf16[128]{0:T(256)(128)(2,1)} %param.28) | copy-start | bytes 772
  7.2 73.3 %copy-start.61 = (bf16[128]{0:T(256)(128)(2,1)S(1)}, bf16[128]{0:T(256)(128)(2,1)}, u32[]{:S(2)}) copy-start(bf16[128]{0:T(256)(128)(2,1)} %param.26) | copy-start | bytes 772
  7.2 91.4 %copy-start.62 = (bf16[128]{0:T(256)(128)(2,1)S(1)}, bf16[128]{0:T(256)(128)(2,1)}, u32[]{:S(2)}) copy-start(bf16[128]{0:T(256)(128)(2,1)} %param.25) | copy-start | bytes 772
  7.3 183.2 %all-gather.16.cloned.1.call-start = ((), (), s32[]{:S(2)}) async-start(), calls=%async_computation.6 | async-start | bytes 2359296 | tf_op jit(solution)/shard_map/all_gather | solution.py:101
  8.0 196.4 %all-gather.18.cloned.1.call-start = ((), (), s32[]{:S(2)}) async-start(), calls=%async_computation.7 | async-start | bytes 2359296 | tf_op jit(solution)/shard_map/all_gather | solution.py:99
  8.7 209.6 %all-gather.20.cloned.1.call-start = ((), (), s32[]{:S(2)}) async-start(), calls=%async_computation.8 | async-start | bytes 2359296 | tf_op jit(solution)/shard_map/all_gather | solution.py:100
  9.5 283.5 %all-gather.22.cloned.1.call-start = ((), (), s32[]{:S(2)}) async-start(), calls=%async_computation.9 | async-start | bytes 2359296 | tf_op jit(solution)/shard_map/all_gather | solution.py:104
  10.0 327.7 %all-gather.24.cloned.1.call-start = ((), (), s32[]{:S(2)}) async-start(), calls=%async_computation.10 | async-start | bytes 9437184 | tf_op jit(solution)/shard_map/all_gather | solution.py:131
  10.6 452.2 %all-gather.26.cloned.1.call-start = ((), (), s32[]{:S(2)}) async-start(), calls=%async_computation.11 | async-start | bytes 9437184 | tf_op jit(solution)/shard_map/all_gather | solution.py:133
  11.2 726.2 %reduce-scatter.7.cloned.1.call-start = ((), (), s32[]{:S(2)}) async-start(), calls=%async_computation.12 | async-start | bytes 4718592 | tf_op jit(solution)/shard_map/reduce_scatter | solution.py:205
  11.3 107.8 %copy-start.63 = (bf16[128]{0:T(256)(128)(2,1)S(1)}, bf16[128]{0:T(256)(128)(2,1)}, u32[]{:S(2)}) copy-start(bf16[128]{0:T(256)(128)(2,1)} %param.30) | copy-start | bytes 772
  11.3 126.3 %copy-start.64 = (bf16[128]{0:T(256)(128)(2,1)S(1)}, bf16[128]{0:T(256)(128)(2,1)}, u32[]{:S(2)}) copy-start(bf16[128]{0:T(256)(128)(2,1)} %param.29) | copy-start | bytes 772
  11.3 143.5 %copy-start.65 = (bf16[128]{0:T(256)(128)(2,1)S(1)}, bf16[128]{0:T(256)(128)(2,1)}, u32[]{:S(2)}) copy-start(bf16[128]{0:T(256)(128)(2,1)} %param.35) | copy-start | bytes 772
  11.3 162.2 %copy-start.66 = (bf16[128]{0:T(256)(128)(2,1)S(1)}, bf16[128]{0:T(256)(128)(2,1)}, u32[]{:S(2)}) copy-start(bf16[128]{0:T(256)(128)(2,1)} %param.36) | copy-start | bytes 772
  298.5 234.1 %copy-start.34 = (f32[1024]{0:T(1024)}, f32[1024]{0:T(1024)S(1)}, u32[]{:S(2)}) copy-start(f32[1024]{0:T(1024)S(1)} %broadcast_multiply_fusion.1) | copy-start | bytes 12292
  299.0 86.8 %copy-start.41 = (f32[1024]{0:T(1024)}, f32[1024]{0:T(1024)S(1)}, u32[]{:S(2)}) copy-start(f32[1024]{0:T(1024)S(1)} %multiply_reduce_fusion.5) | copy-start | bytes 12292
  299.0 38.7 %copy-start.52 = (f32[8,1,512]{2,1,0:T(1,128)S(1)}, f32[8,1,512]{2,1,0:T(1,128)}, u32[]{:S(2)}) copy-start(f32[8,1,512]{2,1,0:T(1,128)} %convert_element_type.270) | copy-start | bytes 49156
  299.0 233.6 %copy-start.39 = (f32[1024]{0:T(1024)}, f32[1024]{0:T(1024)S(1)}, u32[]{:S(2)}) copy-start(f32[1024]{0:T(1024)S(1)} %fusion.63) | copy-start | bytes 12292
  337.7 125.1 %copy-start.56 = (f32[8,1,128]{2,1,0:T(1,128)S(1)}, f32[8,1,128]{2,1,0:T(1,128)}, u32[]{:S(2)}) copy-start(f32[8,1,128]{2,1,0:T(1,128)} %convert_element_type.271) | copy-start | bytes 12292
  462.8 15.0 copy-start.36
  490.9 24.3 %copy-start.7 = (f32[1024,1024]{0,1:T(8,128)S(1)}, f32[1024,1024]{0,1:T(8,128)}, u32[]{:S(2)}) copy-start(f32[1024,1024]{0,1:T(8,128)} %copy-done.6) | copy-start | bytes 12582916
  490.9 24.3 %copy-start.10 = (bf16[1024,1024]{0,1:T(8,128)(2,1)S(1)}, bf16[1024,1024]{0,1:T(8,128)(2,1)}, u32[]{:S(2)}) copy-start(bf16[1024,1024]{0,1:T(8,128)(2,1)} %copy.98) | copy-start | bytes 6291460
  515.2 17.4 %copy-start.42 = (f32[1024]{0:T(1024)S(1)}, f32[1024]{0:T(1024)}, u32[]{:S(2)}) copy-start(f32[1024]{0:T(1024)} %copy-done.41) | copy-start | bytes 12292
  554.1 11.4 copy-start
  599.0 11.4 copy-start
  650.5 179.1 %reduce-scatter.9.cloned.1.call-start = ((), (), s32[]{:S(2)}) async-start(), calls=%async_computation.13 | async-start | bytes 4718592 | tf_op jit(solution)/shard_map/reduce_scatter | solution.py:206
  660.6 261.0 %reduce-scatter.11.cloned.1.call-start = ((), (), s32[]{:S(2)}) async-start(), calls=%async_computation.14 | async-start | bytes 4718592 | tf_op jit(solution)/shard_map/reduce_scatter | solution.py:207
  670.5 342.8 %reduce-scatter.13.cloned.1.call-start = ((), (), s32[]{:S(2)}) async-start(), calls=%async_computation.15 | async-start | bytes 4718592 | tf_op jit(solution)/shard_map/reduce_scatter | solution.py:210
  678.2 621.4 %reduce-scatter.15.cloned.1.call-start = ((), (), s32[]{:S(2)}) async-start(), calls=%async_computation.16 | async-start | bytes 18874368 | tf_op jit(solution)/shard_map/reduce_scatter | solution.py:159
  695.5 889.9 %reduce-scatter.17.cloned.1.call-start = ((), (), s32[]{:S(2)}) async-start(), calls=%async_computation.17 | async-start | bytes 18874368 | tf_op jit(solution)/shard_map/reduce_scatter | solution.py:161
  711.8 949.5 %all-reduce.14.cloned.1.call-start = ((), (), s32[]{:S(2)}) async-start(), calls=%async_computation.18 | async-start | bytes 6291456 | tf_op jit(solution)/shard_map/psum | solution.py:232
  (61 other events, 284.6 us)
Sparse Core Ops, SparseCore 0:
  10.2 52.1 all-gather.15
  64.5 47.9 all-gather.17
  114.6 47.8 all-gather.19
  164.5 47.7 all-gather.21
  214.2 123.4 all-gather.23
  339.7 123.1 all-gather.25
  650.7 86.6 reduce-scatter.6
  741.4 88.1 reduce-scatter.8
  833.3 88.1 reduce-scatter.10
  925.4 87.8 reduce-scatter.12
  1017.1 282.4 reduce-scatter.14
  1303.7 281.7 reduce-scatter.16
  1589.4 68.6 all-reduce.13
where the time goes:
time: 1690 us; the launch traced here: 1680 us
  waiting for transfers between devices  973 us (58%)
  matrix products  298 us (18%)
  blocking collectives  210 us (12%)
  local copies, waits for them, and re-layouts  101 us (6%)
  other arithmetic  80 us (5%)
    reduce_scatter x1, waiting for transfers between devices, shards(): lax.psum_scatter(grad_w_inner, 'shard', scatter_dimension=0, tiled=True)  285 us
    reduce_scatter x1, waiting for transfers between devices, shards(): lax.psum_scatter(grad_w_outer, 'shard', scatter_dimension=0, tiled=True)  283 us
    reduce_scatter x1, waiting for transfers between devices, shards(): lax.psum_scatter(grad_w_key, 'shard', scatter_dimension=0, tiled=True)  90.5 us
    reduce_scatter x1, waiting for transfers between devices, shards(): lax.psum_scatter(grad_w_value, 'shard', scatter_dimension=0, tiled=True)  90.1 us
    reduce_scatter x1, waiting for transfers between devices, shards(): lax.psum_scatter(grad_w_out, 'shard', scatter_dimension=0, tiled=True)  90 us
    dot_general x6, matrix products, project(): return jnp.dot(left, right, preferred_element_type=jnp.float32)  82.4 us
    all_gather x1, waiting for transfers between devices, shards(): lax.all_gather(w_outer, 'shard', axis=0, tiled=True)  77.1 us
    dot_general x6, matrix products, against(): lax.dot_general(left, right, (((1,), (1,)), ((), ())), preferred_element_...  66.6 us
  transfers between devices with their start and end apart: 13, of which 8 were waited for; matrix products, arithmetic and copies ran while one was open for 16% of the time, Pallas kernels for 0%

commit v1 on v0

v1 whole, which is shorter than its diff:
```python
import functools

import jax
import jax.numpy as jnp
from jax import lax
from jax.experimental import pallas as pl
from jax.experimental.pallas import tpu as pltpu
from jax.sharding import PartitionSpec as P

D = 1024
H = 16
DH = 64
SEQ = 512
LANES = 128
PAIRS = D // LANES
AXES = ("rep", "shard")
RING_MOST = 16
LOW = jnp.bfloat16
FULL = jnp.float32


def project(left, right):
    return jnp.dot(left, right, preferred_element_type=FULL)


def gram(left, right):
    return lax.dot_general(left, right, (((0,), (0,)), ((), ())), preferred_element_type=FULL)


def against(left, right):
    return lax.dot_general(left, right, (((1,), (1,)), ((), ())), preferred_element_type=FULL)


def column_sum(values):
    return jnp.sum(values.astype(FULL), axis=0)


def normal(values):
    centre = values - jnp.mean(values, axis=-1, keepdims=True)
    spread = jnp.mean(centre * centre, axis=-1, keepdims=True)
    inverse = lax.rsqrt(spread + 1e-12)
    return centre * inverse, inverse


def normal_back(scaled, unit, inverse):
    mean = jnp.mean(scaled, axis=-1, keepdims=True)
    along = jnp.mean(scaled * unit, axis=-1, keepdims=True)
    return (scaled - mean - unit * along) * inverse


def head_mask(head):
    lane = lax.broadcasted_iota(jnp.int32, (SEQ, LANES), 1)
    return (lane // DH) == head


def attend_kernel(query_ref, key_ref, value_ref, out_ref, lse_ref):
    query = query_ref[...] * LOW(0.125)
    key = key_ref[...]
    value_t = value_ref[...].T
    parts = []
    for head in range(LANES // DH):
        own = jnp.where(head_mask(head), query, jnp.zeros_like(query))
        scores = against(key, own)
        top = jnp.max(scores, axis=0, keepdims=True)
        expo = jnp.exp(scores - top)
        total = jnp.sum(expo, axis=0, keepdims=True)
        mixed = project(value_t[head * DH : (head + 1) * DH], expo.astype(LOW))
        parts.append(mixed * (1.0 / total))
        lse_ref[0, head : head + 1, :] = top + jnp.log(total)
    out_ref[...] = jnp.concatenate(parts, axis=0).T.astype(LOW)


def attend_back_kernel(query_ref, key_ref, value_ref, d_ref, lse_ref, out_ref):
    pair = pl.program_id(1)
    query = query_ref[...] * LOW(0.125)
    key = key_ref[...]
    value = value_ref[...]
    d_out = d_ref[...]
    key_t = key.T
    d_key = None
    d_value = None
    d_query = []
    for head in range(LANES // DH):
        mask = head_mask(head)
        own = jnp.where(mask, query, jnp.zeros_like(query))
        d_own = jnp.where(mask, d_out, jnp.zeros_like(d_out))
        probs = jnp.exp(against(key, own) - lse_ref[0, head : head + 1, :])
        d_probs = against(value, d_own)
        inner = jnp.sum(probs * d_probs, axis=0, keepdims=True)
        d_scores = (probs * (d_probs - inner)).astype(LOW)
        part_value = project(probs.astype(LOW), d_own)
        part_key = project(d_scores, own)
        d_value = part_value if d_value is None else d_value + part_value
        d_key = part_key if d_key is None else d_key + part_key
        d_query.append(project(key_t[head * DH : (head + 1) * DH], d_scores))
    d_query = jnp.concatenate(d_query, axis=0).T * 0.125
    for place, grad in enumerate((d_query, d_key, d_value)):
        start = pl.multiple_of(place * D + pair * LANES, LANES)
        out_ref[:, pl.ds(start, LANES)] = grad.astype(LOW)


def column_block(place):
    return pl.BlockSpec((SEQ, LANES), lambda seq, pair: (seq, place * PAIRS + pair))


LSE_BLOCK = pl.BlockSpec((1, LANES // DH, SEQ), lambda seq, pair: (seq * PAIRS + pair, 0, 0))


def attend(qkv):
    count = qkv.shape[0]
    seqs = count // SEQ
    return pl.pallas_call(
        attend_kernel,
        grid=(seqs, PAIRS),
        in_specs=[column_block(0), column_block(1), column_block(2)],
        out_specs=[column_block(0), LSE_BLOCK],
        out_shape=[
            jax.ShapeDtypeStruct((count, D), LOW),
            jax.ShapeDtypeStruct((seqs * PAIRS, LANES // DH, SEQ), FULL),
        ],
        compiler_params=pltpu.CompilerParams(vmem_limit_bytes=32 * 2**20),
        name="attend",
    )(qkv, qkv, qkv)


def attend_back(qkv, d_attended, lse):
    count = qkv.shape[0]
    return pl.pallas_call(
        attend_back_kernel,
        grid=(count // SEQ, PAIRS),
        in_specs=[column_block(0), column_block(1), column_block(2), column_block(0), LSE_BLOCK],
        out_specs=pl.BlockSpec((SEQ, 3 * D), lambda seq, pair: (seq, 0)),
        out_shape=jax.ShapeDtypeStruct((count, 3 * D), LOW),
        compiler_params=pltpu.CompilerParams(vmem_limit_bytes=40 * 2**20),
        name="attend_back",
    )(qkv, qkv, qkv, d_attended, lse)


def assemble_kernel(count, size, place_ref, *refs):
    chunks, out_ref, sems = refs[:count], refs[count], refs[count + 1]
    copies = []
    for i in range(count):
        rows = chunks[i].shape[0]
        start = pl.multiple_of(place_ref[i], size)
        copies.append(pltpu.make_async_copy(chunks[i], out_ref.at[pl.ds(start, rows)], sems.at[i]))
    for copy in copies:
        copy.start()
    for copy in copies:
        copy.wait()


def assemble(chunks, places, rows):
    count = len(chunks)
    size = min(chunk.shape[0] for chunk in chunks)
    return pl.pallas_call(
        functools.partial(assemble_kernel, count, size),
        in_specs=[pl.BlockSpec(memory_space=pltpu.SMEM)] + [pl.BlockSpec(memory_space=pl.ANY)] * count,
        out_specs=pl.BlockSpec(memory_space=pl.ANY),
        out_shape=jax.ShapeDtypeStruct((rows,) + chunks[0].shape[1:], chunks[0].dtype),
        scratch_shapes=[pltpu.SemaphoreType.DMA((count,))],
        name="assemble",
    )(jnp.stack(places).astype(jnp.int32), *chunks)


class Links:
    def __init__(self, mesh):
        self.reps, self.size = mesh.shape["rep"], mesh.shape["shard"]
        size = self.size
        self.direct = size > RING_MOST or size % 2 == 1
        self.order = list(range(0, size, 2)) + list(range(size - 1, 0, -2))
        self.far = size // 2
        self.near = size - 1 - self.far
        rep = lax.axis_index("rep")
        shard = lax.axis_index("shard")
        self.core = rep % 2
        self.sign = 1 - 2 * self.core
        self.place = jnp.where(shard % 2 == 0, shard // 2, size - 1 - shard // 2)

    def owner(self, step):
        place = (self.place + self.sign * step + 2 * self.size) % self.size
        return jnp.where(place < self.size // 2, 2 * place, 2 * (self.size - place) - 1)

    def hop(self, values, sign):
        pairs = []
        for rep in range(self.reps):
            turn = sign if rep % 2 == 0 else -sign
            for i, shard in enumerate(self.order):
                target = self.order[(i + turn) % self.size]
                pairs.append((rep * self.size + shard, rep * self.size + target))
        return lax.ppermute(values, AXES, pairs)

    def swap(self, values, bit):
        pairs = []
        for rep in range(self.reps):
            for shard in range(self.size):
                pairs.append((rep * self.size + shard, (rep ^ bit) * self.size + shard))
        return lax.ppermute(values, AXES, pairs)

    def round_ring(self, values):
        found = []
        for sign, hops in ((1, self.far), (-1, self.near)):
            moving = values
            for step in range(1, hops + 1):
                moving = self.hop(moving, sign)
                found.append((moving, -sign * step))
        return found

    def gather_small(self, values):
        if self.direct:
            return lax.all_gather(values, "shard", axis=0, tiled=True)
        rows = values.shape[0]
        found = [(values, 0)] + self.round_ring(values)
        chunks = [chunk for chunk, _ in found]
        places = [self.owner(step) * rows for _, step in found]
        return assemble(chunks, places, self.size * rows)

    def gather(self, values):
        if self.direct:
            return lax.all_gather(values, "shard", axis=0, tiled=True)
        rows = values.shape[0]
        half = rows // 2
        mine = lax.dynamic_slice_in_dim(values, self.core * half, half, axis=0)
        chunks = [values]
        places = [self.owner(0) * rows]
        for chunk, step in self.round_ring(mine):
            chunks += [chunk, self.swap(chunk, 1)]
            places.append(self.owner(step) * rows + self.core * half)
            places.append(self.owner(-step) * rows + (1 - self.core) * half)
        return assemble(chunks, places, self.size * rows)

    def reduce(self, values):
        width = values.shape[1]
        rows = values.shape[0] // self.size
        if self.direct:
            own = lax.psum_scatter(values, "shard", scatter_dimension=0, tiled=True)
            return lax.psum(own, "rep").astype(FULL)
        half = rows // 2
        split = values.reshape(self.size, 2, half, width)
        other = lax.dynamic_index_in_dim(split, 1 - self.core, axis=1, keepdims=False)
        other = self.swap(other, 1)

        def piece(step):
            owner = self.owner(step)
            own = lax.dynamic_slice(split, (owner, self.core, 0, 0), (1, 1, half, width))
            pair = lax.dynamic_slice(other, (owner, 0, 0), (1, half, width))
            return own[0, 0].astype(FULL) + pair[0].astype(FULL)

        total = piece(0)
        for sign, hops in ((1, self.far), (-1, self.near)):
            moving = piece(sign * hops).astype(LOW)
            for step in range(hops - 1, -1, -1):
                moving = self.hop(moving, sign)
                if step > 0:
                    moving = (moving.astype(FULL) + piece(sign * step)).astype(LOW)
            total = total + moving.astype(FULL)
        total = total.astype(LOW)
        total = (total.astype(FULL) + self.swap(total, 2).astype(FULL)).astype(LOW)
        pair = self.swap(total, 1)
        low = jnp.where(self.core == 0, total, pair)
        high = jnp.where(self.core == 0, pair, total)
        return jnp.concatenate([low, high], axis=0).astype(FULL)


def shards(
    mesh,
    tokens,
    w_query,
    w_key,
    w_value,
    b_query,
    b_value,
    w_out,
    b_out,
    gain_one,
    shift_one,
    w_inner,
    b_inner,
    w_outer,
    b_outer,
    gain_two,
    shift_two,
    cotangent,
):
    links = Links(mesh)
    size = links.size
    width = D // size
    hidden = b_inner.shape[0]

    vectors = (b_query, b_value, b_out, gain_one, shift_one, b_outer, gain_two, shift_two)
    packed = jnp.concatenate(vectors + (b_inner,))
    used = packed.shape[0]
    room = -(-used // (32 * LANES)) * 32 * LANES
    packed = jnp.pad(packed, (0, room - used)).reshape(room // LANES, LANES)

    whole_qkv = links.gather(jnp.concatenate([w_query, w_key, w_value], axis=1))
    whole_small = links.gather_small(packed).reshape(size, room).astype(FULL)
    whole_out = links.gather(w_out)
    whole_inner = links.gather(w_inner)
    whole_outer = links.gather(w_outer)
    (bias_query, bias_value, bias_out, gain_first, shift_first, bias_outer, gain_second, shift_second) = (
        whole_small[:, i * width : (i + 1) * width].reshape(D) for i in range(len(vectors))
    )
    bias_inner = whole_small[:, used - hidden : used].reshape(size * hidden)

    bias_qkv = jnp.concatenate([bias_query, jnp.zeros((D,), FULL), bias_value])
    qkv = (project(tokens, whole_qkv) + bias_qkv).astype(LOW)
    attended, lse = attend(qkv)
    branch = project(attended, whole_out) + bias_out
    unit_one, inverse_one = normal(tokens.astype(FULL) + branch)
    first = unit_one * gain_first + shift_first
    first_low = first.astype(LOW)
    pre = project(first_low, whole_inner) + bias_inner
    below = 0.5 * (1.0 + lax.erf(pre * (0.5**0.5)))
    active = (pre * below).astype(LOW)
    slope = (below + pre * jnp.exp(-0.5 * pre * pre) * 0.3989422804014327).astype(LOW)
    second = first + project(active, whole_outer) + bias_outer
    unit_two, inverse_two = normal(second)
    output = (unit_two * gain_second + shift_second).astype(LOW)

    cot = cotangent.astype(FULL)
    grad_gain_two = jnp.sum(cot * unit_two, axis=0)
    grad_shift_two = jnp.sum(cot, axis=0)
    d_second = normal_back(cot * gain_second, unit_two, inverse_two)
    d_mid = d_second.astype(LOW)
    own_outer = links.reduce(gram(active, d_mid).astype(LOW))
    grad_b_outer = column_sum(d_mid)
    d_pre = (against(d_mid, whole_outer) * slope.astype(FULL)).astype(LOW)
    own_inner = links.reduce(gram(first_low, d_pre).astype(LOW))
    grad_b_inner = column_sum(d_pre)
    d_first = d_second + against(d_pre, whole_inner)
    grad_gain_one = jnp.sum(d_first * unit_one, axis=0)
    grad_shift_one = jnp.sum(d_first, axis=0)
    d_inner = normal_back(d_first * gain_first, unit_one, inverse_one)
    d_branch = d_inner.astype(LOW)
    own_out = links.reduce(gram(attended, d_branch).astype(LOW))
    grad_b_out = column_sum(d_branch)
    d_attended = against(d_branch, whole_out).astype(LOW)
    d_qkv = attend_back(qkv, d_attended, lse)
    own_qkv = links.reduce(gram(tokens, d_qkv).astype(LOW))
    grad_b_qkv = column_sum(d_qkv)
    d_tokens = (d_inner + against(d_qkv, whole_qkv)).astype(LOW)

    grads = (
        grad_b_qkv[:D],
        grad_b_qkv[2 * D :],
        grad_b_out,
        grad_gain_one,
        grad_shift_one,
        grad_b_outer,
        grad_gain_two,
        grad_shift_two,
    )
    small = jnp.concatenate(
        [grad.reshape(size, width) for grad in grads] + [grad_b_inner.reshape(size, hidden)], axis=1
    )
    small = jnp.pad(small, ((0, 0), (0, room - used))).astype(LOW)
    own_small = links.reduce(small.reshape(size * (room // LANES), LANES)).reshape(room)
    (
        own_bias_query,
        own_bias_value,
        own_bias_out,
        own_gain_one,
        own_shift_one,
        own_bias_outer,
        own_gain_two,
        own_shift_two,
    ) = (own_small[i * width : (i + 1) * width] for i in range(len(vectors)))
    own_bias_inner = own_small[used - hidden : used]
    return (
        output,
        d_tokens,
        own_qkv[:, :D],
        own_qkv[:, D : 2 * D],
        own_qkv[:, 2 * D :],
        own_bias_query,
        own_bias_value,
        own_out,
        own_bias_out,
        own_gain_one,
        own_shift_one,
        own_inner,
        own_bias_inner,
        own_outer,
        own_bias_outer,
        own_gain_two,
        own_shift_two,
    )


def solution(mesh):
    rows = P(("rep", "shard"), None)
    matrix = P("shard", None)
    vector = P("shard")
    return jax.shard_map(
        functools.partial(shards, mesh),
        mesh=mesh,
        in_specs=(
            rows,
            matrix,
            matrix,
            matrix,
            vector,
            vector,
            matrix,
            vector,
            vector,
            vector,
            matrix,
            vector,
            matrix,
            vector,
            vector,
            vector,
            rows,
        ),
        out_specs=(
            rows,
            rows,
            matrix,
            matrix,
            matrix,
            vector,
            vector,
            matrix,
            vector,
            vector,
            vector,
            matrix,
            vector,
            matrix,
            vector,
            vector,
            vector,
        ),
        check_vma=False,
    )
```

time: 1690 us -> 1330 us (0.79)
  Pallas kernels: 0 us -> 833 us
  waiting for transfers between devices: 973 us -> 162 us
  blocking collectives: 210 us -> 0 us
  matrix products: 298 us -> 137 us
  starting transfers between devices: 0.9 us -> 92.3 us
  local copies, waits for them, and re-layouts: 101 us -> 45.5 us
  other arithmetic: 80 us -> 47.3 us
    reduce_scatter x6 -> x0, waiting for transfers between devices: 855 us -> none  [the longest x1 285 us: shards(): lax.psum_scatter(grad_w_inner, 'shard', scatter_dimension=0, tiled=True)]
    pallas_call x0 -> x7, Pallas kernels: none -> 833 us  [the longest x5 774 us: assemble(): pl.pallas_call(functools.partial(assemble_kernel, count, size), in_specs=...]
    all_gather x9 -> x0, blocking collectives: 168 us -> none  [the longest x1 26.3 us: shards(): lax.all_gather(b_inner, 'shard', axis=0, tiled=True)]
    ppermute x0 -> x113, waiting for transfers between devices: none -> 162 us  [the longest x70 144 us: hop(): return lax.ppermute(values, AXES, pairs)]
    dot_general x20 -> x4, matrix products: 181 us -> 48.6 us  [project(): return jnp.dot(left, right, preferred_element_type=FULL)]
    all_gather x6 -> x0, waiting for transfers between devices: 114 us -> none  [the longest x1 77.1 us: shards(): lax.all_gather(w_outer, 'shard', axis=0, tiled=True)]
    ppermute x0 -> x113, starting transfers between devices: none -> 92.3 us  [the longest x70 80.2 us: hop(): return lax.ppermute(values, AXES, pairs)]
    while x51 -> x0, local copies, waits for them, and re-layouts: 41.9 us -> none  [the longest x3 15.4 us: shards(): attended, log_total = lax.map(attend_block, (query_low, key_low, value_low))]
  transfers between devices with their start and end apart: 13 -> 113, of which waited for: 8 -> 43; matrix products, arithmetic and copies ran while one was open for 16% -> 7% of each run, Pallas kernels for 0% -> 41%
where the time goes in v1:
time: 1330 us; the launch traced here: 1320 us
  Pallas kernels  833 us (63%)
  waiting for transfers between devices  162 us (12%)
  matrix products  137 us (10%)
  starting transfers between devices  92.3 us (7%)
  other arithmetic  47.3 us (4%)
  local copies, waits for them, and re-layouts  45.5 us (3%)
    pallas_call x5, Pallas kernels, assemble(): pl.pallas_call(functools.partial(assemble_kernel, count, size), in_specs=...  774 us
    ppermute x70, waiting for transfers between devices, hop(): return lax.ppermute(values, AXES, pairs)  144 us
    ppermute x70, starting transfers between devices, hop(): return lax.ppermute(values, AXES, pairs)  80.2 us
    dot_general x4, matrix products, project(): return jnp.dot(left, right, preferred_element_type=FULL)  48.6 us
    dot_general x4, matrix products, against(): lax.dot_general(left, right, (((1,), (1,)), ((), ())), preferred_element_...  47 us
    dot_general x4, matrix products, gram(): lax.dot_general(left, right, (((0,), (0,)), ((), ())), preferred_element_...  41.7 us
    pallas_call x1, Pallas kernels, attend_back(): pl.pallas_call(attend_back_kernel, grid=(count // SEQ, PAIRS), in_specs=[...  36 us
  transfers between devices with their start and end apart: 113, of which 43 were waited for; matrix products, arithmetic and copies ran while one was open for 7% of the time, Pallas kernels for 41%

profile of v1, /device:TPU:0, one launch (start us, length us, event | category | flops | bytes accessed | tf_op | source)
XLA Modules:
  0.0 1319.5 jit_solution(5903406259337747679)
XLA Ops:
  30.0 5.2 collective-permute-done.23.refs_3_
  40.9 18.6 %collective-permute-done.25.refs_5_ = bf16[64,1024]{1,0:T(8,128)(2,1)S(1)} collective-permute-done((bf16[64,1024]{1,0:T(8,128)(2,1)S(1)}, bf16[64,1024]{1,0:T(8,128)(2,1)S(1)}, u32[]{:S(2)}, u32[]{:S(2)}) %collective-permute-start.25) | collective-permute-done | bytes 131104 | tf_op jit(solution)/shard_map/ppermute | solution.py:190
  70.1 10.8 collective-permute-done.27.refs_7_
  85.8 7.3 collective-permute-done.12.refs_13_
  114.3 65.4 %assemble.7 = bf16[1024,1024]{1,0:T(8,128)(2,1)} custom-call(s32[15]{0:T(128)} %stack.170.place_ref, bf16[128,1024]{1,0:T(8,128)(2,1)} %refs_0_.3, bf16[64,1024]{1,0:T(8,128)(2,1)} %copy-done.36, bf16[64,1024]{1,0:T(8,128)(2,1)} %copy-done.38, bf16[64,1024]{1,0:T(8,128)(2,1)} %copy-done.39, bf16[64,1024]{1,0:T(8,128)(2,1)} %copy-done.41, ...), custom_call_target="tpu_custom_call" | custom-call | tf_op jit(solution)/shard_map/assemble/pallas_call | solution.py:155
  179.8 192.5 %assemble.5 = bf16[1024,3072]{1,0:T(8,128)(2,1)} custom-call(s32[15]{0:T(128)} %stack.170.place_ref, bf16[128,3072]{1,0:T(8,128)(2,1)} %copy-done.10, bf16[64,3072]{1,0:T(8,128)(2,1)} %copy-done.34, bf16[64,3072]{1,0:T(8,128)(2,1)} %copy-done.35, bf16[64,3072]{1,0:T(8,128)(2,1)} %collective-permute-done.2.refs_3_, ...), custom_call_target="tpu_custom_call" | custom-call | tf_op jit(solution)/shard_map/assemble/pallas_call | solution.py:155
  376.7 9.4 fusion.5.query_ref.key_ref.value_ref
  386.1 23.1 %attend.1 = (bf16[1024,1024]{1,0:T(8,128)(2,1)S(1)}, f32[16,2,512]{2,1,0:T(2,128)S(1)}) custom-call(bf16[1024,3072]{1,0:T(8,128)(2,1)S(1)} %fusion.5.query_ref.key_ref.value_ref, bf16[1024,3072]{1,0:T(8,128)(2,1)S(1)} %fusion.5.query_ref.key_ref.value_ref, bf16[1024,3072]{1,0:T(8,128)(2,1)S(1)} %fusion.5.query_ref.key_ref.value_ref), custom_call_target="tpu_custom_call" | custom-call | tf_op jit(solution)/shard_map/attend/pallas_call | solution.py:112
  420.2 6.4 collective-permute-done.41.refs_7_
  430.2 256.0 %assemble.8 = bf16[1024,4096]{1,0:T(8,128)(2,1)} custom-call(s32[15]{0:T(128)} %stack.170.place_ref, bf16[128,4096]{1,0:T(8,128)(2,1)} %refs_0_.4, bf16[64,4096]{1,0:T(8,128)(2,1)} %copy-done.18, bf16[64,4096]{1,0:T(8,128)(2,1)} %collective-permute-done.36.refs_2_, bf16[64,4096]{1,0:T(8,128)(2,1)} %collective-permute-done.37.refs_3_, ...), custom_call_target="tpu_custom_call" | custom-call | tf_op jit(solution)/shard_map/assemble/pallas_call | solution.py:155
  687.3 20.1 %multiply_convert_fusion.1 = (bf16[1024,4096]{1,0:T(8,128)(2,1)}, f32[1024,4096]{1,0:T(8,128)}) fusion(f32[4096]{0:T(1024)S(1)} %bitcast.451, bf16[1024,4096]{1,0:T(8,128)(2,1)} %assemble.8, f32[1024,1024]{0,1:T(8,128)} %copy-done.5, f32[1024]{0:T(1024)S(1)} %get-tuple-element.88, f32[1024]{0:T(1024)S(1)} %get-tuple-element.89, ...), kind=kOutput, calls=%fused_computation.7 | convolution fusion | flops 8620343296 | bytes 37781504 | tf_op jit(solution)/shard_map/dot_general | solution.py:23
  709.2 256.0 %assemble.9 = bf16[4096,1024]{1,0:T(8,128)(2,1)} custom-call(s32[15]{0:T(128)} %stack.195.place_ref, bf16[512,1024]{1,0:T(8,128)(2,1)} %refs_0_.5, bf16[256,1024]{1,0:T(8,128)(2,1)} %collective-permute-done.49.refs_1_, bf16[256,1024]{1,0:T(8,128)(2,1)} %collective-permute-done.50.refs_2_, bf16[256,1024]{1,0:T(8,128)(2,1)} %collective-permute-done.51.refs_3_, ...), custom_call_target="tpu_custom_call" | custom-call | tf_op jit(solution)/shard_map/assemble/pallas_call | solution.py:155
  965.2 16.3 %fusion.117 = (f32[1024]{0:T(1024)S(1)}, f32[1024,1024]{0,1:T(8,128)}) fusion(f32[1024]{0:T(1024)S(1)} %get-tuple-element.87, bf16[1024,4096]{1,0:T(8,128)(2,1)} %get-tuple-element.111, bf16[4096,1024]{1,0:T(8,128)(2,1)} %assemble.9, f32[1024]{0:T(1024)S(1)} %get-tuple-element.88, f32[1024]{0:T(1024)S(1)} %get-tuple-element.89, ...), kind=kOutput, calls=%fused_computation.269 | convolution fusion | flops 8597273600 | bytes 25190400 | tf_op jit(solution)/shard_map/dot_general | solution.py:23
  991.3 19.3 %fusion.118 = (bf16[4096]{0:T(1024)(128)(2,1)S(1)}, bf16[1024,4096]{1,0:T(8,128)(2,1)}) fusion(f32[1024,4096]{1,0:T(8,128)} %get-tuple-element.112, f32[4096]{0:T(1024)S(1)} %bitcast.452, bf16[1024,1024]{0,1:T(8,128)(2,1)S(1)} %get-tuple-element.46, bf16[4096,1024]{1,0:T(8,128)(2,1)S(1)} %bitcast.426), kind=kOutput, calls=%fused_computation.270 | convolution fusion | flops 8648650752 | bytes 35676160 | tf_op jit(solution)/shard_map/dot_general | solution.py:31
  1010.7 17.5 %multiply_reduce_fusion = (bf16[1024]{0:T(1024)(128)(2,1)S(1)}, f32[1024]{0:T(1024)S(1)}, f32[1024]{0:T(1024)S(1)}, bf16[1024]{0:T(1024)(128)(2,1)S(1)}, f32[1024,1024]{0,1:T(8,128)}) fusion(f32[1024,1024]{0,1:T(8,128)S(1)} %copy-done.6, f32[1024]{0:T(1024)S(1)} %add_rsqrt_fusion.1, f32[1024]{0:T(1024)S(1)} %broadcast_multiply_fusion.5, ...), kind=kOutput, calls=%fused_computation.25 | convolution fusion | flops 8608804864 | bytes 31502336 | tf_op jit(solution)/shard_map/dot_general | solution.py:31
  1034.4 36.0 %attend_back.1 = bf16[1024,3072]{1,0:T(8,128)(2,1)S(1)} custom-call(bf16[1024,3072]{1,0:T(8,128)(2,1)} %copy-done, bf16[1024,3072]{1,0:T(8,128)(2,1)} %copy-done, bf16[1024,3072]{1,0:T(8,128)(2,1)} %copy-done, bf16[1024,1024]{1,0:T(8,128)(2,1)S(1)} %convolution_convert_fusion.4.d_ref, f32[16,2,512]{2,1,0:T(2,128)S(1)} %get-tuple-element.20.lse_ref), custom_call_target="tpu_custom_call" | custom-call | tf_op jit(solution)/shard_map/attend_back/pallas_call | solution.py:128
  1070.5 7.9 add_convert_fusion.1
  1078.3 8.9 convolution_convert_fusion.2
  1091.1 6.1 convolution_convert_fusion.3
  1097.2 15.1 %convolution_convert_fusion.1 = bf16[1024,4096]{1,0:T(8,128)(2,1)} fusion(bf16[1024,4096]{1,0:T(8,128)(2,1)} %get-tuple-element.117, f32[1024,1024]{0,1:T(8,128)S(1)} %copy-done.7, f32[1024]{0:T(1024)S(1)} %get-tuple-element.88, f32[1024]{0:T(1024)S(1)} %get-tuple-element.89, f32[1024]{0:T(1024)S(1)} %add_rsqrt_fusion.1, f32[1024]{0:T(1024)S(1)} %broadcast_multiply_fusion.5), kind=kOutput, calls=%fused_computation.11 | convolution fusion | flops 8599371776 | bytes 20987904 | tf_op jit(solution)/shard_map/dot_general | solution.py:27
  1112.4 11.6 convolution_convert_fusion
  1128.1 4.9 dynamic-slice_bitcast_fusion.1
  1185.3 4.8 collective-permute-done.64
  1195.0 6.6 collective-permute-done.65
  1225.7 7.6 collective-permute-done.104
  1236.2 5.6 collective-permute-done.67
  1244.2 5.7 collective-permute-done.95
  1253.8 5.9 collective-permute-done.105
  1262.4 8.5 collective-permute-done.96
  1274.8 7.4 collective-permute-done.106
  1301.9 4.9 collective-permute-done.101
  1308.2 7.0 collective-permute-done.111
  (465 shorter events, 238.8 us)
Async XLA Ops:
  35.2 32.8 %collective-permute-start.35 = (bf16[64,4096]{1,0:T(8,128)(2,1)S(1)}, bf16[64,4096]{1,0:T(8,128)(2,1)S(1)}, u32[]{:S(2)}, u32[]{:S(2)}) collective-permute-start(bf16[64,4096]{1,0:T(8,128)(2,1)S(1)} %constant_dynamic-slice_fusion.17), channel_id=1, source_target_pairs={{0,2},{2,4},{4,6},{6,7},{7,5},{5,3},{3,1},{1,0},{8,9},{10,8},{12,1... | collective-permute-start | bytes 1572872 | tf_op jit(solution)/shard_map/ppermute | solution.py:190
  36.8 24.6 %collective-permute-start.8 = (bf16[64,3072]{1,0:T(8,128)(2,1)S(1)}, bf16[64,3072]{1,0:T(8,128)(2,1)}, u32[]{:S(2)}, u32[]{:S(2)}) collective-permute-start(bf16[64,3072]{1,0:T(8,128)(2,1)S(1)} %constant_dynamic-slice_fusion.19), channel_id=1, source_target_pairs={{0,1},{2,0},{4,2},{6,4},{7,6},{5,7},{3,5},{1,3},{8,10},{10,12},{12... | collective-permute-start | bytes 1179656 | tf_op jit(solution)/shard_map/ppermute | solution.py:190
  37.3 26.1 %collective-permute-start.2 = (bf16[64,3072]{1,0:T(8,128)(2,1)S(1)}, bf16[64,3072]{1,0:T(8,128)(2,1)}, u32[]{:S(2)}, u32[]{:S(2)}) collective-permute-start(bf16[64,3072]{1,0:T(8,128)(2,1)S(1)} %collective-permute-done.refs_1_), channel_id=1, source_target_pairs={{0,2},{2,4},{4,6},{6,7},{7,5},{5,3},{3,1},{1,0},{8,9},{10,8},{12,1... | collective-permute-start | bytes 1179656 | tf_op jit(solution)/shard_map/ppermute | solution.py:190
  40.5 27.5 %collective-permute-start.43 = (bf16[64,4096]{1,0:T(8,128)(2,1)S(1)}, bf16[64,4096]{1,0:T(8,128)(2,1)S(1)}, u32[]{:S(2)}, u32[]{:S(2)}) collective-permute-start(bf16[64,4096]{1,0:T(8,128)(2,1)S(1)} %constant_dynamic-slice_fusion.17), channel_id=1, source_target_pairs={{0,1},{2,0},{4,2},{6,4},{7,6},{5,7},{3,5},{1,3},{8,10},{10,12},{12... | collective-permute-start | bytes 1572872 | tf_op jit(solution)/shard_map/ppermute | solution.py:190
  85.0 24.7 %collective-permute-start.3 = (bf16[64,3072]{1,0:T(8,128)(2,1)}, bf16[64,3072]{1,0:T(8,128)(2,1)}, u32[]{:S(2)}, u32[]{:S(2)}) collective-permute-start(bf16[64,3072]{1,0:T(8,128)(2,1)} %collective-permute-done.2.refs_3_), channel_id=1, source_target_pairs={{0,8},{1,9},{2,10},{3,11},{4,12},{5,13},{6,14},{7,15},{8,0},{9,1},... | collective-permute-start | bytes 1179656 | tf_op jit(solution)/shard_map/ppermute | solution.py:197
  85.1 26.0 %collective-permute-start.11 = (bf16[64,3072]{1,0:T(8,128)(2,1)}, bf16[64,3072]{1,0:T(8,128)(2,1)}, u32[]{:S(2)}, u32[]{:S(2)}) collective-permute-start(bf16[64,3072]{1,0:T(8,128)(2,1)} %collective-permute-done.10.refs_11_), channel_id=1, source_target_pairs={{0,8},{1,9},{2,10},{3,11},{4,12},{5,13},{6,14},{7,15},{8,0},{9,1},... | collective-permute-start | bytes 1179656 | tf_op jit(solution)/shard_map/ppermute | solution.py:197
  85.6 25.7 %collective-permute-start.5 = (bf16[64,3072]{1,0:T(8,128)(2,1)}, bf16[64,3072]{1,0:T(8,128)(2,1)}, u32[]{:S(2)}, u32[]{:S(2)}) collective-permute-start(bf16[64,3072]{1,0:T(8,128)(2,1)} %collective-permute-done.4.refs_5_), channel_id=1, source_target_pairs={{0,8},{1,9},{2,10},{3,11},{4,12},{5,13},{6,14},{7,15},{8,0},{9,1},... | collective-permute-start | bytes 1179656 | tf_op jit(solution)/shard_map/ppermute | solution.py:197
  109.7 262.6 %collective-permute-start.57 = (bf16[256,1024]{1,0:T(8,128)(2,1)}, bf16[256,1024]{1,0:T(8,128)(2,1)S(1)}, u32[]{:S(2)}, u32[]{:S(2)}) collective-permute-start(bf16[256,1024]{1,0:T(8,128)(2,1)} %copy-done.33), channel_id=1, source_target_pairs={{0,1},{2,0},{4,2},{6,4},{7,6},{5,7},{3,5},{1,3},{8,10},{10,12},{12... | collective-permute-start | bytes 1572872 | tf_op jit(solution)/shard_map/ppermute | solution.py:190
  111.1 261.9 %collective-permute-start.36 = (bf16[64,4096]{1,0:T(8,128)(2,1)S(1)}, bf16[64,4096]{1,0:T(8,128)(2,1)}, u32[]{:S(2)}, u32[]{:S(2)}) collective-permute-start(bf16[64,4096]{1,0:T(8,128)(2,1)S(1)} %collective-permute-done.35.refs_1_), channel_id=1, source_target_pairs={{0,8},{1,9},{2,10},{3,11},{4,12},{5,13},{6,14},{7,15},{8,0},{9,1},... | collective-permute-start | bytes 1572872 | tf_op jit(solution)/shard_map/ppermute | solution.py:197
  111.3 263.1 %collective-permute-start.37 = (bf16[64,4096]{1,0:T(8,128)(2,1)S(1)}, bf16[64,4096]{1,0:T(8,128)(2,1)}, u32[]{:S(2)}, u32[]{:S(2)}) collective-permute-start(bf16[64,4096]{1,0:T(8,128)(2,1)S(1)} %collective-permute-done.35.refs_1_), channel_id=1, source_target_pairs={{0,2},{2,4},{4,6},{6,7},{7,5},{5,3},{3,1},{1,0},{8,9},{10,8},{12,1... | collective-permute-start | bytes 1572872 | tf_op jit(solution)/shard_map/ppermute | solution.py:190
  112.9 261.6 %collective-permute-start.44 = (bf16[64,4096]{1,0:T(8,128)(2,1)}, bf16[64,4096]{1,0:T(8,128)(2,1)}, u32[]{:S(2)}, u32[]{:S(2)}) collective-permute-start(bf16[64,4096]{1,0:T(8,128)(2,1)} %copy-done.19), channel_id=1, source_target_pairs={{0,8},{1,9},{2,10},{3,11},{4,12},{5,13},{6,14},{7,15},{8,0},{9,1},... | collective-permute-start | bytes 1572872 | tf_op jit(solution)/shard_map/ppermute | solution.py:197
  112.9 262.3 %collective-permute-start.45 = (bf16[64,4096]{1,0:T(8,128)(2,1)}, bf16[64,4096]{1,0:T(8,128)(2,1)}, u32[]{:S(2)}, u32[]{:S(2)}) collective-permute-start(bf16[64,4096]{1,0:T(8,128)(2,1)} %copy-done.19), channel_id=1, source_target_pairs={{0,1},{2,0},{4,2},{6,4},{7,6},{5,7},{3,5},{1,3},{8,10},{10,12},{12... | collective-permute-start | bytes 1572872 | tf_op jit(solution)/shard_map/ppermute | solution.py:190
  372.3 37.0 %collective-permute-start.51 = (bf16[256,1024]{1,0:T(8,128)(2,1)}, bf16[256,1024]{1,0:T(8,128)(2,1)}, u32[]{:S(2)}, u32[]{:S(2)}) collective-permute-start(bf16[256,1024]{1,0:T(8,128)(2,1)} %collective-permute-done.49.refs_1_), channel_id=1, source_target_pairs={{0,2},{2,4},{4,6},{6,7},{7,5},{5,3},{3,1},{1,0},{8,9},{10,8},{12,1... | collective-permute-start | bytes 1572872 | tf_op jit(solution)/shard_map/ppermute | solution.py:190
  373.0 36.3 %collective-permute-start.59 = (bf16[256,1024]{1,0:T(8,128)(2,1)S(1)}, bf16[256,1024]{1,0:T(8,128)(2,1)}, u32[]{:S(2)}, u32[]{:S(2)}) collective-permute-start(bf16[256,1024]{1,0:T(8,128)(2,1)S(1)} %collective-permute-done.57.refs_9_), channel_id=1, source_target_pairs={{0,1},{2,0},{4,2},{6,4},{7,6},{5,7},{3,5},{1,3},{8,10},{10,12},{12... | collective-permute-start | bytes 1572872 | tf_op jit(solution)/shard_map/ppermute | solution.py:190
  374.4 36.5 %collective-permute-start.38 = (bf16[64,4096]{1,0:T(8,128)(2,1)}, bf16[64,4096]{1,0:T(8,128)(2,1)S(1)}, u32[]{:S(2)}, u32[]{:S(2)}) collective-permute-start(bf16[64,4096]{1,0:T(8,128)(2,1)} %collective-permute-done.37.refs_3_), channel_id=1, source_target_pairs={{0,8},{1,9},{2,10},{3,11},{4,12},{5,13},{6,14},{7,15},{8,0},{9,1},... | collective-permute-start | bytes 1572872 | tf_op jit(solution)/shard_map/ppermute | solution.py:197
  374.5 35.6 %collective-permute-start.39 = (bf16[64,4096]{1,0:T(8,128)(2,1)}, bf16[64,4096]{1,0:T(8,128)(2,1)S(1)}, u32[]{:S(2)}, u32[]{:S(2)}) collective-permute-start(bf16[64,4096]{1,0:T(8,128)(2,1)} %collective-permute-done.37.refs_3_), channel_id=1, source_target_pairs={{0,2},{2,4},{4,6},{6,7},{7,5},{5,3},{3,1},{1,0},{8,9},{10,8},{12,1... | collective-permute-start | bytes 1572872 | tf_op jit(solution)/shard_map/ppermute | solution.py:190
  375.2 36.8 %collective-permute-start.47 = (bf16[64,4096]{1,0:T(8,128)(2,1)}, bf16[64,4096]{1,0:T(8,128)(2,1)S(1)}, u32[]{:S(2)}, u32[]{:S(2)}) collective-permute-start(bf16[64,4096]{1,0:T(8,128)(2,1)} %collective-permute-done.45.refs_11_), channel_id=1, source_target_pairs={{0,1},{2,0},{4,2},{6,4},{7,6},{5,7},{3,5},{1,3},{8,10},{10,12},{12... | collective-permute-start | bytes 1572872 | tf_op jit(solution)/shard_map/ppermute | solution.py:190
  415.2 271.0 %collective-permute-start.50 = (bf16[256,1024]{1,0:T(8,128)(2,1)}, bf16[256,1024]{1,0:T(8,128)(2,1)}, u32[]{:S(2)}, u32[]{:S(2)}) collective-permute-start(bf16[256,1024]{1,0:T(8,128)(2,1)} %collective-permute-done.49.refs_1_), channel_id=1, source_target_pairs={{0,8},{1,9},{2,10},{3,11},{4,12},{5,13},{6,14},{7,15},{8,0},{9,1},... | collective-permute-start | bytes 1572872 | tf_op jit(solution)/shard_map/ppermute | solution.py:197
  418.8 267.8 %collective-permute-start.58 = (bf16[256,1024]{1,0:T(8,128)(2,1)S(1)}, bf16[256,1024]{1,0:T(8,128)(2,1)}, u32[]{:S(2)}, u32[]{:S(2)}) collective-permute-start(bf16[256,1024]{1,0:T(8,128)(2,1)S(1)} %collective-permute-done.57.refs_9_), channel_id=1, source_target_pairs={{0,8},{1,9},{2,10},{3,11},{4,12},{5,13},{6,14},{7,15},{8,0},{9,1},... | collective-permute-start | bytes 1572872 | tf_op jit(solution)/shard_map/ppermute | solution.py:197
  418.9 268.0 %collective-permute-start.61 = (bf16[256,1024]{1,0:T(8,128)(2,1)}, bf16[256,1024]{1,0:T(8,128)(2,1)}, u32[]{:S(2)}, u32[]{:S(2)}) collective-permute-start(bf16[256,1024]{1,0:T(8,128)(2,1)} %collective-permute-done.59.refs_11_), channel_id=1, source_target_pairs={{0,1},{2,0},{4,2},{6,4},{7,6},{5,7},{3,5},{1,3},{8,10},{10,12},{12... | collective-permute-start | bytes 1572872 | tf_op jit(solution)/shard_map/ppermute | solution.py:190
  426.7 260.5 %collective-permute-start.55 = (bf16[256,1024]{1,0:T(8,128)(2,1)S(1)}, bf16[256,1024]{1,0:T(8,128)(2,1)}, u32[]{:S(2)}, u32[]{:S(2)}) collective-permute-start(bf16[256,1024]{1,0:T(8,128)(2,1)S(1)} %collective-permute-done.53.refs_5_), channel_id=1, source_target_pairs={{0,2},{2,4},{4,6},{6,7},{7,5},{5,3},{3,1},{1,0},{8,9},{10,8},{12,1... | collective-permute-start | bytes 1572872 | tf_op jit(solution)/shard_map/ppermute | solution.py:190
  430.1 277.4 %collective-permute-start.52 = (bf16[256,1024]{1,0:T(8,128)(2,1)}, bf16[256,1024]{1,0:T(8,128)(2,1)}, u32[]{:S(2)}, u32[]{:S(2)}) collective-permute-start(bf16[256,1024]{1,0:T(8,128)(2,1)} %collective-permute-done.51.refs_3_), channel_id=1, source_target_pairs={{0,8},{1,9},{2,10},{3,11},{4,12},{5,13},{6,14},{7,15},{8,0},{9,1},... | collective-permute-start | bytes 1572872 | tf_op jit(solution)/shard_map/ppermute | solution.py:197
  687.2 21.9 %collective-permute-start.56 = (bf16[256,1024]{1,0:T(8,128)(2,1)}, bf16[256,1024]{1,0:T(8,128)(2,1)}, u32[]{:S(2)}, u32[]{:S(2)}) collective-permute-start(bf16[256,1024]{1,0:T(8,128)(2,1)} %collective-permute-done.55.refs_7_), channel_id=1, source_target_pairs={{0,8},{1,9},{2,10},{3,11},{4,12},{5,13},{6,14},{7,15},{8,0},{9,1},... | collective-permute-start | bytes 1572872 | tf_op jit(solution)/shard_map/ppermute | solution.py:197
  1125.9 55.2 %collective-permute-start.63 = (bf16[8,64,3072]{2,1,0:T(8,128)(2,1)}, bf16[8,64,3072]{2,1,0:T(8,128)(2,1)}, u32[]{:S(2)}, u32[]{:S(2)}) collective-permute-start(bf16[8,64,3072]{2,1,0:T(8,128)(2,1)} %dynamic-slice_bitcast_fusion.2), channel_id=1, source_target_pairs={{0,8},{1,9},{2,10},{3,11},{4,12},{5,13},{6,14},{7,15},{8,0},{9,1},... | collective-permute-start | bytes 9437192 | tf_op jit(solution)/shard_map/ppermute | solution.py:197
  1139.6 65.5 %collective-permute-start.93 = (bf16[8,64,4096]{2,1,0:T(8,128)(2,1)}, bf16[8,64,4096]{2,1,0:T(8,128)(2,1)S(1)}, u32[]{:S(2)}, u32[]{:S(2)}) collective-permute-start(bf16[8,64,4096]{2,1,0:T(8,128)(2,1)} %dynamic-slice_bitcast_fusion.1), channel_id=1, source_target_pairs={{0,8},{1,9},{2,10},{3,11},{4,12},{5,13},{6,14},{7,15},{8,0},{9,1},... | collective-permute-start | bytes 12582920 | tf_op jit(solution)/shard_map/ppermute | solution.py:197
  1144.5 63.2 %collective-permute-start.103 = (bf16[8,256,1024]{2,1,0:T(8,128)(2,1)S(1)}, bf16[8,256,1024]{2,1,0:T(8,128)(2,1)S(1)}, u32[]{:S(2)}, u32[]{:S(2)}) collective-permute-start(bf16[8,256,1024]{2,1,0:T(8,128)(2,1)S(1)} %dynamic-slice_bitcast_fusion), channel_id=1, source_target_pairs={{0,8},{1,9},{2,10},{3,11},{4,12},{5,13},{6,14},{7,15},{8,0},{9,1},... | collective-permute-start | bytes 12582920 | tf_op jit(solution)/shard_map/ppermute | solution.py:197
  1207.9 25.5 %collective-permute-start.104 = (bf16[256,1024]{1,0:T(8,128)(2,1)S(1)}, bf16[256,1024]{1,0:T(8,128)(2,1)S(1)}, u32[]{:S(2)}, u32[]{:S(2)}) collective-permute-start(bf16[256,1024]{1,0:T(8,128)(2,1)S(1)} %fusion.25), channel_id=1, source_target_pairs={{0,2},{2,4},{4,6},{6,7},{7,5},{5,3},{3,1},{1,0},{8,9},{10,8},{12,1... | collective-permute-start | bytes 1572872 | tf_op jit(solution)/shard_map/ppermute | solution.py:190
  1218.7 23.0 %collective-permute-start.67 = (bf16[64,3072]{1,0:T(8,128)(2,1)S(1)}, bf16[64,3072]{1,0:T(8,128)(2,1)S(1)}, u32[]{:S(2)}, u32[]{:S(2)}) collective-permute-start(bf16[64,3072]{1,0:T(8,128)(2,1)S(1)} %get-tuple-element.61), channel_id=1, source_target_pairs={{0,2},{2,4},{4,6},{6,7},{7,5},{5,3},{3,1},{1,0},{8,9},{10,8},{12,1... | collective-permute-start | bytes 1179656 | tf_op jit(solution)/shard_map/ppermute | solution.py:190
  1223.7 26.2 %collective-permute-start.95 = (bf16[64,4096]{1,0:T(8,128)(2,1)S(1)}, bf16[64,4096]{1,0:T(8,128)(2,1)S(1)}, u32[]{:S(2)}, u32[]{:S(2)}) collective-permute-start(bf16[64,4096]{1,0:T(8,128)(2,1)S(1)} %get-tuple-element.59), channel_id=1, source_target_pairs={{0,2},{2,4},{4,6},{6,7},{7,5},{5,3},{3,1},{1,0},{8,9},{10,8},{12,1... | collective-permute-start | bytes 1572872 | tf_op jit(solution)/shard_map/ppermute | solution.py:190
  1224.8 25.1 %collective-permute-start.98 = (bf16[64,4096]{1,0:T(8,128)(2,1)S(1)}, bf16[64,4096]{1,0:T(8,128)(2,1)S(1)}, u32[]{:S(2)}, u32[]{:S(2)}) collective-permute-start(bf16[64,4096]{1,0:T(8,128)(2,1)S(1)} %get-tuple-element.60), channel_id=1, source_target_pairs={{0,1},{2,0},{4,2},{6,4},{7,6},{5,7},{3,5},{1,3},{8,10},{10,12},{12... | collective-permute-start | bytes 1572872 | tf_op jit(solution)/shard_map/ppermute | solution.py:190
  1233.9 25.8 %collective-permute-start.105 = (bf16[256,1024]{1,0:T(8,128)(2,1)S(1)}, bf16[256,1024]{1,0:T(8,128)(2,1)S(1)}, u32[]{:S(2)}, u32[]{:S(2)}) collective-permute-start(bf16[256,1024]{1,0:T(8,128)(2,1)S(1)} %get-tuple-element.53), channel_id=1, source_target_pairs={{0,2},{2,4},{4,6},{6,7},{7,5},{5,3},{3,1},{1,0},{8,9},{10,8},{12,1... | collective-permute-start | bytes 1572872 | tf_op jit(solution)/shard_map/ppermute | solution.py:190
  1235.0 24.7 %collective-permute-start.108 = (bf16[256,1024]{1,0:T(8,128)(2,1)S(1)}, bf16[256,1024]{1,0:T(8,128)(2,1)S(1)}, u32[]{:S(2)}, u32[]{:S(2)}) collective-permute-start(bf16[256,1024]{1,0:T(8,128)(2,1)S(1)} %get-tuple-element.54), channel_id=1, source_target_pairs={{0,1},{2,0},{4,2},{6,4},{7,6},{5,7},{3,5},{1,3},{8,10},{10,12},{12... | collective-permute-start | bytes 1572872 | tf_op jit(solution)/shard_map/ppermute | solution.py:190
  (152 other events, 2544.5 us)

commit v2 on v1

--- a/solution.py
+++ b/solution.py
@@ -12,7 +12,9 @@
 DH = 64
 SEQ = 512
 LANES = 128
-PAIRS = D // LANES
+GROUPS = 2
+PAIRS = D // LANES // GROUPS
+WIDE = D // GROUPS
 AXES = ("rep", "shard")
 RING_MOST = 16
 LOW = jnp.bfloat16
@@ -53,7 +55,8 @@
     return (lane // DH) == head
 
 
-def attend_kernel(query_ref, key_ref, value_ref, out_ref, lse_ref):
+def attend_kernel(query_ref, key_ref, value_ref, *rest):
+    out_ref, lse_ref = rest[-2:]
     query = query_ref[...] * LOW(0.125)
     key = key_ref[...]
     value_t = value_ref[...].T
@@ -95,71 +98,81 @@
         d_query.append(project(key_t[head * DH : (head + 1) * DH], d_scores))
     d_query = jnp.concatenate(d_query, axis=0).T * 0.125
     for place, grad in enumerate((d_query, d_key, d_value)):
-        start = pl.multiple_of(place * D + pair * LANES, LANES)
+        start = pl.multiple_of(place * WIDE + pair * LANES, LANES)
         out_ref[:, pl.ds(start, LANES)] = grad.astype(LOW)
 
 
-def column_block(place):
-    return pl.BlockSpec((SEQ, LANES), lambda seq, pair: (seq, place * PAIRS + pair))
+def column_block(first):
+    return pl.BlockSpec((SEQ, LANES), lambda seq, pair: (seq, first + pair))
 
 
 LSE_BLOCK = pl.BlockSpec((1, LANES // DH, SEQ), lambda seq, pair: (seq * PAIRS + pair, 0, 0))
 
 
-def attend(qkv):
+def triple():
+    return [column_block(place * PAIRS) for place in range(3)]
+
+
+def attend(qkv, group, before):
     count = qkv.shape[0]
     seqs = count // SEQ
+    kept = [] if before is None else [before]
     return pl.pallas_call(
         attend_kernel,
         grid=(seqs, PAIRS),
-        in_specs=[column_block(0), column_block(1), column_block(2)],
-        out_specs=[column_block(0), LSE_BLOCK],
+        in_specs=triple() + [pl.BlockSpec(memory_space=pl.ANY)] * len(kept),
+        out_specs=[column_block(group * PAIRS), LSE_BLOCK],
         out_shape=[
             jax.ShapeDtypeStruct((count, D), LOW),
             jax.ShapeDtypeStruct((seqs * PAIRS, LANES // DH, SEQ), FULL),
         ],
+        input_output_aliases={3: 0} if kept else {},
         compiler_params=pltpu.CompilerParams(vmem_limit_bytes=32 * 2**20),
         name="attend",
-    )(qkv, qkv, qkv)
-
-
-def attend_back(qkv, d_attended, lse):
+    )(qkv, qkv, qkv, *kept)
+
+
+def attend_back(qkv, d_attended, lse, group):
     count = qkv.shape[0]
     return pl.pallas_call(
         attend_back_kernel,
         grid=(count // SEQ, PAIRS),
-        in_specs=[column_block(0), column_block(1), column_block(2), column_block(0), LSE_BLOCK],
-        out_specs=pl.BlockSpec((SEQ, 3 * D), lambda seq, pair: (seq, 0)),
-        out_shape=jax.ShapeDtypeStruct((count, 3 * D), LOW),
+        in_specs=triple() + [column_block(group * PAIRS), LSE_BLOCK],
+        out_specs=pl.BlockSpec((SEQ, 3 * WIDE), lambda seq, pair: (seq, 0)),
+        out_shape=jax.ShapeDtypeStruct((count, 3 * WIDE), LOW),
         compiler_params=pltpu.CompilerParams(vmem_limit_bytes=40 * 2**20),
         name="attend_back",
     )(qkv, qkv, qkv, d_attended, lse)
 
 
-def assemble_kernel(count, size, place_ref, *refs):
-    chunks, out_ref, sems = refs[:count], refs[count], refs[count + 1]
+def assemble_kernel(moves, align, place_ref, *refs):
+    out_ref, sems = refs[-2], refs[-1]
     copies = []
-    for i in range(count):
-        rows = chunks[i].shape[0]
-        start = pl.multiple_of(place_ref[i], size)
-        copies.append(pltpu.make_async_copy(chunks[i], out_ref.at[pl.ds(start, rows)], sems.at[i]))
+    for i, (which, start, rows) in enumerate(moves):
+        place = pl.multiple_of(place_ref[i], align)
+        source = refs[which].at[pl.ds(start, rows)]
+        copies.append(pltpu.make_async_copy(source, out_ref.at[pl.ds(place, rows)], sems.at[i]))
     for copy in copies:
         copy.start()
     for copy in copies:
         copy.wait()
 
 
-def assemble(chunks, places, rows):
-    count = len(chunks)
-    size = min(chunk.shape[0] for chunk in chunks)
+def assemble(arrays, moves, places, rows):
+    align = min(move[2] for move in moves)
     return pl.pallas_call(
-        functools.partial(assemble_kernel, count, size),
-        in_specs=[pl.BlockSpec(memory_space=pltpu.SMEM)] + [pl.BlockSpec(memory_space=pl.ANY)] * count,
-        out_specs=pl.BlockSpec(memory_space=pl.ANY),
-        out_shape=jax.ShapeDtypeStruct((rows,) + chunks[0].shape[1:], chunks[0].dtype),
-        scratch_shapes=[pltpu.SemaphoreType.DMA((count,))],
+        functools.partial(assemble_kernel, moves, align),
+        in_specs=[pl.BlockSpec(memory_space=pltpu.SMEM)] + [pl.BlockSpec(memory_space=pl.ANY)] * len(arrays),
+        out_specs=pl.BlockSpec(memory_space=pltpu.VMEM),
+        out_shape=jax.ShapeDtypeStruct((rows,) + arrays[0].shape[1:], arrays[0].dtype),
+        scratch_shapes=[pltpu.SemaphoreType.DMA((len(moves),))],
+        compiler_params=pltpu.CompilerParams(vmem_limit_bytes=24 * 2**20),
         name="assemble",
-    )(jnp.stack(places).astype(jnp.int32), *chunks)
+    )(jnp.stack(places).astype(jnp.int32), *arrays)
+
+
+def tie(*values):
+    return lax.optimization_barrier(values)
 
 
 class Links:
@@ -196,48 +209,109 @@
                 pairs.append((rep * self.size + shard, (rep ^ bit) * self.size + shard))
         return lax.ppermute(values, AXES, pairs)
 
-    def round_ring(self, values):
-        found = []
-        for sign, hops in ((1, self.far), (-1, self.near)):
-            moving = values
-            for step in range(1, hops + 1):
-                moving = self.hop(moving, sign)
-                found.append((moving, -sign * step))
-        return found
+    def half_of(self, values):
+        half = values.shape[0] // 2
+        return lax.dynamic_slice_in_dim(values, self.core * half, half, axis=0)
+
 
     def gather_small(self, values):
         if self.direct:
             return lax.all_gather(values, "shard", axis=0, tiled=True)
         rows = values.shape[0]
-        found = [(values, 0)] + self.round_ring(values)
-        chunks = [chunk for chunk, _ in found]
+        found = [(values, 0)]
+        ahead = back = values
+        for step in range(1, self.far + 1):
+            ahead = self.hop(ahead, 1)
+            found.append((ahead, -step))
+            if step <= self.near:
+                back = self.hop(back, -1)
+                found.append((back, step))
+            ahead, back = yield [ahead, back]
+        moves = [(i, 0, rows) for i in range(len(found))]
         places = [self.owner(step) * rows for _, step in found]
-        return assemble(chunks, places, self.size * rows)
+        return assemble([chunk for chunk, _ in found], moves, places, self.size * rows)
 
     def gather(self, values):
         if self.direct:
             return lax.all_gather(values, "shard", axis=0, tiled=True)
         rows = values.shape[0]
         half = rows // 2
-        mine = lax.dynamic_slice_in_dim(values, self.core * half, half, axis=0)
-        chunks = [values]
+        arrays = [values]
+        moves = [(0, 0, rows)]
         places = [self.owner(0) * rows]
-        for chunk, step in self.round_ring(mine):
-            chunks += [chunk, self.swap(chunk, 1)]
-            places.append(self.owner(step) * rows + self.core * half)
-            places.append(self.owner(-step) * rows + (1 - self.core) * half)
-        return assemble(chunks, places, self.size * rows)
-
-    def reduce(self, values):
-        width = values.shape[1]
-        rows = values.shape[0] // self.size
+
+        def keep(chunk, mine, step):
+            moves.append((len(arrays), 0, half))
+            arrays.append(chunk)
+            core = self.core if mine else 1 - self.core
+            places.append(self.owner(step) * rows + core * half)
+
+        ahead = back = self.half_of(values)
+        for step in range(1, self.far + 2):
+            flight = []
+            if step > 1:
+                keep(ahead, True, 1 - step)
+                flight.append((self.swap(ahead, 1), step - 1))
+                if step - 1 <= self.near:
+                    keep(back, True, step - 1)
+                    flight.append((self.swap(back, 1), 1 - step))
+            if step <= self.far:
+                ahead = self.hop(ahead, 1)
+            if step <= self.near:
+                back = self.hop(back, -1)
+            ahead, back, *swapped = yield [ahead, back] + [chunk for chunk, _ in flight]
+            for chunk, (_, place) in zip(swapped, flight):
+                keep(chunk, False, place)
+        return assemble(arrays, moves, places, self.size * rows)
+
+    def gather_halves(self, values):
+        if self.direct:
+            return lax.all_gather(values, "shard", axis=0, tiled=True)
+        rows = values.shape[0]
+        half = rows // 2
+        mine = lax.all_gather(self.half_of(values), "shard", axis=0, tiled=True)
+        other = self.swap(mine, 1)
+        moves, places = [], []
+        for shard in range(self.size):
+            moves += [(0, shard * half, half), (1, shard * half, half)]
+            places += [shard * rows + self.core * half, shard * rows + (1 - self.core) * half]
+        return assemble([mine, other], moves, places, self.size * rows)
+
+    def gather_quarters(self, values):
+        rows = values.shape[0] // self.reps
+        mine = lax.dynamic_slice_in_dim(values, lax.axis_index("rep") * rows, rows, axis=0)
+        return lax.all_gather(mine, ("shard", "rep"), axis=0, tiled=True)
+
+    def reduce_halves(self, values):
         if self.direct:
             own = lax.psum_scatter(values, "shard", scatter_dimension=0, tiled=True)
             return lax.psum(own, "rep").astype(FULL)
-        half = rows // 2
+        width = values.shape[1]
+        half = values.shape[0] // self.size // 2
         split = values.reshape(self.size, 2, half, width)
-        other = lax.dynamic_index_in_dim(split, 1 - self.core, axis=1, keepdims=False)
-        other = self.swap(other, 1)
+        other = self.swap(lax.dynamic_index_in_dim(split, 1 - self.core, axis=1, keepdims=False), 1)
+        (other,) = yield [other]
+        mine = lax.dynamic_index_in_dim(split, self.core, axis=1, keepdims=False)
+        total = (mine.astype(FULL) + other.astype(FULL)).astype(LOW)
+        total = total.reshape(self.size * half, width)
+        return lax.psum_scatter(total, "shard", scatter_dimension=0, tiled=True)
+
+    def finish(self, total):
+        total = (total.astype(FULL) + self.swap(total, 2).astype(FULL)).astype(LOW)
+        pair = self.swap(total, 1)
+        low = jnp.where(self.core == 0, total, pair)
+        high = jnp.where(self.core == 0, pair, total)
+        return jnp.concatenate([low, high], axis=0).astype(FULL)
+
+    def reduce(self, values):
+        if self.direct:
+            own = lax.psum_scatter(values, "shard", scatter_dimension=0, tiled=True)
+            return lax.psum(own, "rep").astype(FULL)
+        width = values.shape[1]
+        half = values.shape[0] // self.size // 2
+        split = values.reshape(self.size, 2, half, width)
+        other = self.swap(lax.dynamic_index_in_dim(split, 1 - self.core, axis=1, keepdims=False), 1)
+        (other,) = yield [other]
 
         def piece(step):
             owner = self.owner(step)
@@ -245,20 +319,60 @@
             pair = lax.dynamic_slice(other, (owner, 0, 0), (1, half, width))
             return own[0, 0].astype(FULL) + pair[0].astype(FULL)
 
-        total = piece(0)
-        for sign, hops in ((1, self.far), (-1, self.near)):
-            moving = piece(sign * hops).astype(LOW)
-            for step in range(hops - 1, -1, -1):
-                moving = self.hop(moving, sign)
+        ahead = piece(self.far).astype(LOW)
+        back = piece(-self.near).astype(LOW)
+        for step in range(self.far - 1, -1, -1):
+            moving = [self.hop(ahead, 1)]
+            if step < self.near:
+                moving.append(self.hop(back, -1))
+            ahead, *rest = yield moving
+            if step > 0:
+                ahead = (ahead.astype(FULL) + piece(step)).astype(LOW)
+            if rest:
+                back = rest[0]
                 if step > 0:
-                    moving = (moving.astype(FULL) + piece(sign * step)).astype(LOW)
-            total = total + moving.astype(FULL)
-        total = total.astype(LOW)
-        total = (total.astype(FULL) + self.swap(total, 2).astype(FULL)).astype(LOW)
-        pair = self.swap(total, 1)
+                    back = (back.astype(FULL) + piece(-step)).astype(LOW)
+        total = (piece(0) + ahead.astype(FULL) + back.astype(FULL)).astype(LOW)
+        (cross,) = yield [self.swap(total, 2)]
+        total = (total.astype(FULL) + cross.astype(FULL)).astype(LOW)
+        (pair,) = yield [self.swap(total, 1)]
         low = jnp.where(self.core == 0, total, pair)
         high = jnp.where(self.core == 0, pair, total)
         return jnp.concatenate([low, high], axis=0).astype(FULL)
+
+
+class Flow:
+    def __init__(self):
+        self.running = {}
+        self.results = {}
+
+    def start(self, name, steps):
+        self._move(name, steps, None)
+
+    def _move(self, name, steps, values):
+        try:
+            self.running[name] = (steps, steps.send(values))
+        except StopIteration as end:
+            self.running.pop(name, None)
+            self.results[name] = end.value
+
+    def advance(self, *values):
+        running = list(self.running.items())
+        flat = list(values)
+        for _, (_, flight) in running:
+            flat += flight
+        tied = tie(*flat) if flat else ()
+        at = len(values)
+        for name, (steps, flight) in running:
+            self._move(name, steps, list(tied[at : at + len(flight)]))
+            at += len(flight)
+        return tied[0] if len(values) == 1 else tuple(tied[: len(values)])
+
+    def take(self, name):
+        while name in self.running:
+            steps, flight = self.running[name]
+            self._move(name, steps, flight)
+        return self.results[name]
 
 
 def shards(
@@ -292,19 +406,45 @@
     room = -(-used // (32 * LANES)) * 32 * LANES
     packed = jnp.pad(packed, (0, room - used)).reshape(room // LANES, LANES)
 
-    whole_qkv = links.gather(jnp.concatenate([w_query, w_key, w_value], axis=1))
-    whole_small = links.gather_small(packed).reshape(size, room).astype(FULL)
-    whole_out = links.gather(w_out)
-    whole_inner = links.gather(w_inner)
-    whole_outer = links.gather(w_outer)
+    own_groups = [
+        jnp.concatenate([w[:, g * WIDE : (g + 1) * WIDE] for w in (w_query, w_key, w_value)], axis=1)
+        for g in range(GROUPS)
+    ]
+    flow = Flow()
+    flow.start("group0", links.gather(own_groups[0]))
+    flow.start("small", links.gather_small(packed))
+    own_groups[1], w_out, w_inner, w_outer = flow.advance(own_groups[1], w_out, w_inner, w_outer)
+    flow.start("group1", links.gather(own_groups[1]))
+    flow.advance()
+    w_inner, w_outer = flow.advance(w_inner, w_outer)
+    whole_inner = links.gather_halves(w_inner)
+    whole_outer = links.gather_quarters(w_outer)
+    flow.advance()
+    whole_groups = [flow.take("group0")]
+    whole_small = flow.take("small").reshape(size, room).astype(FULL)
     (bias_query, bias_value, bias_out, gain_first, shift_first, bias_outer, gain_second, shift_second) = (
         whole_small[:, i * width : (i + 1) * width].reshape(D) for i in range(len(vectors))
     )
     bias_inner = whole_small[:, used - hidden : used].reshape(size * hidden)
 
-    bias_qkv = jnp.concatenate([bias_query, jnp.zeros((D,), FULL), bias_value])
-    qkv = (project(tokens, whole_qkv) + bias_qkv).astype(LOW)
-    attended, lse = attend(qkv)
+    no_bias = jnp.zeros((WIDE,), FULL)
+    projected = []
+    attended, lse = None, []
+    for g in range(GROUPS):
+        columns = slice(g * WIDE, (g + 1) * WIDE)
+        bias = jnp.concatenate([bias_query[columns], no_bias, bias_value[columns]])
+        projected.append((project(tokens, whole_groups[g]) + bias).astype(LOW))
+        if g == 0:
+            projected[g], w_out = flow.advance(projected[g], w_out)
+            flow.start("out", links.gather(w_out))
+        else:
+            projected[g] = flow.advance(projected[g])
+        attended, kept = attend(projected[g], g, attended)
+        lse.append(kept)
+        attended = flow.advance(attended)
+        if g == 0:
+            whole_groups.append(flow.take("group1"))
+    whole_out = flow.take("out")
     branch = project(attended, whole_out) + bias_out
     unit_one, inverse_one = normal(tokens.astype(FULL) + branch)
     first = unit_one * gain_first + shift_first
@@ -322,27 +462,46 @@
     grad_shift_two = jnp.sum(cot, axis=0)
     d_second = normal_back(cot * gain_second, unit_two, inverse_two)
     d_mid = d_second.astype(LOW)
-    own_outer = links.reduce(gram(active, d_mid).astype(LOW))
+    grad_outer = gram(active, d_mid).astype(LOW)
+    grad_outer, d_mid = tie(grad_outer, d_mid)
+    flow.start("outer", links.reduce(grad_outer))
     grad_b_outer = column_sum(d_mid)
     d_pre = (against(d_mid, whole_outer) * slope.astype(FULL)).astype(LOW)
-    own_inner = links.reduce(gram(first_low, d_pre).astype(LOW))
+    d_pre = flow.advance(d_pre)
+    grad_inner = gram(first_low, d_pre).astype(LOW)
+    grad_inner, d_pre = flow.advance(grad_inner, d_pre)
+    flow.start("inner", links.reduce(grad_inner))
     grad_b_inner = column_sum(d_pre)
     d_first = d_second + against(d_pre, whole_inner)
+    d_first = flow.advance(d_first)
     grad_gain_one = jnp.sum(d_first * unit_one, axis=0)
     grad_shift_one = jnp.sum(d_first, axis=0)
     d_inner = normal_back(d_first * gain_first, unit_one, inverse_one)
     d_branch = d_inner.astype(LOW)
-    own_out = links.reduce(gram(attended, d_branch).astype(LOW))
+    grad_out = gram(attended, d_branch).astype(LOW)
+    grad_out, d_branch = flow.advance(grad_out, d_branch)
+    flow.start("out_back", links.reduce(grad_out))
     grad_b_out = column_sum(d_branch)
     d_attended = against(d_branch, whole_out).astype(LOW)
-    d_qkv = attend_back(qkv, d_attended, lse)
-    own_qkv = links.reduce(gram(tokens, d_qkv).astype(LOW))
-    grad_b_qkv = column_sum(d_qkv)
-    d_tokens = (d_inner + against(d_qkv, whole_qkv)).astype(LOW)
+    grad_b_groups = []
+    d_tokens = d_inner
+    for g in range(GROUPS):
+        d_group = attend_back(projected[g], d_attended, lse[g], g)
+        d_group = flow.advance(d_group)
+        grad_group = gram(tokens, d_group).astype(LOW)
+        grad_group, d_group, d_attended = flow.advance(grad_group, d_group, d_attended)
+        flow.start(f"back{g}", links.reduce(grad_group))
+        grad_b_groups.append(column_sum(d_group))
+        d_tokens = d_tokens + against(d_group, whole_groups[g])
+    d_tokens = d_tokens.astype(LOW)
+
+    def joined(parts, place):
+        columns = slice(place * WIDE, (place + 1) * WIDE)
+        return jnp.concatenate([part[..., columns] for part in parts], axis=-1)
 
     grads = (
-        grad_b_qkv[:D],
-        grad_b_qkv[2 * D :],
+        joined(grad_b_groups, 0),
+        joined(grad_b_groups, 2),
         grad_b_out,
         grad_gain_one,
         grad_shift_one,
@@ -354,7 +513,12 @@
         [grad.reshape(size, width) for grad in grads] + [grad_b_inner.reshape(size, hidden)], axis=1
     )
     small = jnp.pad(small, ((0, 0), (0, room - used))).astype(LOW)
-    own_small = links.reduce(small.reshape(size * (room // LANES), LANES)).reshape(room)
+    flow.start("small_back", links.reduce(small.reshape(size * (room // LANES), LANES)))
+    own_outer = flow.take("outer")
+    own_inner = flow.take("inner")
+    own_out = flow.take("out_back")
+    own_small = flow.take("small_back").reshape(room)
+    own_groups = [flow.take(f"back{g}") for g in range(GROUPS)]
     (
         own_bias_query,
         own_bias_value,
@@ -369,9 +533,9 @@
     return (
         output,
         d_tokens,
-        own_qkv[:, :D],
-        own_qkv[:, D : 2 * D],
-        own_qkv[:, 2 * D :],
+        joined(own_groups, 0),
+        joined(own_groups, 1),
+        joined(own_groups, 2),
         own_bias_query,
         own_bias_value,
         own_out,

time: 1330 us -> 637 us (0.48)
  Pallas kernels: 833 us -> 77.3 us
  other arithmetic: 47.3 us -> 85.9 us
  local copies, waits for them, and re-layouts: 45.5 us -> 73.9 us
  between operations: 2.45 us -> 16.2 us
    pallas_call x7 -> x9, Pallas kernels: 833 us -> 77.3 us  [the longest x2 35.6 us: attend_back(): pl.pallas_call(attend_back_kernel, grid=(count // SEQ, PAIRS), in_specs=t...]
    ppermute x70, waiting for transfers between devices: 144 us -> 87.7 us  [hop(): return lax.ppermute(values, AXES, pairs)]
    all_gather x0 -> x2, waiting for transfers between devices: none -> 55.5 us  [the longest x1 55.5 us: gather_halves(): mine = lax.all_gather(self.half_of(values), 'shard', axis=0, tiled=True)]
    convert_element_type x30 -> x38, other arithmetic: 22 us -> 47.3 us  [the longest x5 12.6 us: reduce(): back = (back.astype(FULL) + piece(-step)).astype(LOW)]
    unnamed x168 -> x198, local copies, waits for them, and re-layouts: 26.2 us -> 46.5 us
    dot_general x4 -> x5, matrix products: 47 us -> 56.1 us  [against(): lax.dot_general(left, right, (((1,), (1,)), ((), ())), preferred_element_...]
    dot_general x4 -> x5, matrix products: 41.7 us -> 33.8 us  [gram(): lax.dot_general(left, right, (((0,), (0,)), ((), ())), preferred_element_...]
    dot_general x4 -> x5, matrix products: 48.6 us -> 45.1 us  [project(): return jnp.dot(left, right, preferred_element_type=FULL)]
  transfers between devices with their start and end apart: 113 -> 112, of which waited for: 43 -> 31; matrix products, arithmetic and copies ran while one was open for 7% -> 31% of each run, Pallas kernels for 41% -> 12%
where the time goes in v2:
time: 637 us; the launch traced here: 628 us
  waiting for transfers between devices  157 us (25%)
  matrix products  135 us (21%)
  other arithmetic  85.9 us (13%)
  starting transfers between devices  82.6 us (13%)
  Pallas kernels  77.3 us (12%)
  local copies, waits for them, and re-layouts  73.9 us (12%)
  between operations  16.2 us (3%)
    ppermute x70, waiting for transfers between devices, hop(): return lax.ppermute(values, AXES, pairs)  87.7 us
    ppermute x70, starting transfers between devices, hop(): return lax.ppermute(values, AXES, pairs)  75.3 us
    dot_general x5, matrix products, against(): lax.dot_general(left, right, (((1,), (1,)), ((), ())), preferred_element_...  56.1 us
    all_gather x1, waiting for transfers between devices, gather_halves(): mine = lax.all_gather(self.half_of(values), 'shard', axis=0, tiled=True)  55.5 us
    unnamed x198, local copies, waits for them, and re-layouts  46.5 us
    dot_general x5, matrix products, project(): return jnp.dot(left, right, preferred_element_type=FULL)  45.1 us
    pallas_call x2, Pallas kernels, attend_back(): pl.pallas_call(attend_back_kernel, grid=(count // SEQ, PAIRS), in_specs=t...  35.6 us
    dot_general x5, matrix products, gram(): lax.dot_general(left, right, (((0,), (0,)), ((), ())), preferred_element_...  33.8 us
  transfers between devices with their start and end apart: 112, of which 31 were waited for; matrix products, arithmetic and copies ran while one was open for 31% of the time, Pallas kernels for 12%

profile of v2, /device:TPU:0, one launch (start us, length us, event | category | flops | bytes accessed | tf_op | source)
XLA Modules:
  0.0 627.7 jit_solution(8957333466234158497)
XLA Ops:
  22.1 5.7 collective-permute-done.refs_1_
  70.8 9.6 %collective-permute-done.27.refs_10_ = bf16[64,1536]{1,0:T(8,128)(2,1)S(1)} collective-permute-done((bf16[64,1536]{1,0:T(8,128)(2,1)}, bf16[64,1536]{1,0:T(8,128)(2,1)S(1)}, u32[]{:S(2)}, u32[]{:S(2)}) %collective-permute-start.27) | collective-permute-done | bytes 196640 | tf_op jit(solution)/shard_map/ppermute | solution.py:203
  80.4 55.5 %all-gather.3.cloned.1.call-done.refs_0_ = bf16[512,4096]{1,0:T(8,128)(2,1)} async-done(((bf16[64,4096]{1,0:T(8,128)(2,1)}), bf16[512,4096]{1,0:T(8,128)(2,1)}) %all-gather.3.cloned.1.call-update) | async-done | bytes 4194320 | tf_op jit(solution)/shard_map/all_gather | solution.py:272
  140.9 4.6 assemble.5
  151.6 11.3 %attend.2 = (bf16[1024,1024]{1,0:T(8,128)(2,1)S(1)}, f32[8,2,512]{2,1,0:T(2,128)S(1)}) custom-call(bf16[1024,1536]{1,0:T(8,128)(2,1)S(1)} %fusion.13.query_ref.key_ref.value_ref, bf16[1024,1536]{1,0:T(8,128)(2,1)S(1)} %fusion.13.query_ref.key_ref.value_ref, bf16[1024,1536]{1,0:T(8,128)(2,1)S(1)} %fusion.13.query_ref.key_ref.value_ref), custom_call_target="tpu_custom_call" | custom-call | tf_op jit(solution)/shard_map/attend/pallas_call | solution.py:120
  165.4 4.9 assemble.7
  187.9 11.3 %attend.3 = (bf16[1024,1024]{1,0:T(8,128)(2,1)S(1)}, f32[8,2,512]{2,1,0:T(2,128)S(1)}) custom-call(bf16[1024,1536]{1,0:T(8,128)(2,1)S(1)} %fusion.14.query_ref.key_ref.value_ref, bf16[1024,1536]{1,0:T(8,128)(2,1)S(1)} %fusion.14.query_ref.key_ref.value_ref, ...), custom_call_target="tpu_custom_call", output_to_operand_aliasing={{0}: (3, {})} | custom-call | tf_op jit(solution)/shard_map/attend/pallas_call | solution.py:120
  202.0 5.2 collective-permute-done.47.refs_13_
  218.0 6.2 assemble.9
  224.3 18.7 %multiply_convert_fusion.1 = (bf16[1024,4096]{1,0:T(8,128)(2,1)}, f32[1024,4096]{1,0:T(8,128)}) fusion(f32[4096]{0:T(1024)S(1)} %bitcast.515, bf16[1024,4096]{1,0:T(8,128)(2,1)} %assemble.9, f32[1024,1024]{0,1:T(8,128)S(1)} %get-tuple-element.343, f32[1024]{0:T(1024)S(1)} %get-tuple-element.313, f32[1024]{0:T(1024)S(1)} %get-tuple-element.314, ...), kind=kOutput, calls=%fused_computation.7 | convolution fusion | flops 8620343296 | bytes 37781504 | tf_op jit(solution)/shard_map/dot_general | solution.py:25
  242.9 16.5 %fusion.138 = (f32[1024]{0:T(1024)S(1)}, f32[1024,1024]{0,1:T(8,128)}) fusion(f32[1024]{0:T(1024)S(1)} %copy-done.84, bf16[1024,4096]{1,0:T(8,128)(2,1)} %get-tuple-element.344, bf16[4096,1024]{1,0:T(8,128)(2,1)} %all-gather.5.cloned.1.call-done, f32[1024]{0:T(1024)} %copy-done.82, f32[1024]{0:T(1024)S(1)} %get-tuple-element.314, ...), kind=kOutput, calls=%fused_computation.313 | convolution fusion | flops 8597273600 | bytes 25190400 | tf_op jit(solution)/shard_map/dot_general | solution.py:25
  271.6 10.0 %convolution_convert_fusion.1 = bf16[4096,1024]{1,0:T(8,128)(2,1)S(1)} fusion(bf16[1024,4096]{1,0:T(8,128)(2,1)S(1)} %copy-done.87, bf16[1024,1024]{0,1:T(8,128)(2,1)S(1)} %get-tuple-element.171), kind=kOutput, calls=%fused_computation.10 | convolution fusion | flops 8594128896 | bytes 18874368 | tf_op jit(solution)/shard_map/dot_general | solution.py:29
  286.4 19.8 %multiply_convert_fusion = bf16[1024,4096]{1,0:T(8,128)(2,1)} fusion(f32[1024,4096]{1,0:T(8,128)} %get-tuple-element.345, f32[4096]{0:T(1024)S(1)} %bitcast.516, bf16[1024,1024]{0,1:T(8,128)(2,1)} %copy-done.56, bf16[4096,1024]{1,0:T(8,128)(2,1)} %all-gather.5.cloned.1.call-done), kind=kOutput, calls=%fused_computation.6 | convolution fusion | flops 8644460544 | bytes 35667968 | tf_op jit(solution)/shard_map/dot_general | solution.py:33
  307.9 11.7 %convolution_convert_fusion = bf16[1024,4096]{1,0:T(8,128)(2,1)S(1)} fusion(bf16[1024,4096]{1,0:T(8,128)(2,1)} %multiply_convert_fusion, f32[1024,1024]{0,1:T(8,128)S(1)} %copy-done.48, f32[1024]{0:T(1024)S(1)} %copy-done.83, f32[1024]{0:T(1024)S(1)} %get-tuple-element.314, f32[1024]{0:T(1024)S(1)} %add_rsqrt_fusion.1, f32[1024]{0:T(1024)S(1)} %broadcast_multiply_fusion.5), kind=kOutput, calls=%fused_computation.9 | convolution fusion | flops 8599371776 | bytes 20987904 | tf_op jit(solution)/shard_map/dot_general | solution.py:29
  338.7 17.5 %convolution_add_fusion = f32[1024,1024]{0,1:T(8,128)} fusion(bf16[1024,4096]{1,0:T(8,128)(2,1)} %multiply_convert_fusion, bf16[1024,4096]{1,0:T(8,128)(2,1)} %assemble.9, f32[1024]{0:T(1024)S(1)} %broadcast_multiply_fusion.2, f32[1024]{0:T(1024)S(1)} %add_rsqrt_fusion, f32[1024,1024]{0,1:T(8,128)} %get-tuple-element.347, ...), kind=kOutput, calls=%fused_computation.44 | convolution fusion | flops 8599371776 | bytes 27283456 | tf_op jit(solution)/shard_map/dot_general | solution.py:33
  356.2 4.6 reduce.5
  361.4 5.1 multiply_reduce_fusion
  377.8 6.0 collective-permute-done.55
  403.4 4.8 convolution_convert_fusion.4.d_ref
  408.2 17.8 %attend_back.2 = bf16[1024,1536]{1,0:T(8,128)(2,1)S(1)} custom-call(bf16[1024,1536]{1,0:T(8,128)(2,1)S(1)} %copy-done.3, bf16[1024,1536]{1,0:T(8,128)(2,1)S(1)} %copy-done.3, bf16[1024,1536]{1,0:T(8,128)(2,1)S(1)} %copy-done.3, bf16[1024,1024]{1,0:T(8,128)(2,1)S(1)} %convolution_convert_fusion.4.d_ref, f32[8,2,512]{2,1,0:T(2,128)S(1)} %copy-done.44), custom_call_target="tpu_custom_call" | custom-call | tf_op jit(solution)/shard_map/attend_back/pallas_call | solution.py:137
  437.3 4.9 fusion.15
  442.1 7.4 %collective-permute-done.66 = bf16[64,1024]{1,0:T(8,128)(2,1)S(1)} collective-permute-done((bf16[64,1024]{1,0:T(8,128)(2,1)S(1)}, bf16[64,1024]{1,0:T(8,128)(2,1)S(1)}, u32[]{:S(2)}, u32[]{:S(2)}) %collective-permute-start.66) | collective-permute-done | bytes 131104 | tf_op jit(solution)/shard_map/ppermute | solution.py:203
  450.7 4.7 copy.68
  466.7 5.0 fusion.139
  475.7 17.8 %attend_back.3 = bf16[1024,1536]{1,0:T(8,128)(2,1)S(1)} custom-call(bf16[1024,1536]{1,0:T(8,128)(2,1)S(1)} %fusion.14.query_ref.key_ref.value_ref, bf16[1024,1536]{1,0:T(8,128)(2,1)S(1)} %fusion.14.query_ref.key_ref.value_ref, bf16[1024,1536]{1,0:T(8,128)(2,1)S(1)} %fusion.14.query_ref.key_ref.value_ref, bf16[1024,1024]{1,0:T(8,128)(2,1)S(1)} %copy-done.9, ...), custom_call_target="tpu_custom_call" | custom-call | tf_op jit(solution)/shard_map/attend_back/pallas_call | solution.py:137
  505.9 4.9 fusion.16
  524.0 9.1 %add_convert_fusion.2 = bf16[1024,1024]{0,1:T(8,128)(2,1)} fusion(f32[1024,1024]{0,1:T(8,128)} %fusion.139, f32[1024]{0:T(1024)S(1)} %copy-done.72, f32[1024]{0:T(1024)S(1)} %add_rsqrt_fusion.1, f32[1024,1024]{0,1:T(8,128)} %copy-done.47, f32[1024]{0:T(1024)S(1)} %broadcast_multiply_fusion.5, f32[1024]{0:T(1024)} %copy-done.73, ...), kind=kOutput, calls=%fused_computation.23 | convolution fusion | flops 3231711232 | bytes 20992000 | tf_op jit(solution)/shard_map/dot_general | solution.py:33
  572.0 4.5 collective-permute-done.78
  582.0 5.0 collective-permute-done.86
  597.0 5.5 collective-permute-done.88
  604.9 4.9 collective-permute-done.92
  610.6 5.6 collective-permute-done.93
  (524 shorter events, 285.7 us)
Async XLA Ops:
  7.2 128.6 %all-gather.3.cloned.1.call-start = ((), (), s32[]{:S(2)}) async-start(), calls=%async_computation | async-start | bytes 4718592 | tf_op jit(solution)/shard_map/all_gather | solution.py:272
  59.6 183.3 %all-gather.5.cloned.1.call-start = ((), (), s32[]{:S(2)}) async-start(), calls=%async_computation.1 | async-start | bytes 8650752 | tf_op jit(solution)/shard_map/all_gather | solution.py:283
  65.2 15.2 %collective-permute-start.28 = (bf16[64,1536]{1,0:T(8,128)(2,1)S(1)}, bf16[64,1536]{1,0:T(8,128)(2,1)S(1)}, u32[]{:S(2)}, u32[]{:S(2)}) collective-permute-start(bf16[64,1536]{1,0:T(8,128)(2,1)S(1)} %collective-permute-done.18.refs_5_), channel_id=1, source_target_pairs={{0,8},{1,9},{2,10},{3,11},{4,12},{5,13},{6,14},{7,15},{8,0},{9,1},... | collective-permute-start | bytes 589832 | tf_op jit(solution)/shard_map/ppermute | solution.py:210
  80.3 56.9 %collective-permute-start.30 = (bf16[64,1536]{1,0:T(8,128)(2,1)S(1)}, bf16[64,1536]{1,0:T(8,128)(2,1)}, u32[]{:S(2)}, u32[]{:S(2)}) collective-permute-start(bf16[64,1536]{1,0:T(8,128)(2,1)S(1)} %collective-permute-done.22.refs_13_), channel_id=1, source_target_pairs={{0,8},{1,9},{2,10},{3,11},{4,12},{5,13},{6,14},{7,15},{8,0},{9,1},... | collective-permute-start | bytes 589832 | tf_op jit(solution)/shard_map/ppermute | solution.py:210
  135.8 78.7 %collective-permute-start.49 = (bf16[512,4096]{1,0:T(8,128)(2,1)}, bf16[512,4096]{1,0:T(8,128)(2,1)}, u32[]{:S(2)}, u32[]{:S(2)}) collective-permute-start(bf16[512,4096]{1,0:T(8,128)(2,1)} %all-gather.3.cloned.1.call-done.refs_0_), channel_id=1, source_target_pairs={{0,8},{1,9},{2,10},{3,11},{4,12},{5,13},{6,14},{7,15},{8,0},{9,1},... | collective-permute-start | bytes 12582920 | tf_op jit(solution)/shard_map/ppermute | solution.py:210
  175.4 23.9 %collective-permute-start.41 = (bf16[64,1024]{1,0:T(8,128)(2,1)}, bf16[64,1024]{1,0:T(8,128)(2,1)}, u32[]{:S(2)}, u32[]{:S(2)}) collective-permute-start(bf16[64,1024]{1,0:T(8,128)(2,1)} %collective-permute-done.37.refs_5_), channel_id=1, source_target_pairs={{0,2},{2,4},{4,6},{6,7},{7,5},{5,3},{3,1},{1,0},{8,9},{10,8},{12,1... | collective-permute-start | bytes 393224 | tf_op jit(solution)/shard_map/ppermute | solution.py:203
  176.7 22.6 %collective-permute-start.42 = (bf16[64,1024]{1,0:T(8,128)(2,1)}, bf16[64,1024]{1,0:T(8,128)(2,1)}, u32[]{:S(2)}, u32[]{:S(2)}) collective-permute-start(bf16[64,1024]{1,0:T(8,128)(2,1)} %collective-permute-done.38.refs_6_), channel_id=1, source_target_pairs={{0,1},{2,0},{4,2},{6,4},{7,6},{5,7},{3,5},{1,3},{8,10},{10,12},{12... | collective-permute-start | bytes 393224 | tf_op jit(solution)/shard_map/ppermute | solution.py:203
  177.9 21.4 %collective-permute-start.43 = (bf16[64,1024]{1,0:T(8,128)(2,1)}, bf16[64,1024]{1,0:T(8,128)(2,1)}, u32[]{:S(2)}, u32[]{:S(2)}) collective-permute-start(bf16[64,1024]{1,0:T(8,128)(2,1)} %collective-permute-done.37.refs_5_), channel_id=1, source_target_pairs={{0,8},{1,9},{2,10},{3,11},{4,12},{5,13},{6,14},{7,15},{8,0},{9,1},... | collective-permute-start | bytes 393224 | tf_op jit(solution)/shard_map/ppermute | solution.py:210
  177.9 21.4 %collective-permute-start.44 = (bf16[64,1024]{1,0:T(8,128)(2,1)}, bf16[64,1024]{1,0:T(8,128)(2,1)}, u32[]{:S(2)}, u32[]{:S(2)}) collective-permute-start(bf16[64,1024]{1,0:T(8,128)(2,1)} %collective-permute-done.38.refs_6_), channel_id=1, source_target_pairs={{0,8},{1,9},{2,10},{3,11},{4,12},{5,13},{6,14},{7,15},{8,0},{9,1},... | collective-permute-start | bytes 393224 | tf_op jit(solution)/shard_map/ppermute | solution.py:210
  286.1 20.1 %collective-permute-start.50 = (bf16[8,256,1024]{2,1,0:T(8,128)(2,1)}, bf16[8,256,1024]{2,1,0:T(8,128)(2,1)}, u32[]{:S(2)}, u32[]{:S(2)}) collective-permute-start(bf16[8,256,1024]{2,1,0:T(8,128)(2,1)} %dynamic-slice_bitcast_fusion.1), channel_id=1, source_target_pairs={{0,8},{1,9},{2,10},{3,11},{4,12},{5,13},{6,14},{7,15},{8,0},{9,1},... | collective-permute-start | bytes 12582920 | tf_op jit(solution)/shard_map/ppermute | solution.py:210
  324.3 37.1 %collective-permute-start.54 = (bf16[8,64,4096]{2,1,0:T(8,128)(2,1)}, bf16[8,64,4096]{2,1,0:T(8,128)(2,1)}, u32[]{:S(2)}, u32[]{:S(2)}) collective-permute-start(bf16[8,64,4096]{2,1,0:T(8,128)(2,1)} %dynamic-slice_bitcast_fusion), channel_id=1, source_target_pairs={{0,8},{1,9},{2,10},{3,11},{4,12},{5,13},{6,14},{7,15},{8,0},{9,1},... | collective-permute-start | bytes 12582920 | tf_op jit(solution)/shard_map/ppermute | solution.py:210
  336.7 24.7 %collective-permute-start.52 = (bf16[256,1024]{1,0:T(8,128)(2,1)}, bf16[256,1024]{1,0:T(8,128)(2,1)}, u32[]{:S(2)}, u32[]{:S(2)}) collective-permute-start(bf16[256,1024]{1,0:T(8,128)(2,1)} %get-tuple-element.267), channel_id=1, source_target_pairs={{0,2},{2,4},{4,6},{6,7},{7,5},{5,3},{3,1},{1,0},{8,9},{10,8},{12,1... | collective-permute-start | bytes 1572872 | tf_op jit(solution)/shard_map/ppermute | solution.py:203
  338.3 23.1 %collective-permute-start.53 = (bf16[256,1024]{1,0:T(8,128)(2,1)}, bf16[256,1024]{1,0:T(8,128)(2,1)}, u32[]{:S(2)}, u32[]{:S(2)}) collective-permute-start(bf16[256,1024]{1,0:T(8,128)(2,1)} %get-tuple-element.266), channel_id=1, source_target_pairs={{0,1},{2,0},{4,2},{6,4},{7,6},{5,7},{3,5},{1,3},{8,10},{10,12},{12... | collective-permute-start | bytes 1572872 | tf_op jit(solution)/shard_map/ppermute | solution.py:203
  370.8 14.9 %collective-permute-start.56 = (bf16[256,1024]{1,0:T(8,128)(2,1)S(1)}, bf16[256,1024]{1,0:T(8,128)(2,1)S(1)}, u32[]{:S(2)}, u32[]{:S(2)}) collective-permute-start(bf16[256,1024]{1,0:T(8,128)(2,1)S(1)} %get-tuple-element.264), channel_id=1, source_target_pairs={{0,1},{2,0},{4,2},{6,4},{7,6},{5,7},{3,5},{1,3},{8,10},{10,12},{12... | collective-permute-start | bytes 1572872 | tf_op jit(solution)/shard_map/ppermute | solution.py:203
  372.6 17.1 %collective-permute-start.57 = (bf16[64,4096]{1,0:T(8,128)(2,1)S(1)}, bf16[64,4096]{1,0:T(8,128)(2,1)S(1)}, u32[]{:S(2)}, u32[]{:S(2)}) collective-permute-start(bf16[64,4096]{1,0:T(8,128)(2,1)S(1)} %fusion.38), channel_id=1, source_target_pairs={{0,2},{2,4},{4,6},{6,7},{7,5},{5,3},{3,1},{1,0},{8,9},{10,8},{12,1... | collective-permute-start | bytes 1572872 | tf_op jit(solution)/shard_map/ppermute | solution.py:203
  392.8 33.3 %collective-permute-start.58 = (bf16[256,1024]{1,0:T(8,128)(2,1)}, bf16[256,1024]{1,0:T(8,128)(2,1)}, u32[]{:S(2)}, u32[]{:S(2)}) collective-permute-start(bf16[256,1024]{1,0:T(8,128)(2,1)} %get-tuple-element.263), channel_id=1, source_target_pairs={{0,2},{2,4},{4,6},{6,7},{7,5},{5,3},{3,1},{1,0},{8,9},{10,8},{12,1... | collective-permute-start | bytes 1572872 | tf_op jit(solution)/shard_map/ppermute | solution.py:203
  393.3 32.7 %collective-permute-start.59 = (bf16[256,1024]{1,0:T(8,128)(2,1)}, bf16[256,1024]{1,0:T(8,128)(2,1)}, u32[]{:S(2)}, u32[]{:S(2)}) collective-permute-start(bf16[256,1024]{1,0:T(8,128)(2,1)} %get-tuple-element.262), channel_id=1, source_target_pairs={{0,1},{2,0},{4,2},{6,4},{7,6},{5,7},{3,5},{1,3},{8,10},{10,12},{12... | collective-permute-start | bytes 1572872 | tf_op jit(solution)/shard_map/ppermute | solution.py:203
  396.0 30.1 %collective-permute-start.62 = (bf16[8,64,1024]{2,1,0:T(8,128)(2,1)}, bf16[8,64,1024]{2,1,0:T(8,128)(2,1)}, u32[]{:S(2)}, u32[]{:S(2)}) collective-permute-start(bf16[8,64,1024]{2,1,0:T(8,128)(2,1)} %dynamic-slice_bitcast_fusion.4), channel_id=1, source_target_pairs={{0,8},{1,9},{2,10},{3,11},{4,12},{5,13},{6,14},{7,15},{8,0},{9,1},... | collective-permute-start | bytes 3145736 | tf_op jit(solution)/shard_map/ppermute | solution.py:210
  398.8 27.2 %collective-permute-start.60 = (bf16[64,4096]{1,0:T(8,128)(2,1)}, bf16[64,4096]{1,0:T(8,128)(2,1)}, u32[]{:S(2)}, u32[]{:S(2)}) collective-permute-start(bf16[64,4096]{1,0:T(8,128)(2,1)} %get-tuple-element.261), channel_id=1, source_target_pairs={{0,2},{2,4},{4,6},{6,7},{7,5},{5,3},{3,1},{1,0},{8,9},{10,8},{12,1... | collective-permute-start | bytes 1572872 | tf_op jit(solution)/shard_map/ppermute | solution.py:203
  399.4 26.7 %collective-permute-start.61 = (bf16[64,4096]{1,0:T(8,128)(2,1)}, bf16[64,4096]{1,0:T(8,128)(2,1)}, u32[]{:S(2)}, u32[]{:S(2)}) collective-permute-start(bf16[64,4096]{1,0:T(8,128)(2,1)} %get-tuple-element.260), channel_id=1, source_target_pairs={{0,1},{2,0},{4,2},{6,4},{7,6},{5,7},{3,5},{1,3},{8,10},{10,12},{12... | collective-permute-start | bytes 1572872 | tf_op jit(solution)/shard_map/ppermute | solution.py:203
  429.2 20.4 %collective-permute-start.63 = (bf16[256,1024]{1,0:T(8,128)(2,1)S(1)}, bf16[256,1024]{1,0:T(8,128)(2,1)S(1)}, u32[]{:S(2)}, u32[]{:S(2)}) collective-permute-start(bf16[256,1024]{1,0:T(8,128)(2,1)S(1)} %fusion.30), channel_id=1, source_target_pairs={{0,16},{1,17},{2,18},{3,19},{4,20},{5,21},{6,22},{7,23},{8,24},{9,... | collective-permute-start | bytes 1572872 | tf_op jit(solution)/shard_map/ppermute | solution.py:210
  433.5 16.1 %collective-permute-start.64 = (bf16[64,4096]{1,0:T(8,128)(2,1)S(1)}, bf16[64,4096]{1,0:T(8,128)(2,1)S(1)}, u32[]{:S(2)}, u32[]{:S(2)}) collective-permute-start(bf16[64,4096]{1,0:T(8,128)(2,1)S(1)} %get-tuple-element.259), channel_id=1, source_target_pairs={{0,2},{2,4},{4,6},{6,7},{7,5},{5,3},{3,1},{1,0},{8,9},{10,8},{12,1... | collective-permute-start | bytes 1572872 | tf_op jit(solution)/shard_map/ppermute | solution.py:203
  434.2 15.4 %collective-permute-start.65 = (bf16[64,4096]{1,0:T(8,128)(2,1)S(1)}, bf16[64,4096]{1,0:T(8,128)(2,1)S(1)}, u32[]{:S(2)}, u32[]{:S(2)}) collective-permute-start(bf16[64,4096]{1,0:T(8,128)(2,1)S(1)} %get-tuple-element.258), channel_id=1, source_target_pairs={{0,1},{2,0},{4,2},{6,4},{7,6},{5,7},{3,5},{1,3},{8,10},{10,12},{12... | collective-permute-start | bytes 1572872 | tf_op jit(solution)/shard_map/ppermute | solution.py:203
  450.7 47.9 %collective-permute-start.67 = (bf16[256,1024]{1,0:T(8,128)(2,1)}, bf16[256,1024]{1,0:T(8,128)(2,1)}, u32[]{:S(2)}, u32[]{:S(2)}) collective-permute-start(bf16[256,1024]{1,0:T(8,128)(2,1)} %add_convert_fusion.5), channel_id=1, source_target_pairs={{0,8},{1,9},{2,10},{3,11},{4,12},{5,13},{6,14},{7,15},{8,0},{9,1},... | collective-permute-start | bytes 1572872 | tf_op jit(solution)/shard_map/ppermute | solution.py:210
  458.2 40.4 %collective-permute-start.72 = (bf16[8,64,1536]{2,1,0:T(8,128)(2,1)}, bf16[8,64,1536]{2,1,0:T(8,128)(2,1)}, u32[]{:S(2)}, u32[]{:S(2)}) collective-permute-start(bf16[8,64,1536]{2,1,0:T(8,128)(2,1)} %dynamic-slice_bitcast_fusion.3), channel_id=1, source_target_pairs={{0,8},{1,9},{2,10},{3,11},{4,12},{5,13},{6,14},{7,15},{8,0},{9,1},... | collective-permute-start | bytes 4718600 | tf_op jit(solution)/shard_map/ppermute | solution.py:210
  462.0 36.6 %collective-permute-start.68 = (bf16[64,4096]{1,0:T(8,128)(2,1)}, bf16[64,4096]{1,0:T(8,128)(2,1)}, u32[]{:S(2)}, u32[]{:S(2)}) collective-permute-start(bf16[64,4096]{1,0:T(8,128)(2,1)} %get-tuple-element.257), channel_id=1, source_target_pairs={{0,2},{2,4},{4,6},{6,7},{7,5},{5,3},{3,1},{1,0},{8,9},{10,8},{12,1... | collective-permute-start | bytes 1572872 | tf_op jit(solution)/shard_map/ppermute | solution.py:203
  462.6 35.9 %collective-permute-start.69 = (bf16[64,4096]{1,0:T(8,128)(2,1)}, bf16[64,4096]{1,0:T(8,128)(2,1)}, u32[]{:S(2)}, u32[]{:S(2)}) collective-permute-start(bf16[64,4096]{1,0:T(8,128)(2,1)} %get-tuple-element.256), channel_id=1, source_target_pairs={{0,1},{2,0},{4,2},{6,4},{7,6},{5,7},{3,5},{1,3},{8,10},{10,12},{12... | collective-permute-start | bytes 1572872 | tf_op jit(solution)/shard_map/ppermute | solution.py:203
  465.8 27.7 %collective-permute-start.70 = (bf16[64,1024]{1,0:T(8,128)(2,1)}, bf16[64,1024]{1,0:T(8,128)(2,1)S(1)}, u32[]{:S(2)}, u32[]{:S(2)}) collective-permute-start(bf16[64,1024]{1,0:T(8,128)(2,1)} %get-tuple-element.287), channel_id=1, source_target_pairs={{0,2},{2,4},{4,6},{6,7},{7,5},{5,3},{3,1},{1,0},{8,9},{10,8},{12,1... | collective-permute-start | bytes 393224 | tf_op jit(solution)/shard_map/ppermute | solution.py:203
  544.3 35.8 %collective-permute-start.85 = (bf16[8,64,1536]{2,1,0:T(8,128)(2,1)}, bf16[8,64,1536]{2,1,0:T(8,128)(2,1)S(1)}, u32[]{:S(2)}, u32[]{:S(2)}) collective-permute-start(bf16[8,64,1536]{2,1,0:T(8,128)(2,1)} %dynamic-slice_bitcast_fusion.2), channel_id=1, source_target_pairs={{0,8},{1,9},{2,10},{3,11},{4,12},{5,13},{6,14},{7,15},{8,0},{9,1},... | collective-permute-start | bytes 4718600 | tf_op jit(solution)/shard_map/ppermute | solution.py:210
  548.4 19.0 %collective-permute-start.77 = (bf16[64,1536]{1,0:T(8,128)(2,1)S(1)}, bf16[64,1536]{1,0:T(8,128)(2,1)S(1)}, u32[]{:S(2)}, u32[]{:S(2)}) collective-permute-start(bf16[64,1536]{1,0:T(8,128)(2,1)S(1)} %get-tuple-element.272), channel_id=1, source_target_pairs={{0,2},{2,4},{4,6},{6,7},{7,5},{5,3},{3,1},{1,0},{8,9},{10,8},{12,1... | collective-permute-start | bytes 589832 | tf_op jit(solution)/shard_map/ppermute | solution.py:203
  549.1 18.3 %collective-permute-start.80 = (bf16[64,1536]{1,0:T(8,128)(2,1)S(1)}, bf16[64,1536]{1,0:T(8,128)(2,1)S(1)}, u32[]{:S(2)}, u32[]{:S(2)}) collective-permute-start(bf16[64,1536]{1,0:T(8,128)(2,1)S(1)} %get-tuple-element.273), channel_id=1, source_target_pairs={{0,1},{2,0},{4,2},{6,4},{7,6},{5,7},{3,5},{1,3},{8,10},{10,12},{12... | collective-permute-start | bytes 589832 | tf_op jit(solution)/shard_map/ppermute | solution.py:203
  557.8 22.2 %collective-permute-start.109 = (bf16[64,4096]{1,0:T(8,128)(2,1)S(1)}, bf16[64,4096]{1,0:T(8,128)(2,1)S(1)}, u32[]{:S(2)}, u32[]{:S(2)}) collective-permute-start(bf16[64,4096]{1,0:T(8,128)(2,1)S(1)} %add_convert_fusion.4), channel_id=1, source_target_pairs={{0,8},{1,9},{2,10},{3,11},{4,12},{5,13},{6,14},{7,15},{8,0},{9,1},... | collective-permute-start | bytes 1572872 | tf_op jit(solution)/shard_map/ppermute | solution.py:210
  (168 other events, 1556.7 us)
Sparse Core Ops, SparseCore 0:
  59.7 76.0 all-gather.2
  139.2 79.1 all-gather.4

commit v3 on v2

--- a/solution.py
+++ b/solution.py
@@ -171,6 +171,32 @@
     )(jnp.stack(places).astype(jnp.int32), *arrays)
 
 
+def pack_kernel(size, rows, *refs):
+    out_ref = refs[-1]
+    out_ref[...] = jnp.zeros_like(out_ref)
+    for shard in range(size):
+        at = 0
+        for ref in refs[:-1]:
+            width = ref.shape[1] // size
+            for start in range(0, width, LANES):
+                count = min(LANES, width - start)
+                line = ref[:, shard * width + start : shard * width + start + count]
+                out_ref[shard * rows + at : shard * rows + at + 1, :count] = line
+                at += 1
+
+
+def pack(vectors, size, rows):
+    if vectors[0].shape[1] // size < LANES:
+        small = jnp.concatenate([vector.reshape(size, -1) for vector in vectors], axis=1)
+        small = jnp.pad(small, ((0, 0), (0, rows * LANES - small.shape[1])))
+        return small.reshape(size * rows, LANES).astype(LOW)
+    return pl.pallas_call(
+        functools.partial(pack_kernel, size, rows),
+        out_shape=jax.ShapeDtypeStruct((size * rows, LANES), FULL),
+        name="pack",
+    )(*vectors).astype(LOW)
+
+
 def tie(*values):
     return lax.optimization_barrier(values)
 
@@ -264,44 +290,16 @@
                 keep(chunk, False, place)
         return assemble(arrays, moves, places, self.size * rows)
 
-    def gather_halves(self, values):
-        if self.direct:
-            return lax.all_gather(values, "shard", axis=0, tiled=True)
-        rows = values.shape[0]
-        half = rows // 2
-        mine = lax.all_gather(self.half_of(values), "shard", axis=0, tiled=True)
-        other = self.swap(mine, 1)
-        moves, places = [], []
-        for shard in range(self.size):
-            moves += [(0, shard * half, half), (1, shard * half, half)]
-            places += [shard * rows + self.core * half, shard * rows + (1 - self.core) * half]
-        return assemble([mine, other], moves, places, self.size * rows)
-
     def gather_quarters(self, values):
         rows = values.shape[0] // self.reps
         mine = lax.dynamic_slice_in_dim(values, lax.axis_index("rep") * rows, rows, axis=0)
         return lax.all_gather(mine, ("shard", "rep"), axis=0, tiled=True)
 
-    def reduce_halves(self, values):
-        if self.direct:
-            own = lax.psum_scatter(values, "shard", scatter_dimension=0, tiled=True)
-            return lax.psum(own, "rep").astype(FULL)
-        width = values.shape[1]
-        half = values.shape[0] // self.size // 2
-        split = values.reshape(self.size, 2, half, width)
-        other = self.swap(lax.dynamic_index_in_dim(split, 1 - self.core, axis=1, keepdims=False), 1)
-        (other,) = yield [other]
-        mine = lax.dynamic_index_in_dim(split, self.core, axis=1, keepdims=False)
-        total = (mine.astype(FULL) + other.astype(FULL)).astype(LOW)
-        total = total.reshape(self.size * half, width)
-        return lax.psum_scatter(total, "shard", scatter_dimension=0, tiled=True)
-
-    def finish(self, total):
-        total = (total.astype(FULL) + self.swap(total, 2).astype(FULL)).astype(LOW)
-        pair = self.swap(total, 1)
-        low = jnp.where(self.core == 0, total, pair)
-        high = jnp.where(self.core == 0, pair, total)
-        return jnp.concatenate([low, high], axis=0).astype(FULL)
+    def scatter_quarters(self, values):
+        return lax.psum_scatter(values, ("shard", "rep"), scatter_dimension=0, tiled=True)
+
+    def join_quarters(self, values):
+        return lax.all_gather(values, "rep", axis=0, tiled=True).astype(FULL)
 
     def reduce(self, values):
         if self.direct:
@@ -400,25 +398,25 @@
     width = D // size
     hidden = b_inner.shape[0]
 
-    vectors = (b_query, b_value, b_out, gain_one, shift_one, b_outer, gain_two, shift_two)
-    packed = jnp.concatenate(vectors + (b_inner,))
-    used = packed.shape[0]
-    room = -(-used // (32 * LANES)) * 32 * LANES
-    packed = jnp.pad(packed, (0, room - used)).reshape(room // LANES, LANES)
-
     own_groups = [
         jnp.concatenate([w[:, g * WIDE : (g + 1) * WIDE] for w in (w_query, w_key, w_value)], axis=1)
         for g in range(GROUPS)
     ]
+    vectors = (b_query, b_value, b_out, gain_one, shift_one, b_outer, gain_two, shift_two)
+    used = len(vectors) * width + hidden
+    room = -(-used // (32 * LANES)) * 32 * LANES
     flow = Flow()
     flow.start("group0", links.gather(own_groups[0]))
-    flow.start("small", links.gather_small(packed))
-    own_groups[1], w_out, w_inner, w_outer = flow.advance(own_groups[1], w_out, w_inner, w_outer)
+    *vectors, b_inner, own_groups[1], w_inner, w_outer = flow.advance(
+        *vectors, b_inner, own_groups[1], w_inner, w_outer
+    )
+    whole_inner = links.gather_quarters(w_inner)
+    whole_outer = links.gather_quarters(w_outer)
+    packed = jnp.pad(jnp.concatenate(vectors + [b_inner]), (0, room - used))
+    flow.start("small", links.gather_small(packed.reshape(room // LANES, LANES)))
+    flow.advance()
     flow.start("group1", links.gather(own_groups[1]))
     flow.advance()
-    w_inner, w_outer = flow.advance(w_inner, w_outer)
-    whole_inner = links.gather_halves(w_inner)
-    whole_outer = links.gather_quarters(w_outer)
     flow.advance()
     whole_groups = [flow.take("group0")]
     whole_small = flow.take("small").reshape(size, room).astype(FULL)
@@ -464,16 +462,14 @@
     d_mid = d_second.astype(LOW)
     grad_outer = gram(active, d_mid).astype(LOW)
     grad_outer, d_mid = tie(grad_outer, d_mid)
-    flow.start("outer", links.reduce(grad_outer))
+    part_outer = links.scatter_quarters(grad_outer)
     grad_b_outer = column_sum(d_mid)
     d_pre = (against(d_mid, whole_outer) * slope.astype(FULL)).astype(LOW)
-    d_pre = flow.advance(d_pre)
     grad_inner = gram(first_low, d_pre).astype(LOW)
-    grad_inner, d_pre = flow.advance(grad_inner, d_pre)
-    flow.start("inner", links.reduce(grad_inner))
+    grad_inner, d_pre = tie(grad_inner, d_pre)
+    part_inner = links.scatter_quarters(grad_inner)
     grad_b_inner = column_sum(d_pre)
     d_first = d_second + against(d_pre, whole_inner)
-    d_first = flow.advance(d_first)
     grad_gain_one = jnp.sum(d_first * unit_one, axis=0)
     grad_shift_one = jnp.sum(d_first, axis=0)
     d_inner = normal_back(d_first * gain_first, unit_one, inverse_one)
@@ -483,39 +479,45 @@
     flow.start("out_back", links.reduce(grad_out))
     grad_b_out = column_sum(d_branch)
     d_attended = against(d_branch, whole_out).astype(LOW)
+    def joined(parts, place):
+        columns = slice(place * WIDE, (place + 1) * WIDE)
+        return jnp.concatenate([part[..., columns] for part in parts], axis=-1)
+
     grad_b_groups = []
-    d_tokens = d_inner
+    d_groups = []
     for g in range(GROUPS):
         d_group = attend_back(projected[g], d_attended, lse[g], g)
-        d_group = flow.advance(d_group)
+        if g == 0:
+            d_group, part_outer = flow.advance(d_group, part_outer)
+            own_outer = links.join_quarters(part_outer)
+        else:
+            d_group = flow.advance(d_group)
+        grad_b_groups.append(column_sum(d_group))
+        if g == GROUPS - 1:
+            grads = (
+                joined(grad_b_groups, 0),
+                joined(grad_b_groups, 2),
+                grad_b_out,
+                grad_gain_one,
+                grad_shift_one,
+                grad_b_outer,
+                grad_gain_two,
+                grad_shift_two,
+                grad_b_inner,
+            )
+            small = pack([grad.reshape(1, -1) for grad in grads], size, room // LANES)
+            small, d_group = tie(small, d_group)
+            flow.start("small_back", links.reduce(small))
         grad_group = gram(tokens, d_group).astype(LOW)
         grad_group, d_group, d_attended = flow.advance(grad_group, d_group, d_attended)
         flow.start(f"back{g}", links.reduce(grad_group))
-        grad_b_groups.append(column_sum(d_group))
-        d_tokens = d_tokens + against(d_group, whole_groups[g])
-    d_tokens = d_tokens.astype(LOW)
-
-    def joined(parts, place):
-        columns = slice(place * WIDE, (place + 1) * WIDE)
-        return jnp.concatenate([part[..., columns] for part in parts], axis=-1)
-
-    grads = (
-        joined(grad_b_groups, 0),
-        joined(grad_b_groups, 2),
-        grad_b_out,
-        grad_gain_one,
-        grad_shift_one,
-        grad_b_outer,
-        grad_gain_two,
-        grad_shift_two,
-    )
-    small = jnp.concatenate(
-        [grad.reshape(size, width) for grad in grads] + [grad_b_inner.reshape(size, hidden)], axis=1
-    )
-    small = jnp.pad(small, ((0, 0), (0, room - used))).astype(LOW)
-    flow.start("small_back", links.reduce(small.reshape(size * (room // LANES), LANES)))
-    own_outer = flow.take("outer")
-    own_inner = flow.take("inner")
+        d_groups.append(d_group)
+    d_groups[0] = flow.advance(d_groups[0])
+    d_tokens = d_inner + against(d_groups[0], whole_groups[0])
+    d_tokens = flow.advance(d_tokens)
+    d_tokens = (d_tokens + against(d_groups[1], whole_groups[1])).astype(LOW)
+    d_tokens, part_inner = flow.advance(d_tokens, part_inner)
+    own_inner = links.join_quarters(part_inner)
     own_out = flow.take("out_back")
     own_small = flow.take("small_back").reshape(room)
     own_groups = [flow.take(f"back{g}") for g in range(GROUPS)]

time: 637 us -> 608 us (0.954)
  other arithmetic: 85.9 us -> 60.9 us
  local copies, waits for them, and re-layouts: 73.9 us -> 59.8 us
  waiting for transfers between devices: 157 us -> 170 us
    reduce_scatter x0 -> x2, waiting for transfers between devices: none -> 106 us  [scatter_quarters(): lax.psum_scatter(values, ('shard', 'rep'), scatter_dimension=0, tiled=True)]
    all_gather x1 -> x2, waiting for transfers between devices: 55.5 us -> 0.01 us  [join_quarters(): return lax.all_gather(values, 'rep', axis=0, tiled=True).astype(FULL)]
    ppermute x70 -> x56, waiting for transfers between devices: 87.7 us -> 42.3 us  [hop(): return lax.ppermute(values, AXES, pairs)]
    all_gather x1 -> x2, waiting for transfers between devices: 0.01 us -> 9.46 us  [gather_quarters(): return lax.all_gather(mine, ('shard', 'rep'), axis=0, tiled=True)]
    ppermute x70 -> x56, starting transfers between devices: 75.3 us -> 66.2 us  [hop(): return lax.ppermute(values, AXES, pairs)]
    dot_general x5, matrix products: 33.8 us -> 41.6 us  [gram(): lax.dot_general(left, right, (((0,), (0,)), ((), ())), preferred_element_...]
    convert_element_type x0 -> x4, other arithmetic: none -> 7.74 us  [the longest x2 5.7 us: join_quarters(): return lax.all_gather(values, 'rep', axis=0, tiled=True).astype(FULL)]
    reduce_sum x2 -> x0, other arithmetic: 7.67 us -> none  [the longest x1 5.11 us: shards(): grad_gain_one = jnp.sum(d_first * unit_one, axis=0)]
  transfers between devices with their start and end apart: 112 -> 95, of which waited for: 31 -> 27; matrix products, arithmetic and copies ran while one was open for 31% -> 32% of each run, Pallas kernels for 12% -> 12%
where the time goes in v3:
time: 608 us; the launch traced here: 598 us
  waiting for transfers between devices  170 us (28%)
  matrix products  140 us (23%)
  starting transfers between devices  80 us (13%)
  Pallas kernels  71.4 us (12%)
  other arithmetic  60.9 us (10%)
  local copies, waits for them, and re-layouts  59.8 us (10%)
  between operations  16 us (3%)
    reduce_scatter x2, waiting for transfers between devices, scatter_quarters(): lax.psum_scatter(values, ('shard', 'rep'), scatter_dimension=0, tiled=True)  106 us
    ppermute x56, starting transfers between devices, hop(): return lax.ppermute(values, AXES, pairs)  66.2 us
    dot_general x5, matrix products, against(): lax.dot_general(left, right, (((1,), (1,)), ((), ())), preferred_element_...  49 us
    dot_general x5, matrix products, project(): return jnp.dot(left, right, preferred_element_type=FULL)  48.9 us
    ppermute x56, waiting for transfers between devices, hop(): return lax.ppermute(values, AXES, pairs)  42.3 us
    dot_general x5, matrix products, gram(): lax.dot_general(left, right, (((0,), (0,)), ((), ())), preferred_element_...  41.6 us
    unnamed x160, local copies, waits for them, and re-layouts  39.4 us
    pallas_call x2, Pallas kernels, attend_back(): pl.pallas_call(attend_back_kernel, grid=(count // SEQ, PAIRS), in_specs=t...  35.7 us
  transfers between devices with their start and end apart: 95, of which 27 were waited for; matrix products, arithmetic and copies ran while one was open for 32% of the time, Pallas kernels for 12%

profile of v3, /device:TPU:0, one launch (start us, length us, event | category | flops | bytes accessed | tf_op | source)
XLA Modules:
  0.0 598.0 jit_solution(10167543831812588295)
XLA Ops:
  12.8 5.1 collective-permute-done.refs_1_
  31.7 4.6 collective-permute-start.15
  78.3 4.8 assemble.4
  83.1 3.6 fusion.13.query_ref.key_ref.value_ref
  90.9 11.3 %attend.2 = (bf16[1024,1024]{1,0:T(8,128)(2,1)S(1)}, f32[8,2,512]{2,1,0:T(2,128)S(1)}) custom-call(bf16[1024,1536]{1,0:T(8,128)(2,1)S(1)} %fusion.13.query_ref.key_ref.value_ref, bf16[1024,1536]{1,0:T(8,128)(2,1)S(1)} %fusion.13.query_ref.key_ref.value_ref, bf16[1024,1536]{1,0:T(8,128)(2,1)S(1)} %fusion.13.query_ref.key_ref.value_ref), custom_call_target="tpu_custom_call" | custom-call | tf_op jit(solution)/shard_map/attend/pallas_call | solution.py:120
  107.7 3.6 assemble.6
  111.4 3.6 fusion.14.query_ref.key_ref.value_ref
  119.6 3.9 copy.62
  123.6 3.9 copy.65
  129.1 11.3 %attend.3 = (bf16[1024,1024]{1,0:T(8,128)(2,1)S(1)}, f32[8,2,512]{2,1,0:T(2,128)S(1)}) custom-call(bf16[1024,1536]{1,0:T(8,128)(2,1)S(1)} %fusion.14.query_ref.key_ref.value_ref, bf16[1024,1536]{1,0:T(8,128)(2,1)S(1)} %fusion.14.query_ref.key_ref.value_ref, ...), custom_call_target="tpu_custom_call", output_to_operand_aliasing={{0}: (3, {})} | custom-call | tf_op jit(solution)/shard_map/attend/pallas_call | solution.py:120
  151.6 4.7 fusion.109
  159.1 20.5 %multiply_convert_fusion.1 = (bf16[1024,4096]{1,0:T(8,128)(2,1)}, f32[1024,4096]{1,0:T(8,128)}) fusion(f32[4096]{0:T(1024)S(1)} %bitcast.376, bf16[1024,4096]{1,0:T(8,128)(2,1)} %all-gather.5.cloned.1.call-done, f32[1024,1024]{0,1:T(8,128)} %get-tuple-element.350, f32[1024]{0:T(1024)S(1)} %copy-done.61, f32[1024]{0:T(1024)S(1)} %get-tuple-element.321, ...), kind=kOutput, calls=%fused_computation.8 | convolution fusion | flops 8620343296 | bytes 37781504 | tf_op jit(solution)/shard_map/dot_general | solution.py:25
  179.6 9.4 %all-gather.7.cloned.1.call-done = bf16[4096,1024]{1,0:T(8,128)(2,1)} async-done(((bf16[128,1024]{1,0:T(8,128)(2,1)}), bf16[4096,1024]{1,0:T(8,128)(2,1)}) %all-gather.7.cloned.1.call-update) | async-done | bytes 8388624 | tf_op jit(solution)/shard_map/all_gather | solution.py:296
  189.1 16.4 %fusion.110 = (f32[1024]{0:T(1024)S(1)}, f32[1024,1024]{0,1:T(8,128)}) fusion(f32[1024]{0:T(1024)S(1)} %copy-done.62, bf16[1024,4096]{1,0:T(8,128)(2,1)} %get-tuple-element.351, bf16[4096,1024]{1,0:T(8,128)(2,1)} %all-gather.7.cloned.1.call-done, f32[1024]{0:T(1024)S(1)} %copy-done.61, f32[1024]{0:T(1024)S(1)} %get-tuple-element.321, ...), kind=kOutput, calls=%fused_computation.254 | convolution fusion | flops 8597273600 | bytes 25190400 | tf_op jit(solution)/shard_map/dot_general | solution.py:25
  208.9 4.0 fusion.11
  217.8 11.3 %convolution_convert_fusion.1 = bf16[4096,1024]{1,0:T(8,128)(2,1)} fusion(bf16[1024,4096]{1,0:T(8,128)(2,1)S(1)} %copy-done.72, bf16[1024,1024]{0,1:T(8,128)(2,1)S(1)} %get-tuple-element.187), kind=kOutput, calls=%fused_computation.11 | convolution fusion | flops 8594128896 | bytes 18874368 | tf_op jit(solution)/shard_map/dot_general | solution.py:29
  229.2 18.5 %multiply_convert_fusion = bf16[1024,4096]{1,0:T(8,128)(2,1)S(1)} fusion(bf16[1024,1024]{0,1:T(8,128)(2,1)} %copy-done.45, bf16[4096,1024]{1,0:T(8,128)(2,1)} %all-gather.7.cloned.1.call-done, f32[1024,4096]{1,0:T(8,128)} %get-tuple-element.352, f32[4096]{0:T(1024)S(1)} %bitcast.377), kind=kOutput, calls=%fused_computation.7 | convolution fusion | flops 8644460544 | bytes 35667968 | tf_op jit(solution)/shard_map/dot_general | solution.py:33
  251.0 13.6 %convolution_convert_fusion = bf16[1024,4096]{1,0:T(8,128)(2,1)} fusion(bf16[1024,4096]{1,0:T(8,128)(2,1)S(1)} %multiply_convert_fusion, f32[1024,1024]{0,1:T(8,128)} %get-tuple-element.350, f32[1024]{0:T(1024)S(1)} %copy-done.61, f32[1024]{0:T(1024)S(1)} %get-tuple-element.321, f32[1024]{0:T(1024)S(1)} %add_rsqrt_fusion.1, ...), kind=kOutput, calls=%fused_computation.10 | convolution fusion | flops 8599371776 | bytes 20987904 | tf_op jit(solution)/shard_map/dot_general | solution.py:29
  264.7 18.9 %multiply_reduce_fusion = (f32[1024]{0:T(1024)}, f32[1024]{0:T(1024)S(1)}, f32[1024]{0:T(1024)S(1)}, f32[1024]{0:T(1024)}, f32[1024,1024]{0,1:T(8,128)S(1)}) fusion(f32[1024,1024]{0,1:T(8,128)} %get-tuple-element.350, f32[1024]{0:T(1024)S(1)} %add_rsqrt_fusion.1, f32[1024]{0:T(1024)S(1)} %broadcast_multiply_fusion.5, f32[1024]{0:T(1024)S(1)} %get-tuple-element.321, ...), kind=kOutput, calls=%fused_computation.28 | convolution fusion | flops 8608804864 | bytes 31506432 | tf_op jit(solution)/shard_map/dot_general | solution.py:33
  295.6 17.8 %attend_back.2 = bf16[1024,1536]{1,0:T(8,128)(2,1)S(1)} custom-call(bf16[1024,1536]{1,0:T(8,128)(2,1)S(1)} %copy-done.3, bf16[1024,1536]{1,0:T(8,128)(2,1)S(1)} %copy-done.3, bf16[1024,1536]{1,0:T(8,128)(2,1)S(1)} %copy-done.3, bf16[1024,1024]{1,0:T(8,128)(2,1)S(1)} %convolution_convert_fusion.4.d_ref, f32[8,2,512]{2,1,0:T(2,128)S(1)} %copy-done.39), custom_call_target="tpu_custom_call" | custom-call | tf_op jit(solution)/shard_map/attend_back/pallas_call | solution.py:137
  315.2 61.2 %reduce-scatter.3.cloned.1.call-done = bf16[128,1024]{1,0:T(8,128)(2,1)} async-done(((bf16[4096,1024]{1,0:T(8,128)(2,1)}), bf16[128,1024]{1,0:T(8,128)(2,1)}) %reduce-scatter.3.cloned.1.call-update) | async-done | bytes 262160 | tf_op jit(solution)/shard_map/reduce_scatter | solution.py:299
  378.2 7.8 %fusion.15 = bf16[1024,1536]{0,1:T(8,128)(2,1)} fusion(bf16[1024,1536]{1,0:T(8,128)(2,1)} %copy-done.4, bf16[1024,1024]{1,0:T(8,128)(2,1)} %param.17), kind=kOutput, calls=%fused_computation.46 | convolution fusion | flops 3222798336 | bytes 8388608 | tf_op jit(solution)/shard_map/dot_general | solution.py:29
  386.0 4.9 copy.67
  394.7 3.9 copy.71
  401.1 5.3 convert_reduce_fusion
  411.0 17.8 %attend_back.3 = bf16[1024,1536]{1,0:T(8,128)(2,1)S(1)} custom-call(bf16[1024,1536]{1,0:T(8,128)(2,1)S(1)} %fusion.14.query_ref.key_ref.value_ref, bf16[1024,1536]{1,0:T(8,128)(2,1)S(1)} %fusion.14.query_ref.key_ref.value_ref, bf16[1024,1536]{1,0:T(8,128)(2,1)S(1)} %fusion.14.query_ref.key_ref.value_ref, bf16[1024,1024]{1,0:T(8,128)(2,1)S(1)} %copy-done.10, ...), custom_call_target="tpu_custom_call" | custom-call | tf_op jit(solution)/shard_map/attend_back/pallas_call | solution.py:137
  443.2 6.5 %fusion.16 = bf16[1024,1536]{0,1:T(8,128)(2,1)} fusion(bf16[1024,1536]{1,0:T(8,128)(2,1)S(1)} %copy-done.8, bf16[1024,1024]{1,0:T(8,128)(2,1)} %param.17), kind=kOutput, calls=%fused_computation.47 | convolution fusion | flops 3222798336 | bytes 8388608 | tf_op jit(solution)/shard_map/dot_general | solution.py:29
  450.3 4.7 copy.68
  484.0 5.8 convolution_add_fusion.1
  503.4 44.7 %reduce-scatter.5.cloned.1.call-done = bf16[32,4096]{1,0:T(8,128)(2,1)} async-done(((bf16[1024,4096]{1,0:T(8,128)(2,1)}), bf16[32,4096]{1,0:T(8,128)(2,1)}) %reduce-scatter.5.cloned.1.call-update) | async-done | bytes 262160 | tf_op jit(solution)/shard_map/reduce_scatter | solution.py:299
  570.5 5.4 collective-permute-done.82
  577.4 6.3 %collective-permute-done.83 = bf16[64,1536]{1,0:T(8,128)(2,1)S(1)} collective-permute-done((bf16[64,1536]{1,0:T(8,128)(2,1)S(1)}, bf16[64,1536]{1,0:T(8,128)(2,1)S(1)}, u32[]{:S(2)}, u32[]{:S(2)}) %collective-permute-start.83) | collective-permute-done | bytes 196640 | tf_op jit(solution)/shard_map/ppermute | solution.py:236
  (437 shorter events, 216.7 us)
Async XLA Ops:
  7.3 151.8 %all-gather.5.cloned.1.call-start = ((), (), s32[]{:S(2)}) async-start(), calls=%async_computation.2 | async-start | bytes 8650752 | tf_op jit(solution)/shard_map/all_gather | solution.py:296
  19.1 169.9 %all-gather.7.cloned.1.call-start = ((), (), s32[]{:S(2)}) async-start(), calls=%async_computation.3 | async-start | bytes 8650752 | tf_op jit(solution)/shard_map/all_gather | solution.py:296
  20.9 355.5 %reduce-scatter.3.cloned.1.call-start = ((), (), s32[]{:S(2)}) async-start(), calls=%async_computation.4 | async-start | bytes 8650752 | tf_op jit(solution)/shard_map/reduce_scatter | solution.py:299
  70.9 15.9 %collective-permute-start.27 = (bf16[64,1536]{1,0:T(8,128)(2,1)S(1)}, bf16[64,1536]{1,0:T(8,128)(2,1)}, u32[]{:S(2)}, u32[]{:S(2)}) collective-permute-start(bf16[64,1536]{1,0:T(8,128)(2,1)S(1)} %collective-permute-done.21.refs_5_), channel_id=1, source_target_pairs={{0,2},{2,4},{4,6},{6,7},{7,5},{5,3},{3,1},{1,0},{8,9},{10,8},{12,1... | collective-permute-start | bytes 589832 | tf_op jit(solution)/shard_map/ppermute | solution.py:229
  72.4 14.8 %collective-permute-start.29 = (bf16[64,1536]{1,0:T(8,128)(2,1)S(1)}, bf16[64,1536]{1,0:T(8,128)(2,1)}, u32[]{:S(2)}, u32[]{:S(2)}) collective-permute-start(bf16[64,1536]{1,0:T(8,128)(2,1)S(1)} %collective-permute-done.21.refs_5_), channel_id=1, source_target_pairs={{0,8},{1,9},{2,10},{3,11},{4,12},{5,13},{6,14},{7,15},{8,0},{9,1},... | collective-permute-start | bytes 589832 | tf_op jit(solution)/shard_map/ppermute | solution.py:236
  72.4 14.7 %collective-permute-start.28 = (bf16[64,1536]{1,0:T(8,128)(2,1)S(1)}, bf16[64,1536]{1,0:T(8,128)(2,1)}, u32[]{:S(2)}, u32[]{:S(2)}) collective-permute-start(bf16[64,1536]{1,0:T(8,128)(2,1)S(1)} %collective-permute-done.22.refs_6_), channel_id=1, source_target_pairs={{0,1},{2,0},{4,2},{6,4},{7,6},{5,7},{3,5},{1,3},{8,10},{10,12},{12... | collective-permute-start | bytes 589832 | tf_op jit(solution)/shard_map/ppermute | solution.py:229
  73.2 14.0 %collective-permute-start.30 = (bf16[64,1536]{1,0:T(8,128)(2,1)S(1)}, bf16[64,1536]{1,0:T(8,128)(2,1)}, u32[]{:S(2)}, u32[]{:S(2)}) collective-permute-start(bf16[64,1536]{1,0:T(8,128)(2,1)S(1)} %collective-permute-done.22.refs_6_), channel_id=1, source_target_pairs={{0,8},{1,9},{2,10},{3,11},{4,12},{5,13},{6,14},{7,15},{8,0},{9,1},... | collective-permute-start | bytes 589832 | tf_op jit(solution)/shard_map/ppermute | solution.py:236
  87.2 15.1 %collective-permute-start.31 = (bf16[64,1536]{1,0:T(8,128)(2,1)}, bf16[64,1536]{1,0:T(8,128)(2,1)S(1)}, u32[]{:S(2)}, u32[]{:S(2)}) collective-permute-start(bf16[64,1536]{1,0:T(8,128)(2,1)} %collective-permute-done.27.refs_9_), channel_id=1, source_target_pairs={{0,2},{2,4},{4,6},{6,7},{7,5},{5,3},{3,1},{1,0},{8,9},{10,8},{12,1... | collective-permute-start | bytes 589832 | tf_op jit(solution)/shard_map/ppermute | solution.py:229
  88.3 14.0 %collective-permute-start.32 = (bf16[64,1536]{1,0:T(8,128)(2,1)}, bf16[64,1536]{1,0:T(8,128)(2,1)S(1)}, u32[]{:S(2)}, u32[]{:S(2)}) collective-permute-start(bf16[64,1536]{1,0:T(8,128)(2,1)} %collective-permute-done.27.refs_9_), channel_id=1, source_target_pairs={{0,8},{1,9},{2,10},{3,11},{4,12},{5,13},{6,14},{7,15},{8,0},{9,1},... | collective-permute-start | bytes 589832 | tf_op jit(solution)/shard_map/ppermute | solution.py:236
  88.3 14.0 %collective-permute-start.33 = (bf16[64,1536]{1,0:T(8,128)(2,1)}, bf16[64,1536]{1,0:T(8,128)(2,1)S(1)}, u32[]{:S(2)}, u32[]{:S(2)}) collective-permute-start(bf16[64,1536]{1,0:T(8,128)(2,1)} %collective-permute-done.28.refs_10_), channel_id=1, source_target_pairs={{0,8},{1,9},{2,10},{3,11},{4,12},{5,13},{6,14},{7,15},{8,0},{9,1},... | collective-permute-start | bytes 589832 | tf_op jit(solution)/shard_map/ppermute | solution.py:236
  116.4 24.0 %collective-permute-start.41 = (bf16[64,1024]{1,0:T(8,128)(2,1)}, bf16[64,1024]{1,0:T(8,128)(2,1)}, u32[]{:S(2)}, u32[]{:S(2)}) collective-permute-start(bf16[64,1024]{1,0:T(8,128)(2,1)} %collective-permute-done.37.refs_5_), channel_id=1, source_target_pairs={{0,2},{2,4},{4,6},{6,7},{7,5},{5,3},{3,1},{1,0},{8,9},{10,8},{12,1... | collective-permute-start | bytes 393224 | tf_op jit(solution)/shard_map/ppermute | solution.py:229
  118.9 21.6 %collective-permute-start.42 = (bf16[64,1024]{1,0:T(8,128)(2,1)}, bf16[64,1024]{1,0:T(8,128)(2,1)}, u32[]{:S(2)}, u32[]{:S(2)}) collective-permute-start(bf16[64,1024]{1,0:T(8,128)(2,1)} %collective-permute-done.38.refs_6_), channel_id=1, source_target_pairs={{0,1},{2,0},{4,2},{6,4},{7,6},{5,7},{3,5},{1,3},{8,10},{10,12},{12... | collective-permute-start | bytes 393224 | tf_op jit(solution)/shard_map/ppermute | solution.py:229
  119.1 21.4 %collective-permute-start.43 = (bf16[64,1024]{1,0:T(8,128)(2,1)}, bf16[64,1024]{1,0:T(8,128)(2,1)}, u32[]{:S(2)}, u32[]{:S(2)}) collective-permute-start(bf16[64,1024]{1,0:T(8,128)(2,1)} %collective-permute-done.37.refs_5_), channel_id=1, source_target_pairs={{0,8},{1,9},{2,10},{3,11},{4,12},{5,13},{6,14},{7,15},{8,0},{9,1},... | collective-permute-start | bytes 393224 | tf_op jit(solution)/shard_map/ppermute | solution.py:236
  119.1 21.3 %collective-permute-start.44 = (bf16[64,1024]{1,0:T(8,128)(2,1)}, bf16[64,1024]{1,0:T(8,128)(2,1)}, u32[]{:S(2)}, u32[]{:S(2)}) collective-permute-start(bf16[64,1024]{1,0:T(8,128)(2,1)} %collective-permute-done.38.refs_6_), channel_id=1, source_target_pairs={{0,8},{1,9},{2,10},{3,11},{4,12},{5,13},{6,14},{7,15},{8,0},{9,1},... | collective-permute-start | bytes 393224 | tf_op jit(solution)/shard_map/ppermute | solution.py:236
  229.1 201.5 %all-gather.11.cloned.1.call-start = ((), (), s32[]{:S(2)}) async-start(), calls=%async_computation.7 | async-start | bytes 1310720 | tf_op jit(solution)/shard_map/all_gather | solution.py:302
  293.0 22.2 %collective-permute-start.49 = (bf16[8,64,1024]{2,1,0:T(8,128)(2,1)S(1)}, bf16[8,64,1024]{2,1,0:T(8,128)(2,1)}, u32[]{:S(2)}, u32[]{:S(2)}) collective-permute-start(bf16[8,64,1024]{2,1,0:T(8,128)(2,1)S(1)} %dynamic-slice_bitcast_fusion.2), channel_id=1, source_target_pairs={{0,8},{1,9},{2,10},{3,11},{4,12},{5,13},{6,14},{7,15},{8,0},{9,1},... | collective-permute-start | bytes 3145736 | tf_op jit(solution)/shard_map/ppermute | solution.py:236
  376.4 171.7 %reduce-scatter.5.cloned.1.call-start = ((), (), s32[]{:S(2)}) async-start(), calls=%async_computation.5 | async-start | bytes 8650752 | tf_op jit(solution)/shard_map/reduce_scatter | solution.py:299
  377.0 210.9 %all-gather.9.cloned.1.call-start = ((), (), s32[]{:S(2)}) async-start(), calls=%async_computation.6 | async-start | bytes 1310720 | tf_op jit(solution)/shard_map/all_gather | solution.py:302
  393.7 39.8 %collective-permute-start.53 = (bf16[8,64,1536]{2,1,0:T(8,128)(2,1)}, bf16[8,64,1536]{2,1,0:T(8,128)(2,1)}, u32[]{:S(2)}, u32[]{:S(2)}) collective-permute-start(bf16[8,64,1536]{2,1,0:T(8,128)(2,1)} %dynamic-slice_bitcast_fusion.1), channel_id=1, source_target_pairs={{0,8},{1,9},{2,10},{3,11},{4,12},{5,13},{6,14},{7,15},{8,0},{9,1},... | collective-permute-start | bytes 4718600 | tf_op jit(solution)/shard_map/ppermute | solution.py:236
  408.9 24.7 %collective-permute-start.51 = (bf16[64,1024]{1,0:T(8,128)(2,1)}, bf16[64,1024]{1,0:T(8,128)(2,1)S(1)}, u32[]{:S(2)}, u32[]{:S(2)}) collective-permute-start(bf16[64,1024]{1,0:T(8,128)(2,1)} %get-tuple-element.298), channel_id=1, source_target_pairs={{0,2},{2,4},{4,6},{6,7},{7,5},{5,3},{3,1},{1,0},{8,9},{10,8},{12,1... | collective-permute-start | bytes 393224 | tf_op jit(solution)/shard_map/ppermute | solution.py:229
  408.9 24.7 %collective-permute-start.52 = (bf16[64,1024]{1,0:T(8,128)(2,1)}, bf16[64,1024]{1,0:T(8,128)(2,1)S(1)}, u32[]{:S(2)}, u32[]{:S(2)}) collective-permute-start(bf16[64,1024]{1,0:T(8,128)(2,1)} %get-tuple-element.297), channel_id=1, source_target_pairs={{0,1},{2,0},{4,2},{6,4},{7,6},{5,7},{3,5},{1,3},{8,10},{10,12},{12... | collective-permute-start | bytes 393224 | tf_op jit(solution)/shard_map/ppermute | solution.py:229
  456.7 15.5 %collective-permute-start.63 = (bf16[8,64,1536]{2,1,0:T(8,128)(2,1)S(1)}, bf16[8,64,1536]{2,1,0:T(8,128)(2,1)S(1)}, u32[]{:S(2)}, u32[]{:S(2)}) collective-permute-start(bf16[8,64,1536]{2,1,0:T(8,128)(2,1)S(1)} %dynamic-slice_bitcast_fusion), channel_id=1, source_target_pairs={{0,8},{1,9},{2,10},{3,11},{4,12},{5,13},{6,14},{7,15},{8,0},{9,1},... | collective-permute-start | bytes 4718600 | tf_op jit(solution)/shard_map/ppermute | solution.py:236
  473.5 16.3 %collective-permute-start.64 = (bf16[64,1024]{1,0:T(8,128)(2,1)S(1)}, bf16[64,1024]{1,0:T(8,128)(2,1)S(1)}, u32[]{:S(2)}, u32[]{:S(2)}) collective-permute-start(bf16[64,1024]{1,0:T(8,128)(2,1)S(1)} %fusion.50), channel_id=1, source_target_pairs={{0,16},{1,17},{2,18},{3,19},{4,20},{5,21},{6,22},{7,23},{8,24},{9,... | collective-permute-start | bytes 393224 | tf_op jit(solution)/shard_map/ppermute | solution.py:236
  474.9 14.8 %collective-permute-start.65 = (bf16[64,1536]{1,0:T(8,128)(2,1)S(1)}, bf16[64,1536]{1,0:T(8,128)(2,1)S(1)}, u32[]{:S(2)}, u32[]{:S(2)}) collective-permute-start(bf16[64,1536]{1,0:T(8,128)(2,1)S(1)} %get-tuple-element.288), channel_id=1, source_target_pairs={{0,2},{2,4},{4,6},{6,7},{7,5},{5,3},{3,1},{1,0},{8,9},{10,8},{12,1... | collective-permute-start | bytes 589832 | tf_op jit(solution)/shard_map/ppermute | solution.py:229
  475.2 14.6 %collective-permute-start.66 = (bf16[64,1536]{1,0:T(8,128)(2,1)S(1)}, bf16[64,1536]{1,0:T(8,128)(2,1)S(1)}, u32[]{:S(2)}, u32[]{:S(2)}) collective-permute-start(bf16[64,1536]{1,0:T(8,128)(2,1)S(1)} %get-tuple-element.287), channel_id=1, source_target_pairs={{0,1},{2,0},{4,2},{6,4},{7,6},{5,7},{3,5},{1,3},{8,10},{10,12},{12... | collective-permute-start | bytes 589832 | tf_op jit(solution)/shard_map/ppermute | solution.py:229
  489.8 58.3 %collective-permute-start.70 = (bf16[64,1024]{1,0:T(8,128)(2,1)S(1)}, bf16[64,1024]{1,0:T(8,128)(2,1)S(1)}, u32[]{:S(2)}, u32[]{:S(2)}) collective-permute-start(bf16[64,1024]{1,0:T(8,128)(2,1)S(1)} %add_convert_fusion.6), channel_id=1, source_target_pairs={{0,8},{1,9},{2,10},{3,11},{4,12},{5,13},{6,14},{7,15},{8,0},{9,1},... | collective-permute-start | bytes 393224 | tf_op jit(solution)/shard_map/ppermute | solution.py:236
  491.3 56.8 %collective-permute-start.71 = (bf16[64,1536]{1,0:T(8,128)(2,1)S(1)}, bf16[64,1536]{1,0:T(8,128)(2,1)S(1)}, u32[]{:S(2)}, u32[]{:S(2)}) collective-permute-start(bf16[64,1536]{1,0:T(8,128)(2,1)S(1)} %get-tuple-element.286), channel_id=1, source_target_pairs={{0,2},{2,4},{4,6},{6,7},{7,5},{5,3},{3,1},{1,0},{8,9},{10,8},{12,1... | collective-permute-start | bytes 589832 | tf_op jit(solution)/shard_map/ppermute | solution.py:229
  492.4 55.7 %collective-permute-start.72 = (bf16[64,1536]{1,0:T(8,128)(2,1)S(1)}, bf16[64,1536]{1,0:T(8,128)(2,1)}, u32[]{:S(2)}, u32[]{:S(2)}) collective-permute-start(bf16[64,1536]{1,0:T(8,128)(2,1)S(1)} %get-tuple-element.285), channel_id=1, source_target_pairs={{0,1},{2,0},{4,2},{6,4},{7,6},{5,7},{3,5},{1,3},{8,10},{10,12},{12... | collective-permute-start | bytes 589832 | tf_op jit(solution)/shard_map/ppermute | solution.py:229
  500.2 47.9 %collective-permute-start.75 = (bf16[64,1536]{1,0:T(8,128)(2,1)}, bf16[64,1536]{1,0:T(8,128)(2,1)S(1)}, u32[]{:S(2)}, u32[]{:S(2)}) collective-permute-start(bf16[64,1536]{1,0:T(8,128)(2,1)} %get-tuple-element.284), channel_id=1, source_target_pairs={{0,2},{2,4},{4,6},{6,7},{7,5},{5,3},{3,1},{1,0},{8,9},{10,8},{12,1... | collective-permute-start | bytes 589832 | tf_op jit(solution)/shard_map/ppermute | solution.py:229
  501.5 46.6 %collective-permute-start.76 = (bf16[64,1536]{1,0:T(8,128)(2,1)}, bf16[64,1536]{1,0:T(8,128)(2,1)S(1)}, u32[]{:S(2)}, u32[]{:S(2)}) collective-permute-start(bf16[64,1536]{1,0:T(8,128)(2,1)} %get-tuple-element.283), channel_id=1, source_target_pairs={{0,1},{2,0},{4,2},{6,4},{7,6},{5,7},{3,5},{1,3},{8,10},{10,12},{12... | collective-permute-start | bytes 589832 | tf_op jit(solution)/shard_map/ppermute | solution.py:229
  552.7 14.2 %collective-permute-start.79 = (bf16[64,1536]{1,0:T(8,128)(2,1)S(1)}, bf16[64,1536]{1,0:T(8,128)(2,1)S(1)}, u32[]{:S(2)}, u32[]{:S(2)}) collective-permute-start(bf16[64,1536]{1,0:T(8,128)(2,1)S(1)} %get-tuple-element.281), channel_id=1, source_target_pairs={{0,2},{2,4},{4,6},{6,7},{7,5},{5,3},{3,1},{1,0},{8,9},{10,8},{12,1... | collective-permute-start | bytes 589832 | tf_op jit(solution)/shard_map/ppermute | solution.py:229
  552.8 14.2 %collective-permute-start.81 = (bf16[64,1536]{1,0:T(8,128)(2,1)S(1)}, bf16[64,1536]{1,0:T(8,128)(2,1)S(1)}, u32[]{:S(2)}, u32[]{:S(2)}) collective-permute-start(bf16[64,1536]{1,0:T(8,128)(2,1)S(1)} %get-tuple-element.282), channel_id=1, source_target_pairs={{0,1},{2,0},{4,2},{6,4},{7,6},{5,7},{3,5},{1,3},{8,10},{10,12},{12... | collective-permute-start | bytes 589832 | tf_op jit(solution)/shard_map/ppermute | solution.py:229
  (136 other events, 1249.4 us)
Sparse Core Ops, SparseCore 0:
  19.3 87.4 all-gather.4
  110.2 78.8 all-gather.6
  229.3 147.1 reduce-scatter.2
  377.8 12.7 all-gather.10
  392.7 155.3 reduce-scatter.4
  559.0 14.4 all-gather.8

commit v4 on v3

--- a/solution.py
+++ b/solution.py
@@ -31,10 +31,6 @@
 
 def against(left, right):
     return lax.dot_general(left, right, (((1,), (1,)), ((), ())), preferred_element_type=FULL)
-
-
-def column_sum(values):
-    return jnp.sum(values.astype(FULL), axis=0)
 
 
 def normal(values):
@@ -73,8 +69,8 @@
     out_ref[...] = jnp.concatenate(parts, axis=0).T.astype(LOW)
 
 
-def attend_back_kernel(query_ref, key_ref, value_ref, d_ref, lse_ref, out_ref):
-    pair = pl.program_id(1)
+def attend_back_kernel(query_ref, key_ref, value_ref, d_ref, lse_ref, out_ref, sum_ref):
+    seq, pair = pl.program_id(0), pl.program_id(1)
     query = query_ref[...] * LOW(0.125)
     key = key_ref[...]
     value = value_ref[...]
@@ -100,6 +96,9 @@
     for place, grad in enumerate((d_query, d_key, d_value)):
         start = pl.multiple_of(place * WIDE + pair * LANES, LANES)
         out_ref[:, pl.ds(start, LANES)] = grad.astype(LOW)
+        total = jnp.sum(grad, axis=0, keepdims=True)
+        before = sum_ref[0:1, pl.ds(start, LANES)]
+        sum_ref[0:1, pl.ds(start, LANES)] = jnp.where(seq == 0, total, before + total)
 
 
 def column_block(first):
@@ -138,11 +137,255 @@
         attend_back_kernel,
         grid=(count // SEQ, PAIRS),
         in_specs=triple() + [column_block(group * PAIRS), LSE_BLOCK],
-        out_specs=pl.BlockSpec((SEQ, 3 * WIDE), lambda seq, pair: (seq, 0)),
-        out_shape=jax.ShapeDtypeStruct((count, 3 * WIDE), LOW),
+        out_specs=[
+            pl.BlockSpec((SEQ, 3 * WIDE), lambda seq, pair: (seq, 0)),
+            pl.BlockSpec((8, 3 * WIDE), lambda seq, pair: (0, 0)),
+        ],
+        out_shape=[
+            jax.ShapeDtypeStruct((count, 3 * WIDE), LOW),
+            jax.ShapeDtypeStruct((8, 3 * WIDE), FULL),
+        ],
         compiler_params=pltpu.CompilerParams(vmem_limit_bytes=40 * 2**20),
         name="attend_back",
     )(qkv, qkv, qkv, d_attended, lse)
+
+
+ROWS = 256
+COLUMNS = 512
+PARTS = 2
+(QUERY, VALUE, OUT, GAIN_ONE, SHIFT_ONE, OUTER, GAIN_TWO, SHIFT_TWO) = range(8)
+
+
+def line(ref, row):
+    return ref[row : row + 1, :]
+
+
+def kept(shape):
+    return pl.BlockSpec(shape, lambda i: (0,) * len(shape), pipeline_mode=pl.Buffered(1))
+
+
+def rows_of(width):
+    return pl.BlockSpec((ROWS, width), lambda i: (i, 0))
+
+
+def columns_of(height):
+    return pl.BlockSpec((height, COLUMNS), lambda i: (0, i))
+
+
+def add_line(ref, row, values):
+    ref[row : row + 1, :] += jnp.sum(values, axis=0, keepdims=True)
+
+
+def clear(ref):
+    @pl.when(pl.program_id(0) == 0)
+    def _():
+        ref[...] = jnp.zeros_like(ref)
+
+
+def pieces(rows):
+    step = rows // PARTS
+    return [slice(i * step, (i + 1) * step) for i in range(PARTS)]
+
+
+LIMIT = pltpu.CompilerParams(vmem_limit_bytes=48 * 2**20)
+
+
+def out_kernel(attended_ref, w_ref, tokens_ref, vec_ref, unit_ref, inverse_ref, low_ref):
+    for rows in pieces(ROWS):
+        branch = project(attended_ref[rows, :], w_ref[...]) + line(vec_ref, OUT)
+        unit, inverse = normal(tokens_ref[rows, :].astype(FULL) + branch)
+        unit_ref[rows, :] = unit
+        inverse_ref[rows, :] = jnp.broadcast_to(inverse, (inverse.shape[0], LANES))
+        low_ref[rows, :] = (unit * line(vec_ref, GAIN_ONE) + line(vec_ref, SHIFT_ONE)).astype(LOW)
+
+
+def out_norm(attended, w_out, tokens, vec):
+    count = tokens.shape[0]
+    return pl.pallas_call(
+        out_kernel,
+        grid=(count // ROWS,),
+        in_specs=[rows_of(D), kept((D, D)), rows_of(D), kept((8, D))],
+        out_specs=[rows_of(D), rows_of(LANES), rows_of(D)],
+        out_shape=[
+            jax.ShapeDtypeStruct((count, D), FULL),
+            jax.ShapeDtypeStruct((count, LANES), FULL),
+            jax.ShapeDtypeStruct((count, D), LOW),
+        ],
+        compiler_params=LIMIT,
+        name="out_norm",
+    )(attended, w_out, tokens, vec)
+
+
+def inner_kernel(low_ref, w_ref, bias_ref, active_ref, slope_ref):
+    for rows in pieces(low_ref.shape[0]):
+        pre = project(low_ref[rows, :], w_ref[...]) + bias_ref[...]
+        below = 0.5 * (1.0 + lax.erf(pre * (0.5**0.5)))
+        active_ref[rows, :] = (pre * below).astype(LOW)
+        slope_ref[rows, :] = (below + pre * jnp.exp(-0.5 * pre * pre) * 0.3989422804014327).astype(LOW)
+
+
+def inner_gelu(low, w_inner, bias):
+    count, hidden = low.shape[0], w_inner.shape[1]
+    return pl.pallas_call(
+        inner_kernel,
+        grid=(hidden // COLUMNS,),
+        in_specs=[kept((count, D)), columns_of(D), columns_of(1)],
+        out_specs=[columns_of(count), columns_of(count)],
+        out_shape=[jax.ShapeDtypeStruct((count, hidden), LOW)] * 2,
+        compiler_params=LIMIT,
+        name="inner_gelu",
+    )(low, w_inner, bias)
+
+
+def outer_kernel(active_ref, w_ref, unit_ref, vec_ref, cot_ref, out_ref, d_ref, d_low_ref, sum_ref):
+    clear(sum_ref)
+    for rows in pieces(ROWS):
+        first = unit_ref[rows, :] * line(vec_ref, GAIN_ONE) + line(vec_ref, SHIFT_ONE)
+        second = first + project(active_ref[rows, :], w_ref[...]) + line(vec_ref, OUTER)
+        unit, inverse = normal(second)
+        out_ref[rows, :] = (unit * line(vec_ref, GAIN_TWO) + line(vec_ref, SHIFT_TWO)).astype(LOW)
+        cot = cot_ref[rows, :].astype(FULL)
+        d_second = normal_back(cot * line(vec_ref, GAIN_TWO), unit, inverse)
+        d_ref[rows, :] = d_second
+        d_low_ref[rows, :] = d_second.astype(LOW)
+        add_line(sum_ref, 0, cot * unit)
+        add_line(sum_ref, 1, cot)
+        add_line(sum_ref, 2, d_second)
+
+
+def outer_norms(active, w_outer, unit, vec, cotangent):
+    count, hidden = active.shape
+    return pl.pallas_call(
+        outer_kernel,
+        grid=(count // ROWS,),
+        in_specs=[rows_of(hidden), kept((hidden, D)), rows_of(D), kept((8, D)), rows_of(D)],
+        out_specs=[rows_of(D), rows_of(D), rows_of(D), kept((8, D))],
+        out_shape=[
+            jax.ShapeDtypeStruct((count, D), LOW),
+            jax.ShapeDtypeStruct((count, D), FULL),
+            jax.ShapeDtypeStruct((count, D), LOW),
+            jax.ShapeDtypeStruct((8, D), FULL),
+        ],
+        compiler_params=LIMIT,
+        name="outer_norms",
+    )(active, w_outer, unit, vec, cotangent)
+
+
+def outer_back_kernel(d_ref, w_ref, slope_ref, out_ref, sum_ref):
+    sum_ref[...] = jnp.zeros_like(sum_ref)
+    for rows in pieces(d_ref.shape[0]):
+        d_pre = against(d_ref[rows, :], w_ref[...]) * slope_ref[rows, :].astype(FULL)
+        out_ref[rows, :] = d_pre.astype(LOW)
+        add_line(sum_ref, 0, d_pre)
+
+
+def outer_back(d_mid, w_outer, slope):
+    count, hidden = slope.shape
+    return pl.pallas_call(
+        outer_back_kernel,
+        grid=(hidden // COLUMNS,),
+        in_specs=[kept((count, D)), pl.BlockSpec((COLUMNS, D), lambda i: (i, 0)), columns_of(count)],
+        out_specs=[columns_of(count), columns_of(1)],
+        out_shape=[
+            jax.ShapeDtypeStruct((count, hidden), LOW),
+            jax.ShapeDtypeStruct((1, hidden), FULL),
+        ],
+        compiler_params=LIMIT,
+        name="outer_back",
+    )(d_mid, w_outer, slope)
+
+
+def inner_back_kernel(
+    d_pre_ref, w_ref, d_ref, unit_ref, inverse_ref, vec_ref, w_out_ref, out_ref, low_ref, attended_ref, sum_ref
+):
+    clear(sum_ref)
+    for rows in pieces(ROWS):
+        d_first = d_ref[rows, :] + against(d_pre_ref[rows, :], w_ref[...])
+        unit = unit_ref[rows, :]
+        d_inner = normal_back(d_first * line(vec_ref, GAIN_ONE), unit, inverse_ref[rows, 0:1])
+        low = d_inner.astype(LOW)
+        out_ref[rows, :] = d_inner
+        low_ref[rows, :] = low
+        attended_ref[rows, :] = against(low, w_out_ref[...]).astype(LOW)
+        add_line(sum_ref, 0, d_first * unit)
+        add_line(sum_ref, 1, d_first)
+        add_line(sum_ref, 2, d_inner)
+
+
+def inner_back(d_pre, w_inner, d_second, unit, inverse, vec, w_out):
+    count, hidden = d_pre.shape
+    return pl.pallas_call(
+        inner_back_kernel,
+        grid=(count // ROWS,),
+        in_specs=[
+            rows_of(hidden),
+            kept((D, hidden)),
+            rows_of(D),
+            rows_of(D),
+            rows_of(LANES),
+            kept((8, D)),
+            kept((D, D)),
+        ],
+        out_specs=[rows_of(D), rows_of(D), rows_of(D), kept((8, D))],
+        out_shape=[
+            jax.ShapeDtypeStruct((count, D), FULL),
+            jax.ShapeDtypeStruct((count, D), LOW),
+            jax.ShapeDtypeStruct((count, D), LOW),
+            jax.ShapeDtypeStruct((8, D), FULL),
+        ],
+        compiler_params=LIMIT,
+        name="inner_back",
+    )(d_pre, w_inner, d_second, unit, inverse, vec, w_out)
+
+
+def tokens_kernel(base_ref, d_ref, w_ref, out_ref):
+    out_ref[...] = (base_ref[...] + against(d_ref[...], w_ref[...])).astype(out_ref.dtype)
+
+
+def tokens_back(base, d_group, w_group, kind):
+    count, wide = d_group.shape
+    return pl.pallas_call(
+        tokens_kernel,
+        grid=(count // ROWS,),
+        in_specs=[rows_of(D), rows_of(wide), kept((D, wide))],
+        out_specs=rows_of(D),
+        out_shape=jax.ShapeDtypeStruct((count, D), kind),
+        compiler_params=LIMIT,
+        name="tokens_back",
+    )(base, d_group, w_group)
+
+
+def turn_kernel(ref, out_ref):
+    out_ref[...] = ref[...].T
+
+
+def turn(values):
+    count, width = values.shape
+    return pl.pallas_call(
+        turn_kernel,
+        grid=(count // ROWS,),
+        in_specs=[rows_of(width)],
+        out_specs=pl.BlockSpec((width, ROWS), lambda i: (0, i)),
+        out_shape=jax.ShapeDtypeStruct((width, count), values.dtype),
+        name="turn",
+    )(values)
+
+
+def product_kernel(left_ref, right_ref, out_ref):
+    out_ref[...] = project(left_ref[...], right_ref[...]).astype(LOW)
+
+
+def product(left, right):
+    height, depth = left.shape
+    return pl.pallas_call(
+        product_kernel,
+        grid=(right.shape[1] // COLUMNS,),
+        in_specs=[kept((height, depth)), columns_of(depth)],
+        out_specs=columns_of(height),
+        out_shape=jax.ShapeDtypeStruct((height, right.shape[1]), LOW),
+        compiler_params=LIMIT,
+        name="product",
+    )(left, right)
 
 
 def assemble_kernel(moves, align, place_ref, *refs):
@@ -171,30 +414,68 @@
     )(jnp.stack(places).astype(jnp.int32), *arrays)
 
 
-def pack_kernel(size, rows, *refs):
+def pack_kernel(size, rows, vectors, *refs):
     out_ref = refs[-1]
     out_ref[...] = jnp.zeros_like(out_ref)
     for shard in range(size):
-        at = 0
-        for ref in refs[:-1]:
-            width = ref.shape[1] // size
-            for start in range(0, width, LANES):
-                count = min(LANES, width - start)
-                line = ref[:, shard * width + start : shard * width + start + count]
-                out_ref[shard * rows + at : shard * rows + at + 1, :count] = line
+        at = shard * rows
+        for spans in vectors:
+            lines = []
+            for which, row, first, length in spans:
+                lines += [(which, row, first + i) for i in range(0, length, LANES)]
+            share = len(lines) // size
+            for which, row, first in lines[shard * share : (shard + 1) * share]:
+                out_ref[at : at + 1, :] = refs[which][row : row + 1, first : first + LANES]
                 at += 1
 
 
-def pack(vectors, size, rows):
-    if vectors[0].shape[1] // size < LANES:
-        small = jnp.concatenate([vector.reshape(size, -1) for vector in vectors], axis=1)
+def pack(arrays, vectors, size, rows):
+    if any(sum(span[3] for span in spans) % (size * LANES) for spans in vectors):
+        whole = [
+            jnp.concatenate([arrays[which][row, first : first + length] for which, row, first, length in spans])
+            for spans in vectors
+        ]
+        small = jnp.concatenate([vector.reshape(size, -1) for vector in whole], axis=1)
         small = jnp.pad(small, ((0, 0), (0, rows * LANES - small.shape[1])))
         return small.reshape(size * rows, LANES).astype(LOW)
     return pl.pallas_call(
-        functools.partial(pack_kernel, size, rows),
+        functools.partial(pack_kernel, size, rows, vectors),
         out_shape=jax.ShapeDtypeStruct((size * rows, LANES), FULL),
         name="pack",
-    )(*vectors).astype(LOW)
+    )(*arrays).astype(LOW)
+
+
+def unpack_kernel(count, place_ref, *refs):
+    vec_ref, bias_ref, group_ref = refs[count:]
+    group_ref[...] = jnp.zeros_like(group_ref)
+    hidden = bias_ref.shape[1] // count
+    for i in range(count):
+        chunk = refs[i][...].astype(FULL)
+        owner = place_ref[i]
+        start = pl.multiple_of(owner * LANES, LANES)
+        for row in range(8):
+            vec_ref[row : row + 1, pl.ds(start, LANES)] = chunk[row : row + 1, :]
+        for row in range(hidden // LANES):
+            first = pl.multiple_of(owner * hidden + row * LANES, LANES)
+            bias_ref[:, pl.ds(first, LANES)] = chunk[8 + row : 9 + row, :]
+        group = owner * LANES // WIDE
+        for place, row in ((0, QUERY), (2, VALUE)):
+            first = pl.multiple_of(group * 2 * WIDE + place * WIDE + start, LANES)
+            group_ref[:, pl.ds(first, LANES)] = chunk[row : row + 1, :]
+
+
+def unpack(chunks, owners, hidden):
+    count = len(chunks)
+    return pl.pallas_call(
+        functools.partial(unpack_kernel, count),
+        in_specs=[pl.BlockSpec(memory_space=pltpu.SMEM)] + [pl.BlockSpec(memory_space=pltpu.VMEM)] * count,
+        out_shape=[
+            jax.ShapeDtypeStruct((8, D), FULL),
+            jax.ShapeDtypeStruct((1, hidden), FULL),
+            jax.ShapeDtypeStruct((1, 3 * D), FULL),
+        ],
+        name="unpack",
+    )(jnp.stack(owners).astype(jnp.int32), *chunks)
 
 
 def tie(*values):
@@ -240,10 +521,16 @@
         return lax.dynamic_slice_in_dim(values, self.core * half, half, axis=0)
 
 
-    def gather_small(self, values):
+    def gather_small(self, values, hidden):
         if self.direct:
-            return lax.all_gather(values, "shard", axis=0, tiled=True)
-        rows = values.shape[0]
+            small = lax.all_gather(values, "shard", axis=0, tiled=True).reshape(self.size, -1).astype(FULL)
+            width, share = D // self.size, hidden // self.size
+            vec = small[:, : 8 * width].reshape(self.size, 8, width).swapaxes(0, 1).reshape(8, D)
+            bias = small[:, 8 * width : 8 * width + share].reshape(1, hidden)
+            none = jnp.zeros((WIDE,), FULL)
+            spans = [slice(g * WIDE, (g + 1) * WIDE) for g in range(GROUPS)]
+            parts = [part for span in spans for part in (vec[QUERY, span], none, vec[VALUE, span])]
+            return vec, bias, jnp.concatenate(parts).reshape(1, 3 * D)
         found = [(values, 0)]
         ahead = back = values
         for step in range(1, self.far + 1):
@@ -253,9 +540,8 @@
                 back = self.hop(back, -1)
                 found.append((back, step))
             ahead, back = yield [ahead, back]
-        moves = [(i, 0, rows) for i in range(len(found))]
-        places = [self.owner(step) * rows for _, step in found]
-        return assemble([chunk for chunk, _ in found], moves, places, self.size * rows)
+        owners = [self.owner(step) for _, step in found]
+        return unpack([chunk for chunk, _ in found], owners, hidden)
 
     def gather(self, values):
         if self.direct:
@@ -295,11 +581,30 @@
         mine = lax.dynamic_slice_in_dim(values, lax.axis_index("rep") * rows, rows, axis=0)
         return lax.all_gather(mine, ("shard", "rep"), axis=0, tiled=True)
 
-    def scatter_quarters(self, values):
-        return lax.psum_scatter(values, ("shard", "rep"), scatter_dimension=0, tiled=True)
-
-    def join_quarters(self, values):
-        return lax.all_gather(values, "rep", axis=0, tiled=True).astype(FULL)
+    def reduce_halves(self, values, rounds):
+        if self.direct:
+            own = lax.psum_scatter(values, "shard", scatter_dimension=0, tiled=True)
+            return lax.psum(own, "rep").astype(FULL)
+        width = values.shape[1]
+        half = values.shape[0] // self.size // 2
+        split = values.reshape(self.size, 2, half, width)
+        other = self.swap(lax.dynamic_index_in_dim(split, 1 - self.core, axis=1, keepdims=False), 1)
+        (other,) = yield [other]
+        mine = lax.dynamic_index_in_dim(split, self.core, axis=1, keepdims=False)
+        total = (mine.astype(FULL) + other.astype(FULL)).astype(LOW).reshape(self.size * half, width)
+        total = lax.psum_scatter(total, "shard", scatter_dimension=0, tiled=True)
+        for _ in range(rounds):
+            yield []
+        (total,) = yield [total]
+        return (yield from self.finish(total))
+
+    def finish(self, total):
+        (cross,) = yield [self.swap(total, 2)]
+        total = (total.astype(FULL) + cross.astype(FULL)).astype(LOW)
+        (pair,) = yield [self.swap(total, 1)]
+        low = jnp.where(self.core == 0, total, pair)
+        high = jnp.where(self.core == 0, pair, total)
+        return jnp.concatenate([low, high], axis=0).astype(FULL)
 
     def reduce(self, values):
         if self.direct:
@@ -331,12 +636,7 @@
                 if step > 0:
                     back = (back.astype(FULL) + piece(-step)).astype(LOW)
         total = (piece(0) + ahead.astype(FULL) + back.astype(FULL)).astype(LOW)
-        (cross,) = yield [self.swap(total, 2)]
-        total = (total.astype(FULL) + cross.astype(FULL)).astype(LOW)
-        (pair,) = yield [self.swap(total, 1)]
-        low = jnp.where(self.core == 0, total, pair)
-        high = jnp.where(self.core == 0, pair, total)
-        return jnp.concatenate([low, high], axis=0).astype(FULL)
+        return (yield from self.finish(total))
 
 
 class Flow:
@@ -413,114 +713,76 @@
     whole_inner = links.gather_quarters(w_inner)
     whole_outer = links.gather_quarters(w_outer)
     packed = jnp.pad(jnp.concatenate(vectors + [b_inner]), (0, room - used))
-    flow.start("small", links.gather_small(packed.reshape(room // LANES, LANES)))
+    flow.start("small", links.gather_small(packed.reshape(room // LANES, LANES), size * hidden))
     flow.advance()
+    tokens_turned, own_groups[1] = tie(turn(tokens), own_groups[1])
     flow.start("group1", links.gather(own_groups[1]))
     flow.advance()
     flow.advance()
     whole_groups = [flow.take("group0")]
-    whole_small = flow.take("small").reshape(size, room).astype(FULL)
-    (bias_query, bias_value, bias_out, gain_first, shift_first, bias_outer, gain_second, shift_second) = (
-        whole_small[:, i * width : (i + 1) * width].reshape(D) for i in range(len(vectors))
-    )
-    bias_inner = whole_small[:, used - hidden : used].reshape(size * hidden)
-
-    no_bias = jnp.zeros((WIDE,), FULL)
+    vec, bias_inner, bias_groups = flow.take("small")
+
     projected = []
     attended, lse = None, []
     for g in range(GROUPS):
-        columns = slice(g * WIDE, (g + 1) * WIDE)
-        bias = jnp.concatenate([bias_query[columns], no_bias, bias_value[columns]])
+        bias = bias_groups[:, g * 3 * WIDE : (g + 1) * 3 * WIDE]
         projected.append((project(tokens, whole_groups[g]) + bias).astype(LOW))
         if g == 0:
             projected[g], w_out = flow.advance(projected[g], w_out)
             flow.start("out", links.gather(w_out))
         else:
             projected[g] = flow.advance(projected[g])
-        attended, kept = attend(projected[g], g, attended)
-        lse.append(kept)
+        attended, logs = attend(projected[g], g, attended)
+        lse.append(logs)
         attended = flow.advance(attended)
         if g == 0:
             whole_groups.append(flow.take("group1"))
     whole_out = flow.take("out")
-    branch = project(attended, whole_out) + bias_out
-    unit_one, inverse_one = normal(tokens.astype(FULL) + branch)
-    first = unit_one * gain_first + shift_first
-    first_low = first.astype(LOW)
-    pre = project(first_low, whole_inner) + bias_inner
-    below = 0.5 * (1.0 + lax.erf(pre * (0.5**0.5)))
-    active = (pre * below).astype(LOW)
-    slope = (below + pre * jnp.exp(-0.5 * pre * pre) * 0.3989422804014327).astype(LOW)
-    second = first + project(active, whole_outer) + bias_outer
-    unit_two, inverse_two = normal(second)
-    output = (unit_two * gain_second + shift_second).astype(LOW)
-
-    cot = cotangent.astype(FULL)
-    grad_gain_two = jnp.sum(cot * unit_two, axis=0)
-    grad_shift_two = jnp.sum(cot, axis=0)
-    d_second = normal_back(cot * gain_second, unit_two, inverse_two)
-    d_mid = d_second.astype(LOW)
-    grad_outer = gram(active, d_mid).astype(LOW)
-    grad_outer, d_mid = tie(grad_outer, d_mid)
-    part_outer = links.scatter_quarters(grad_outer)
-    grad_b_outer = column_sum(d_mid)
-    d_pre = (against(d_mid, whole_outer) * slope.astype(FULL)).astype(LOW)
-    grad_inner = gram(first_low, d_pre).astype(LOW)
-    grad_inner, d_pre = tie(grad_inner, d_pre)
-    part_inner = links.scatter_quarters(grad_inner)
-    grad_b_inner = column_sum(d_pre)
-    d_first = d_second + against(d_pre, whole_inner)
-    grad_gain_one = jnp.sum(d_first * unit_one, axis=0)
-    grad_shift_one = jnp.sum(d_first, axis=0)
-    d_inner = normal_back(d_first * gain_first, unit_one, inverse_one)
-    d_branch = d_inner.astype(LOW)
-    grad_out = gram(attended, d_branch).astype(LOW)
-    grad_out, d_branch = flow.advance(grad_out, d_branch)
+    unit_one, inverse_one, first_low = out_norm(attended, whole_out, tokens, vec)
+    active, slope = inner_gelu(first_low, whole_inner, bias_inner)
+    output, d_second, d_mid, sums_two = outer_norms(active, whole_outer, unit_one, vec, cotangent)
+
+    grad_outer, d_mid = tie(gram(active, d_mid).astype(LOW), d_mid)
+    flow.start("outer_back", links.reduce_halves(grad_outer, 5))
+    d_pre, sum_inner = outer_back(d_mid, whole_outer, slope)
+    d_pre = flow.advance(d_pre)
+    grad_inner, d_pre = flow.advance(gram(first_low, d_pre).astype(LOW), d_pre)
+    flow.start("inner_back", links.reduce(grad_inner))
+    d_inner, d_branch, d_attended, sums_one = inner_back(
+        d_pre, whole_inner, d_second, unit_one, inverse_one, vec, whole_out
+    )
+    d_branch, d_attended = flow.advance(d_branch, d_attended)
+    grad_out, d_attended = tie(gram(attended, d_branch).astype(LOW), d_attended)
     flow.start("out_back", links.reduce(grad_out))
-    grad_b_out = column_sum(d_branch)
-    d_attended = against(d_branch, whole_out).astype(LOW)
+
+    d_groups, sums_group = [], []
+    for g in range(GROUPS):
+        d_group, sums = attend_back(projected[g], d_attended, lse[g], g)
+        d_group, sums = flow.advance(d_group, sums)
+        sums_group.append(sums)
+        if g == GROUPS - 1:
+            arrays = [sums_one, sums_two, sum_inner] + sums_group
+            spans = [[(3 + h, 0, place * WIDE, WIDE) for h in range(GROUPS)] for place in (0, 2)]
+            spans += [[(i, row, 0, D)] for i, row in ((0, 2), (0, 0), (0, 1), (1, 2), (1, 0), (1, 1))]
+            spans += [[(2, 0, 0, size * hidden)]]
+            small, d_group = tie(pack(arrays, spans, size, room // LANES), d_group)
+            flow.start("small_back", links.reduce(small))
+        grad_group, d_group, d_attended = flow.advance(product(tokens_turned, d_group), d_group, d_attended)
+        flow.start(f"back{g}", links.reduce(grad_group))
+        d_groups.append(d_group)
+    d_groups[0] = flow.advance(d_groups[0])
+    d_tokens = flow.advance(tokens_back(d_inner, d_groups[0], whole_groups[0], FULL))
+    d_tokens = flow.advance(tokens_back(d_tokens, d_groups[1], whole_groups[1], LOW))
+    own_inner = flow.take("inner_back")
+    own_outer = flow.take("outer_back")
+    own_out = flow.take("out_back")
+    own_small = flow.take("small_back").reshape(room)
+    own_groups = [flow.take(f"back{g}") for g in range(GROUPS)]
+
     def joined(parts, place):
         columns = slice(place * WIDE, (place + 1) * WIDE)
         return jnp.concatenate([part[..., columns] for part in parts], axis=-1)
 
-    grad_b_groups = []
-    d_groups = []
-    for g in range(GROUPS):
-        d_group = attend_back(projected[g], d_attended, lse[g], g)
-        if g == 0:
-            d_group, part_outer = flow.advance(d_group, part_outer)
-            own_outer = links.join_quarters(part_outer)
-        else:
-            d_group = flow.advance(d_group)
-        grad_b_groups.append(column_sum(d_group))
-        if g == GROUPS - 1:
-            grads = (
-                joined(grad_b_groups, 0),
-                joined(grad_b_groups, 2),
-                grad_b_out,
-                grad_gain_one,
-                grad_shift_one,
-                grad_b_outer,
-                grad_gain_two,
-                grad_shift_two,
-                grad_b_inner,
-            )
-            small = pack([grad.reshape(1, -1) for grad in grads], size, room // LANES)
-            small, d_group = tie(small, d_group)
-            flow.start("small_back", links.reduce(small))
-        grad_group = gram(tokens, d_group).astype(LOW)
-        grad_group, d_group, d_attended = flow.advance(grad_group, d_group, d_attended)
-        flow.start(f"back{g}", links.reduce(grad_group))
-        d_groups.append(d_group)
-    d_groups[0] = flow.advance(d_groups[0])
-    d_tokens = d_inner + against(d_groups[0], whole_groups[0])
-    d_tokens = flow.advance(d_tokens)
-    d_tokens = (d_tokens + against(d_groups[1], whole_groups[1])).astype(LOW)
-    d_tokens, part_inner = flow.advance(d_tokens, part_inner)
-    own_inner = links.join_quarters(part_inner)
-    own_out = flow.take("out_back")
-    own_small = flow.take("small_back").reshape(room)
-    own_groups = [flow.take(f"back{g}") for g in range(GROUPS)]
     (
         own_bias_query,
         own_bias_value,

time: 608 us -> 561 us (0.923)
  Pallas kernels: 71.4 us -> 201 us
  matrix products: 140 us -> 32.4 us
  waiting for transfers between devices: 170 us -> 92.4 us
  starting transfers between devices: 80 us -> 87.2 us
    pallas_call x1 -> x12, Pallas kernels: 1.48 us -> 131 us  [the longest x1 35.4 us: inner_back(): pl.pallas_call(inner_back_kernel, grid=(count // ROWS,), in_specs=[rows_o...]
    reduce_scatter x2 -> x1, waiting for transfers between devices: 106 us -> 0.02 us  [reduce_halves(): total = lax.psum_scatter(total, 'shard', scatter_dimension=0, tiled=True)]
    dot_general x5 -> x0, matrix products: 49 us -> none  [against(): lax.dot_general(left, right, (((1,), (1,)), ((), ())), preferred_element_...]
    dot_general x5 -> x2, matrix products: 48.9 us -> 7.29 us  [project(): return jnp.dot(left, right, preferred_element_type=FULL)]
    ppermute x56 -> x63, waiting for transfers between devices: 42.3 us -> 68.5 us  [hop(): return lax.ppermute(values, AXES, pairs)]
    reduce_sum x8 -> x0, other arithmetic: 19.3 us -> none  [the longest x5 9.8 us: column_sum(): return jnp.sum(values.astype(FULL), axis=0)]
    dot_general x5 -> x3, matrix products: 41.6 us -> 25.2 us  [gram(): lax.dot_general(left, right, (((0,), (0,)), ((), ())), preferred_element_...]
    ppermute x33 -> x39, waiting for transfers between devices: 12 us -> 23.9 us  [swap(): return lax.ppermute(values, AXES, pairs)]
  transfers between devices with their start and end apart: 95 -> 105, of which waited for: 27 -> 25; matrix products, arithmetic and copies ran while one was open for 32% -> 13% of each run, Pallas kernels for 12% -> 33%
where the time goes in v4:
time: 561 us; the launch traced here: 550 us
  Pallas kernels  201 us (36%)
  waiting for transfers between devices  92.4 us (16%)
  starting transfers between devices  87.2 us (16%)
  local copies, waits for them, and re-layouts  65.1 us (12%)
  other arithmetic  56 us (10%)
  matrix products  32.4 us (6%)
  between operations  15.3 us (3%)
    ppermute x63, starting transfers between devices, hop(): return lax.ppermute(values, AXES, pairs)  71.6 us
    ppermute x63, waiting for transfers between devices, hop(): return lax.ppermute(values, AXES, pairs)  68.5 us
    unnamed x186, local copies, waits for them, and re-layouts  48.4 us
    pallas_call x2, Pallas kernels, attend_back(): pl.pallas_call(attend_back_kernel, grid=(count // SEQ, PAIRS), in_specs=t...  36.2 us
    pallas_call x1, Pallas kernels, inner_back(): pl.pallas_call(inner_back_kernel, grid=(count // ROWS,), in_specs=[rows_o...  35.4 us
    dot_general x3, matrix products, gram(): lax.dot_general(left, right, (((0,), (0,)), ((), ())), preferred_element_...  25.2 us
    ppermute x39, waiting for transfers between devices, swap(): return lax.ppermute(values, AXES, pairs)  23.9 us
    pallas_call x2, Pallas kernels, attend(): pl.pallas_call(attend_kernel, grid=(seqs, PAIRS), in_specs=triple() + [pl...  22.6 us
  transfers between devices with their start and end apart: 105, of which 25 were waited for; matrix products, arithmetic and copies ran while one was open for 13% of the time, Pallas kernels for 33%

profile of v4, /device:TPU:0, one launch (start us, length us, event | category | flops | bytes accessed | tf_op | source)
XLA Modules:
  0.0 549.9 jit_solution(8942881608314181453)
XLA Ops:
  12.9 5.1 collective-permute-done.1.refs_2_
  24.4 4.2 turn.1.left_ref
  37.3 4.8 collective-permute-done.3.refs_6_
  51.5 4.2 collective-permute-done.13.refs_4_
  58.6 4.6 collective-permute-done.19.refs_5_
  84.8 5.3 assemble.3.w_ref
  90.1 3.6 fusion.1.query_ref.key_ref.value_ref
  97.8 11.3 %attend.2 = (bf16[1024,1024]{1,0:T(8,128)(2,1)S(1)}, f32[8,2,512]{2,1,0:T(2,128)S(1)}) custom-call(bf16[1024,1536]{1,0:T(8,128)(2,1)S(1)} %fusion.1.query_ref.key_ref.value_ref, bf16[1024,1536]{1,0:T(8,128)(2,1)S(1)} %fusion.1.query_ref.key_ref.value_ref, bf16[1024,1536]{1,0:T(8,128)(2,1)S(1)} %fusion.1.query_ref.key_ref.value_ref), custom_call_target="tpu_custom_call" | custom-call | tf_op jit(solution)/shard_map/attend/pallas_call | solution.py:119
  112.2 3.4 assemble.4.w_ref
  115.7 3.6 fusion.2.query_ref.key_ref.value_ref
  125.1 11.3 %attend.3 = (bf16[1024,1024]{1,0:T(8,128)(2,1)S(1)}, f32[8,2,512]{2,1,0:T(2,128)S(1)}) custom-call(bf16[1024,1536]{1,0:T(8,128)(2,1)S(1)} %fusion.2.query_ref.key_ref.value_ref, bf16[1024,1536]{1,0:T(8,128)(2,1)S(1)} %fusion.2.query_ref.key_ref.value_ref, bf16[1024,1536]{1,0:T(8,128)(2,1)S(1)} %fusion.2.query_ref.key_ref.value_ref, ...), custom_call_target="tpu_custom_call", output_to_operand_aliasing={{0}: (3, {})} | custom-call | tf_op jit(solution)/shard_map/attend/pallas_call | solution.py:119
  139.9 6.1 %collective-permute-done.47.refs_13_ = bf16[64,1024]{1,0:T(8,128)(2,1)} collective-permute-done((bf16[64,1024]{1,0:T(8,128)(2,1)}, bf16[64,1024]{1,0:T(8,128)(2,1)}, u32[]{:S(2)}, u32[]{:S(2)}) %collective-permute-start.47) | collective-permute-done | bytes 131104 | tf_op jit(solution)/shard_map/ppermute | solution.py:510
  160.0 7.9 %out_norm.1 = (f32[1024,1024]{1,0:T(8,128)}, f32[1024,128]{1,0:T(8,128)S(1)}, bf16[1024,1024]{1,0:T(8,128)(2,1)S(1)}) custom-call(bf16[1024,1024]{1,0:T(8,128)(2,1)S(1)} %copy-done.15, bf16[1024,1024]{1,0:T(8,128)(2,1)} %copy-done.6, bf16[1024,1024]{1,0:T(8,128)(2,1)} %tokens_ref.1, f32[8,1024]{1,0:T(8,128)S(1)} %copy-done.27), custom_call_target="tpu_custom_call" | custom-call | tf_op jit(solution)/shard_map/out_norm/pallas_call | solution.py:204
  171.7 18.5 %inner_gelu.1 = (bf16[1024,4096]{1,0:T(8,128)(2,1)}, bf16[1024,4096]{1,0:T(8,128)(2,1)}) custom-call(bf16[1024,1024]{1,0:T(8,128)(2,1)S(1)} %copy-done.21, bf16[1024,4096]{1,0:T(8,128)(2,1)} %all-gather.3.cloned.1.call-done.w_ref, f32[1,4096]{1,0:T(1,128)S(1)} %copy-done.56), custom_call_target="tpu_custom_call" | custom-call | tf_op jit(solution)/shard_map/inner_gelu/pallas_call | solution.py:229
  191.8 18.4 %outer_norms.1 = (bf16[1024,1024]{1,0:T(8,128)(2,1)}, f32[1024,1024]{1,0:T(8,128)}, bf16[1024,1024]{1,0:T(8,128)(2,1)S(1)}, f32[8,1024]{1,0:T(8,128)S(1)}) custom-call(bf16[1024,4096]{1,0:T(8,128)(2,1)} %get-tuple-element.232.active_ref, bf16[4096,1024]{1,0:T(8,128)(2,1)} %all-gather.5.cloned.1.call-done.w_ref, f32[1024,1024]{1,0:T(8,128)} %get-tuple-element.234.unit_ref, ...), custom_call_target="tpu_custom_call" | custom-call | tf_op jit(solution)/shard_map/outer_norms/pallas_call | solution.py:258
  210.2 11.4 %convolution_convert_fusion.1 = bf16[4096,1024]{1,0:T(8,128)(2,1)S(1)} fusion(bf16[1024,4096]{1,0:T(8,128)(2,1)} %get-tuple-element.232.active_ref, bf16[1024,1024]{1,0:T(8,128)(2,1)S(1)} %get-tuple-element.237.d_ref), kind=kOutput, calls=%fused_computation.3 | convolution fusion | flops 8594128896 | bytes 18874368 | tf_op jit(solution)/shard_map/dot_general | solution.py:29
  226.1 15.8 %outer_back.1 = (bf16[1024,4096]{1,0:T(8,128)(2,1)}, f32[1,4096]{1,0:T(1,128)S(1)}) custom-call(bf16[1024,1024]{1,0:T(8,128)(2,1)S(1)} %get-tuple-element.237.d_ref, bf16[4096,1024]{1,0:T(8,128)(2,1)} %all-gather.5.cloned.1.call-done.w_ref, bf16[1024,4096]{1,0:T(8,128)(2,1)} %get-tuple-element.238.slope_ref), custom_call_target="tpu_custom_call" | custom-call | tf_op jit(solution)/shard_map/outer_back/pallas_call | solution.py:284
  243.9 11.4 %convolution_convert_fusion = bf16[1024,4096]{1,0:T(8,128)(2,1)S(1)} fusion(bf16[1024,1024]{1,0:T(8,128)(2,1)S(1)} %copy-done.22, bf16[1024,4096]{1,0:T(8,128)(2,1)} %get-tuple-element.242.d_pre_ref), kind=kOutput, calls=%fused_computation.2 | convolution fusion | flops 8594128896 | bytes 18874368 | tf_op jit(solution)/shard_map/dot_general | solution.py:29
  261.3 7.7 %fusion = bf16[8,256,1024]{2,1,0:T(8,128)(2,1)} fusion(bf16[8,256,1024]{2,1,0:T(8,128)(2,1)} %copy-done.61, bf16[8,2,256,1024]{3,2,1,0:T(8,128)(2,1)} %bitcast.365, s32[]{:T(128)S(6)} %select_n.592), kind=kLoop, calls=%fused_computation.1 | loop fusion | flops 8388608 | bytes 12582916 | tf_op jit(solution)/shard_map/convert_element_type | solution.py:594
  270.0 35.4 %inner_back.1 = (f32[1024,1024]{1,0:T(8,128)}, bf16[1024,1024]{1,0:T(8,128)(2,1)S(1)}, bf16[1024,1024]{1,0:T(8,128)(2,1)S(1)}, f32[8,1024]{1,0:T(8,128)S(1)}) custom-call(bf16[1024,4096]{1,0:T(8,128)(2,1)} %get-tuple-element.242.d_pre_ref, bf16[1024,4096]{1,0:T(8,128)(2,1)} %all-gather.3.cloned.1.call-done.w_ref, f32[1024,1024]{1,0:T(8,128)} %get-tuple-element.243.d_ref, ...), custom_call_target="tpu_custom_call" | custom-call | tf_op jit(solution)/shard_map/inner_back/pallas_call | solution.py:317
  317.3 18.0 %attend_back.2 = (bf16[1024,1536]{1,0:T(8,128)(2,1)S(1)}, f32[8,1536]{1,0:T(8,128)S(1)}) custom-call(bf16[1024,1536]{1,0:T(8,128)(2,1)S(1)} %copy-done.3, bf16[1024,1536]{1,0:T(8,128)(2,1)S(1)} %copy-done.3, bf16[1024,1536]{1,0:T(8,128)(2,1)S(1)} %copy-done.3, bf16[1024,1024]{1,0:T(8,128)(2,1)S(1)} %copy-done.18, f32[8,2,512]{2,1,0:T(2,128)S(1)} %get-tuple-element.253.lse_ref), custom_call_target="tpu_custom_call" | custom-call | tf_op jit(solution)/shard_map/attend_back/pallas_call | solution.py:136
  344.9 6.4 %product.2 = bf16[1024,1536]{1,0:T(8,128)(2,1)} custom-call(bf16[1024,1024]{1,0:T(8,128)(2,1)S(1)} %copy-done.4, bf16[1024,1536]{1,0:T(8,128)(2,1)} %copy-done.8), custom_call_target="tpu_custom_call" | custom-call | tf_op jit(solution)/shard_map/product/pallas_call | solution.py:380
  351.3 16.7 %collective-permute-done.55 = bf16[64,1024]{1,0:T(8,128)(2,1)S(1)} collective-permute-done((bf16[64,1024]{1,0:T(8,128)(2,1)S(1)}, bf16[64,1024]{1,0:T(8,128)(2,1)S(1)}, u32[]{:S(2)}, u32[]{:S(2)}) %collective-permute-start.55) | collective-permute-done | bytes 131104 | tf_op jit(solution)/shard_map/ppermute | solution.py:510
  383.5 18.2 %attend_back.3 = (bf16[1024,1536]{1,0:T(8,128)(2,1)S(1)}, f32[8,1536]{1,0:T(8,128)S(1)}) custom-call(bf16[1024,1536]{1,0:T(8,128)(2,1)S(1)} %fusion.2.query_ref.key_ref.value_ref, bf16[1024,1536]{1,0:T(8,128)(2,1)S(1)} %fusion.2.query_ref.key_ref.value_ref, bf16[1024,1536]{1,0:T(8,128)(2,1)S(1)} %fusion.2.query_ref.key_ref.value_ref, ...), custom_call_target="tpu_custom_call" | custom-call | tf_op jit(solution)/shard_map/attend_back/pallas_call | solution.py:136
  420.1 5.2 product.3
  444.7 5.6 %collective-permute-done.72 = bf16[64,1536]{1,0:T(8,128)(2,1)S(1)} collective-permute-done((bf16[64,1536]{1,0:T(8,128)(2,1)S(1)}, bf16[64,1536]{1,0:T(8,128)(2,1)S(1)}, u32[]{:S(2)}, u32[]{:S(2)}) %collective-permute-start.72) | collective-permute-done | bytes 196640 | tf_op jit(solution)/shard_map/ppermute | solution.py:510
  450.3 3.6 collective-permute-done.68
  453.9 10.8 %collective-permute-done.67 = bf16[256,1024]{1,0:T(8,128)(2,1)S(1)} collective-permute-done((bf16[256,1024]{1,0:T(8,128)(2,1)S(1)}, bf16[256,1024]{1,0:T(8,128)(2,1)S(1)}, u32[]{:S(2)}, u32[]{:S(2)}) %collective-permute-start.67) | collective-permute-done | bytes 524320 | tf_op jit(solution)/shard_map/ppermute | solution.py:517
  480.7 8.0 %tokens_back.2.base_ref = f32[1024,1024]{1,0:T(8,128)} custom-call(f32[1024,1024]{1,0:T(8,128)} %get-tuple-element.245.base_ref, bf16[1024,1536]{1,0:T(8,128)(2,1)S(1)} %copy-done.9, bf16[1024,1536]{1,0:T(8,128)(2,1)} %copy-done.7), custom_call_target="tpu_custom_call" | custom-call | tf_op jit(solution)/shard_map/tokens_back/pallas_call | solution.py:347
  502.1 7.6 %tokens_back.3 = bf16[1024,1024]{1,0:T(8,128)(2,1)} custom-call(f32[1024,1024]{1,0:T(8,128)} %tokens_back.2.base_ref, bf16[1024,1536]{1,0:T(8,128)(2,1)S(1)} %copy-done.13, bf16[1024,1536]{1,0:T(8,128)(2,1)} %copy-done.10), custom_call_target="tpu_custom_call" | custom-call | tf_op jit(solution)/shard_map/tokens_back/pallas_call | solution.py:347
  526.1 5.1 collective-permute-done.93
  532.8 6.0 %collective-permute-done.96 = bf16[64,1536]{1,0:T(8,128)(2,1)S(1)} collective-permute-done((bf16[64,1536]{1,0:T(8,128)(2,1)S(1)}, bf16[64,1536]{1,0:T(8,128)(2,1)S(1)}, u32[]{:S(2)}, u32[]{:S(2)}) %collective-permute-start.96) | collective-permute-done | bytes 196640 | tf_op jit(solution)/shard_map/ppermute | solution.py:517
  (463 shorter events, 229.3 us)
Async XLA Ops:
  7.3 162.7 %all-gather.3.cloned.1.call-start = ((), (), s32[]{:S(2)}) async-start(), calls=%async_computation.1 | async-start | bytes 8650752 | tf_op jit(solution)/shard_map/all_gather | solution.py:582
  19.2 171.0 %all-gather.5.cloned.1.call-start = ((), (), s32[]{:S(2)}) async-start(), calls=%async_computation.2 | async-start | bytes 8650752 | tf_op jit(solution)/shard_map/all_gather | solution.py:582
  20.9 409.3 %reduce-scatter.2.cloned.1.call-start = ((), (), s32[]{:S(2)}) async-start(), calls=%async_computation.3 | async-start | bytes 4718592 | tf_op jit(solution)/shard_map/reduce_scatter | solution.py:595
  76.0 17.7 %collective-permute-start.29 = (bf16[64,1536]{1,0:T(8,128)(2,1)S(1)}, bf16[64,1536]{1,0:T(8,128)(2,1)}, u32[]{:S(2)}, u32[]{:S(2)}) collective-permute-start(bf16[64,1536]{1,0:T(8,128)(2,1)S(1)} %collective-permute-done.21.refs_5_), channel_id=1, source_target_pairs={{0,8},{1,9},{2,10},{3,11},{4,12},{5,13},{6,14},{7,15},{8,0},{9,1},... | collective-permute-start | bytes 589832 | tf_op jit(solution)/shard_map/ppermute | solution.py:517
  76.1 17.7 %collective-permute-start.27 = (bf16[64,1536]{1,0:T(8,128)(2,1)S(1)}, bf16[64,1536]{1,0:T(8,128)(2,1)}, u32[]{:S(2)}, u32[]{:S(2)}) collective-permute-start(bf16[64,1536]{1,0:T(8,128)(2,1)S(1)} %collective-permute-done.21.refs_5_), channel_id=1, source_target_pairs={{0,2},{2,4},{4,6},{6,7},{7,5},{5,3},{3,1},{1,0},{8,9},{10,8},{12,1... | collective-permute-start | bytes 589832 | tf_op jit(solution)/shard_map/ppermute | solution.py:510
  78.1 15.7 %collective-permute-start.30 = (bf16[64,1536]{1,0:T(8,128)(2,1)}, bf16[64,1536]{1,0:T(8,128)(2,1)}, u32[]{:S(2)}, u32[]{:S(2)}) collective-permute-start(bf16[64,1536]{1,0:T(8,128)(2,1)} %collective-permute-done.22.refs_6_), channel_id=1, source_target_pairs={{0,8},{1,9},{2,10},{3,11},{4,12},{5,13},{6,14},{7,15},{8,0},{9,1},... | collective-permute-start | bytes 589832 | tf_op jit(solution)/shard_map/ppermute | solution.py:517
  78.1 16.5 %collective-permute-start.28 = (bf16[64,1536]{1,0:T(8,128)(2,1)}, bf16[64,1536]{1,0:T(8,128)(2,1)}, u32[]{:S(2)}, u32[]{:S(2)}) collective-permute-start(bf16[64,1536]{1,0:T(8,128)(2,1)} %collective-permute-done.22.refs_6_), channel_id=1, source_target_pairs={{0,1},{2,0},{4,2},{6,4},{7,6},{5,7},{3,5},{1,3},{8,10},{10,12},{12... | collective-permute-start | bytes 589832 | tf_op jit(solution)/shard_map/ppermute | solution.py:510
  120.8 17.0 %collective-permute-start.43 = (bf16[64,1024]{1,0:T(8,128)(2,1)S(1)}, bf16[64,1024]{1,0:T(8,128)(2,1)S(1)}, u32[]{:S(2)}, u32[]{:S(2)}) collective-permute-start(bf16[64,1024]{1,0:T(8,128)(2,1)S(1)} %collective-permute-done.37.refs_5_), channel_id=1, source_target_pairs={{0,8},{1,9},{2,10},{3,11},{4,12},{5,13},{6,14},{7,15},{8,0},{9,1},... | collective-permute-start | bytes 393224 | tf_op jit(solution)/shard_map/ppermute | solution.py:517
  123.2 15.9 %collective-permute-start.42 = (bf16[64,1024]{1,0:T(8,128)(2,1)S(1)}, bf16[64,1024]{1,0:T(8,128)(2,1)}, u32[]{:S(2)}, u32[]{:S(2)}) collective-permute-start(bf16[64,1024]{1,0:T(8,128)(2,1)S(1)} %collective-permute-done.38.refs_6_), channel_id=1, source_target_pairs={{0,1},{2,0},{4,2},{6,4},{7,6},{5,7},{3,5},{1,3},{8,10},{10,12},{12... | collective-permute-start | bytes 393224 | tf_op jit(solution)/shard_map/ppermute | solution.py:510
  224.3 17.6 %collective-permute-start.49 = (bf16[8,256,1024]{2,1,0:T(8,128)(2,1)}, bf16[8,256,1024]{2,1,0:T(8,128)(2,1)S(1)}, u32[]{:S(2)}, u32[]{:S(2)}) collective-permute-start(bf16[8,256,1024]{2,1,0:T(8,128)(2,1)} %dynamic-slice_bitcast_fusion.1), channel_id=1, source_target_pairs={{0,8},{1,9},{2,10},{3,11},{4,12},{5,13},{6,14},{7,15},{8,0},{9,1},... | collective-permute-start | bytes 12582920 | tf_op jit(solution)/shard_map/ppermute | solution.py:517
  261.0 44.5 %collective-permute-start.50 = (bf16[8,64,4096]{2,1,0:T(8,128)(2,1)}, bf16[8,64,4096]{2,1,0:T(8,128)(2,1)}, u32[]{:S(2)}, u32[]{:S(2)}) collective-permute-start(bf16[8,64,4096]{2,1,0:T(8,128)(2,1)} %dynamic-slice_bitcast_fusion), channel_id=1, source_target_pairs={{0,8},{1,9},{2,10},{3,11},{4,12},{5,13},{6,14},{7,15},{8,0},{9,1},... | collective-permute-start | bytes 12582920 | tf_op jit(solution)/shard_map/ppermute | solution.py:517
  310.2 27.4 %collective-permute-start.52 = (bf16[8,64,1024]{2,1,0:T(8,128)(2,1)}, bf16[8,64,1024]{2,1,0:T(8,128)(2,1)}, u32[]{:S(2)}, u32[]{:S(2)}) collective-permute-start(bf16[8,64,1024]{2,1,0:T(8,128)(2,1)} %dynamic-slice_bitcast_fusion.4), channel_id=1, source_target_pairs={{0,8},{1,9},{2,10},{3,11},{4,12},{5,13},{6,14},{7,15},{8,0},{9,1},... | collective-permute-start | bytes 3145736 | tf_op jit(solution)/shard_map/ppermute | solution.py:517
  312.6 25.1 %collective-permute-start.51 = (bf16[64,4096]{1,0:T(8,128)(2,1)}, bf16[64,4096]{1,0:T(8,128)(2,1)}, u32[]{:S(2)}, u32[]{:S(2)}) collective-permute-start(bf16[64,4096]{1,0:T(8,128)(2,1)} %fusion.17), channel_id=1, source_target_pairs={{0,2},{2,4},{4,6},{6,7},{7,5},{5,3},{3,1},{1,0},{8,9},{10,8},{12,1... | collective-permute-start | bytes 1572872 | tf_op jit(solution)/shard_map/ppermute | solution.py:510
  340.1 28.8 %collective-permute-start.54 = (bf16[64,4096]{1,0:T(8,128)(2,1)S(1)}, bf16[64,4096]{1,0:T(8,128)(2,1)}, u32[]{:S(2)}, u32[]{:S(2)}) collective-permute-start(bf16[64,4096]{1,0:T(8,128)(2,1)S(1)} %get-tuple-element.325), channel_id=1, source_target_pairs={{0,1},{2,0},{4,2},{6,4},{7,6},{5,7},{3,5},{1,3},{8,10},{10,12},{12... | collective-permute-start | bytes 1572872 | tf_op jit(solution)/shard_map/ppermute | solution.py:510
  340.7 28.3 %collective-permute-start.53 = (bf16[64,4096]{1,0:T(8,128)(2,1)S(1)}, bf16[64,4096]{1,0:T(8,128)(2,1)}, u32[]{:S(2)}, u32[]{:S(2)}) collective-permute-start(bf16[64,4096]{1,0:T(8,128)(2,1)S(1)} %get-tuple-element.326), channel_id=1, source_target_pairs={{0,2},{2,4},{4,6},{6,7},{7,5},{5,3},{3,1},{1,0},{8,9},{10,8},{12,1... | collective-permute-start | bytes 1572872 | tf_op jit(solution)/shard_map/ppermute | solution.py:510
  343.2 24.8 %collective-permute-start.55 = (bf16[64,1024]{1,0:T(8,128)(2,1)S(1)}, bf16[64,1024]{1,0:T(8,128)(2,1)S(1)}, u32[]{:S(2)}, u32[]{:S(2)}) collective-permute-start(bf16[64,1024]{1,0:T(8,128)(2,1)S(1)} %fusion.62), channel_id=1, source_target_pairs={{0,2},{2,4},{4,6},{6,7},{7,5},{5,3},{3,1},{1,0},{8,9},{10,8},{12,1... | collective-permute-start | bytes 393224 | tf_op jit(solution)/shard_map/ppermute | solution.py:510
  371.6 32.3 %collective-permute-start.60 = (bf16[8,64,1536]{2,1,0:T(8,128)(2,1)}, bf16[8,64,1536]{2,1,0:T(8,128)(2,1)}, u32[]{:S(2)}, u32[]{:S(2)}) collective-permute-start(bf16[8,64,1536]{2,1,0:T(8,128)(2,1)} %dynamic-slice_bitcast_fusion.3), channel_id=1, source_target_pairs={{0,8},{1,9},{2,10},{3,11},{4,12},{5,13},{6,14},{7,15},{8,0},{9,1},... | collective-permute-start | bytes 4718600 | tf_op jit(solution)/shard_map/ppermute | solution.py:517
  376.0 28.0 %collective-permute-start.57 = (bf16[64,4096]{1,0:T(8,128)(2,1)}, bf16[64,4096]{1,0:T(8,128)(2,1)}, u32[]{:S(2)}, u32[]{:S(2)}) collective-permute-start(bf16[64,4096]{1,0:T(8,128)(2,1)} %get-tuple-element.323), channel_id=1, source_target_pairs={{0,1},{2,0},{4,2},{6,4},{7,6},{5,7},{3,5},{1,3},{8,10},{10,12},{12... | collective-permute-start | bytes 1572872 | tf_op jit(solution)/shard_map/ppermute | solution.py:510
  377.6 26.3 %collective-permute-start.56 = (bf16[64,4096]{1,0:T(8,128)(2,1)}, bf16[64,4096]{1,0:T(8,128)(2,1)}, u32[]{:S(2)}, u32[]{:S(2)}) collective-permute-start(bf16[64,4096]{1,0:T(8,128)(2,1)} %get-tuple-element.324), channel_id=1, source_target_pairs={{0,2},{2,4},{4,6},{6,7},{7,5},{5,3},{3,1},{1,0},{8,9},{10,8},{12,1... | collective-permute-start | bytes 1572872 | tf_op jit(solution)/shard_map/ppermute | solution.py:510
  379.9 24.1 %collective-permute-start.59 = (bf16[64,1024]{1,0:T(8,128)(2,1)}, bf16[64,1024]{1,0:T(8,128)(2,1)S(1)}, u32[]{:S(2)}, u32[]{:S(2)}) collective-permute-start(bf16[64,1024]{1,0:T(8,128)(2,1)} %get-tuple-element.343), channel_id=1, source_target_pairs={{0,1},{2,0},{4,2},{6,4},{7,6},{5,7},{3,5},{1,3},{8,10},{10,12},{12... | collective-permute-start | bytes 393224 | tf_op jit(solution)/shard_map/ppermute | solution.py:510
  381.5 22.4 %collective-permute-start.58 = (bf16[64,1024]{1,0:T(8,128)(2,1)}, bf16[64,1024]{1,0:T(8,128)(2,1)S(1)}, u32[]{:S(2)}, u32[]{:S(2)}) collective-permute-start(bf16[64,1024]{1,0:T(8,128)(2,1)} %get-tuple-element.344), channel_id=1, source_target_pairs={{0,2},{2,4},{4,6},{6,7},{7,5},{5,3},{3,1},{1,0},{8,9},{10,8},{12,1... | collective-permute-start | bytes 393224 | tf_op jit(solution)/shard_map/ppermute | solution.py:510
  410.6 19.6 %collective-permute-start.62 = (bf16[64,4096]{1,0:T(8,128)(2,1)}, bf16[64,4096]{1,0:T(8,128)(2,1)S(1)}, u32[]{:S(2)}, u32[]{:S(2)}) collective-permute-start(bf16[64,4096]{1,0:T(8,128)(2,1)} %get-tuple-element.321), channel_id=1, source_target_pairs={{0,1},{2,0},{4,2},{6,4},{7,6},{5,7},{3,5},{1,3},{8,10},{10,12},{12... | collective-permute-start | bytes 1572872 | tf_op jit(solution)/shard_map/ppermute | solution.py:510
  412.3 17.9 %collective-permute-start.61 = (bf16[64,4096]{1,0:T(8,128)(2,1)}, bf16[64,4096]{1,0:T(8,128)(2,1)S(1)}, u32[]{:S(2)}, u32[]{:S(2)}) collective-permute-start(bf16[64,4096]{1,0:T(8,128)(2,1)} %get-tuple-element.322), channel_id=1, source_target_pairs={{0,2},{2,4},{4,6},{6,7},{7,5},{5,3},{3,1},{1,0},{8,9},{10,8},{12,1... | collective-permute-start | bytes 1572872 | tf_op jit(solution)/shard_map/ppermute | solution.py:510
  413.7 16.4 %collective-permute-start.65 = (bf16[64,1536]{1,0:T(8,128)(2,1)S(1)}, bf16[64,1536]{1,0:T(8,128)(2,1)}, u32[]{:S(2)}, u32[]{:S(2)}) collective-permute-start(bf16[64,1536]{1,0:T(8,128)(2,1)S(1)} %fusion.47), channel_id=1, source_target_pairs={{0,2},{2,4},{4,6},{6,7},{7,5},{5,3},{3,1},{1,0},{8,9},{10,8},{12,1... | collective-permute-start | bytes 589832 | tf_op jit(solution)/shard_map/ppermute | solution.py:510
  437.5 27.2 %collective-permute-start.74 = (bf16[8,64,1536]{2,1,0:T(8,128)(2,1)S(1)}, bf16[8,64,1536]{2,1,0:T(8,128)(2,1)S(1)}, u32[]{:S(2)}, u32[]{:S(2)}) collective-permute-start(bf16[8,64,1536]{2,1,0:T(8,128)(2,1)S(1)} %dynamic-slice_bitcast_fusion.2), channel_id=1, source_target_pairs={{0,8},{1,9},{2,10},{3,11},{4,12},{5,13},{6,14},{7,15},{8,0},{9,1},... | collective-permute-start | bytes 4718600 | tf_op jit(solution)/shard_map/ppermute | solution.py:517
  440.8 23.9 %collective-permute-start.67 = (bf16[256,1024]{1,0:T(8,128)(2,1)S(1)}, bf16[256,1024]{1,0:T(8,128)(2,1)S(1)}, u32[]{:S(2)}, u32[]{:S(2)}) collective-permute-start(bf16[256,1024]{1,0:T(8,128)(2,1)S(1)} %copy-done.65), channel_id=1, source_target_pairs={{0,16},{1,17},{2,18},{3,19},{4,20},{5,21},{6,22},{7,23},{8,24},{9,... | collective-permute-start | bytes 1572872 | tf_op jit(solution)/shard_map/ppermute | solution.py:517
  472.2 16.5 %collective-permute-start.75 = (bf16[256,1024]{1,0:T(8,128)(2,1)}, bf16[256,1024]{1,0:T(8,128)(2,1)}, u32[]{:S(2)}, u32[]{:S(2)}) collective-permute-start(bf16[256,1024]{1,0:T(8,128)(2,1)} %add_convert_fusion.3), channel_id=1, source_target_pairs={{0,8},{1,9},{2,10},{3,11},{4,12},{5,13},{6,14},{7,15},{8,0},{9,1},... | collective-permute-start | bytes 1572872 | tf_op jit(solution)/shard_map/ppermute | solution.py:517
  472.2 16.5 %collective-permute-start.76 = (bf16[64,4096]{1,0:T(8,128)(2,1)}, bf16[64,4096]{1,0:T(8,128)(2,1)}, u32[]{:S(2)}, u32[]{:S(2)}) collective-permute-start(bf16[64,4096]{1,0:T(8,128)(2,1)} %add_convert_fusion.2), channel_id=1, source_target_pairs={{0,8},{1,9},{2,10},{3,11},{4,12},{5,13},{6,14},{7,15},{8,0},{9,1},... | collective-permute-start | bytes 1572872 | tf_op jit(solution)/shard_map/ppermute | solution.py:517
  489.3 20.3 %collective-permute-start.86 = (bf16[16,128]{1,0:T(8,128)(2,1)S(1)}, bf16[16,128]{1,0:T(8,128)(2,1)S(1)}, u32[]{:S(2)}, u32[]{:S(2)}) collective-permute-start(bf16[16,128]{1,0:T(8,128)(2,1)S(1)} %get-tuple-element.370), channel_id=1, source_target_pairs={{0,2},{2,4},{4,6},{6,7},{7,5},{5,3},{3,1},{1,0},{8,9},{10,8},{12,1... | collective-permute-start | bytes 12296 | tf_op jit(solution)/shard_map/ppermute | solution.py:510
  492.1 19.2 %collective-permute-start.89 = (bf16[64,1536]{1,0:T(8,128)(2,1)S(1)}, bf16[64,1536]{1,0:T(8,128)(2,1)S(1)}, u32[]{:S(2)}, u32[]{:S(2)}) collective-permute-start(bf16[64,1536]{1,0:T(8,128)(2,1)S(1)} %get-tuple-element.331), channel_id=1, source_target_pairs={{0,1},{2,0},{4,2},{6,4},{7,6},{5,7},{3,5},{1,3},{8,10},{10,12},{12... | collective-permute-start | bytes 589832 | tf_op jit(solution)/shard_map/ppermute | solution.py:510
  492.7 18.6 %collective-permute-start.88 = (bf16[64,1536]{1,0:T(8,128)(2,1)S(1)}, bf16[64,1536]{1,0:T(8,128)(2,1)S(1)}, u32[]{:S(2)}, u32[]{:S(2)}) collective-permute-start(bf16[64,1536]{1,0:T(8,128)(2,1)S(1)} %get-tuple-element.332), channel_id=1, source_target_pairs={{0,2},{2,4},{4,6},{6,7},{7,5},{5,3},{3,1},{1,0},{8,9},{10,8},{12,1... | collective-permute-start | bytes 589832 | tf_op jit(solution)/shard_map/ppermute | solution.py:510
  495.6 15.7 %collective-permute-start.85 = (bf16[64,1536]{1,0:T(8,128)(2,1)S(1)}, bf16[64,1536]{1,0:T(8,128)(2,1)S(1)}, u32[]{:S(2)}, u32[]{:S(2)}) collective-permute-start(bf16[64,1536]{1,0:T(8,128)(2,1)S(1)} %get-tuple-element.333), channel_id=1, source_target_pairs={{0,1},{2,0},{4,2},{6,4},{7,6},{5,7},{3,5},{1,3},{8,10},{10,12},{12... | collective-permute-start | bytes 589832 | tf_op jit(solution)/shard_map/ppermute | solution.py:510
  (162 other events, 1371.3 us)
Sparse Core Ops, SparseCore 0:
  19.3 85.5 all-gather.2
  108.3 81.3 all-gather.4
  269.1 99.5 reduce-scatter.1

commit v5 on v4

--- a/solution.py
+++ b/solution.py
@@ -15,7 +15,7 @@
 GROUPS = 2
 PAIRS = D // LANES // GROUPS
 WIDE = D // GROUPS
-AXES = ("rep", "shard")
+AXES = ("cross", "core", "shard")
 RING_MOST = 16
 LOW = jnp.bfloat16
 FULL = jnp.float32
@@ -182,9 +182,9 @@
         ref[...] = jnp.zeros_like(ref)
 
 
-def pieces(rows):
-    step = rows // PARTS
-    return [slice(i * step, (i + 1) * step) for i in range(PARTS)]
+def pieces(rows, count=PARTS):
+    step = rows // count
+    return [slice(i * step, (i + 1) * step) for i in range(count)]
 
 
 LIMIT = pltpu.CompilerParams(vmem_limit_bytes=48 * 2**20)
@@ -217,7 +217,7 @@
 
 
 def inner_kernel(low_ref, w_ref, bias_ref, active_ref, slope_ref):
-    for rows in pieces(low_ref.shape[0]):
+    for rows in pieces(low_ref.shape[0], 4):
         pre = project(low_ref[rows, :], w_ref[...]) + bias_ref[...]
         below = 0.5 * (1.0 + lax.erf(pre * (0.5**0.5)))
         active_ref[rows, :] = (pre * below).astype(LOW)
@@ -273,8 +273,9 @@
 
 def outer_back_kernel(d_ref, w_ref, slope_ref, out_ref, sum_ref):
     sum_ref[...] = jnp.zeros_like(sum_ref)
-    for rows in pieces(d_ref.shape[0]):
-        d_pre = against(d_ref[rows, :], w_ref[...]) * slope_ref[rows, :].astype(FULL)
+    turned = w_ref[...].T
+    for rows in pieces(d_ref.shape[0], 4):
+        d_pre = project(d_ref[rows, :], turned) * slope_ref[rows, :].astype(FULL)
         out_ref[rows, :] = d_pre.astype(LOW)
         add_line(sum_ref, 0, d_pre)
 
@@ -296,43 +297,60 @@
 
 
 def inner_back_kernel(
-    d_pre_ref, w_ref, d_ref, unit_ref, inverse_ref, vec_ref, w_out_ref, out_ref, low_ref, attended_ref, sum_ref
+    d_pre_ref, w_ref, d_ref, unit_ref, inverse_ref, vec_ref, w_out_ref, out_ref, low_ref, attended_ref, sum_ref, total_ref
 ):
-    clear(sum_ref)
-    for rows in pieces(ROWS):
-        d_first = d_ref[rows, :] + against(d_pre_ref[rows, :], w_ref[...])
-        unit = unit_ref[rows, :]
-        d_inner = normal_back(d_first * line(vec_ref, GAIN_ONE), unit, inverse_ref[rows, 0:1])
-        low = d_inner.astype(LOW)
-        out_ref[rows, :] = d_inner
-        low_ref[rows, :] = low
-        attended_ref[rows, :] = against(low, w_out_ref[...]).astype(LOW)
-        add_line(sum_ref, 0, d_first * unit)
-        add_line(sum_ref, 1, d_first)
-        add_line(sum_ref, 2, d_inner)
+    step = pl.program_id(0)
+    turned = w_ref[...].T
+    for rows in pieces(total_ref.shape[0], 4):
+        part = project(d_pre_ref[rows, :], turned)
+
+        @pl.when(step == 0)
+        def _():
+            total_ref[rows, :] = d_ref[rows, :] + part
+
+        @pl.when(step > 0)
+        def _():
+            total_ref[rows, :] += part
+
+    @pl.when(step == pl.num_programs(0) - 1)
+    def _():
+        sum_ref[...] = jnp.zeros_like(sum_ref)
+        w_out_turned = w_out_ref[...].T
+        for rows in pieces(total_ref.shape[0], 8):
+            d_first = total_ref[rows, :]
+            unit = unit_ref[rows, :]
+            d_inner = normal_back(d_first * line(vec_ref, GAIN_ONE), unit, inverse_ref[rows, 0:1])
+            low = d_inner.astype(LOW)
+            out_ref[rows, :] = d_inner
+            low_ref[rows, :] = low
+            attended_ref[rows, :] = project(low, w_out_turned).astype(LOW)
+            add_line(sum_ref, 0, d_first * unit)
+            add_line(sum_ref, 1, d_first)
+            add_line(sum_ref, 2, d_inner)
 
 
 def inner_back(d_pre, w_inner, d_second, unit, inverse, vec, w_out):
     count, hidden = d_pre.shape
     return pl.pallas_call(
         inner_back_kernel,
-        grid=(count // ROWS,),
+        grid=(hidden // COLUMNS,),
         in_specs=[
-            rows_of(hidden),
-            kept((D, hidden)),
-            rows_of(D),
-            rows_of(D),
-            rows_of(LANES),
+            columns_of(count),
+            columns_of(D),
+            kept((count, D)),
+            kept((count, D)),
+            kept((count, LANES)),
             kept((8, D)),
             kept((D, D)),
         ],
-        out_specs=[rows_of(D), rows_of(D), rows_of(D), kept((8, D))],
+        out_specs=[kept((count, D)), kept((count, D)), kept((count, D)), kept((8, D))],
         out_shape=[
             jax.ShapeDtypeStruct((count, D), FULL),
             jax.ShapeDtypeStruct((count, D), LOW),
             jax.ShapeDtypeStruct((count, D), LOW),
             jax.ShapeDtypeStruct((8, D), FULL),
         ],
+        scratch_shapes=[pltpu.VMEM((count, D), FULL)],
         compiler_params=LIMIT,
         name="inner_back",
     )(d_pre, w_inner, d_second, unit, inverse, vec, w_out)
@@ -484,15 +502,14 @@
 
 class Links:
     def __init__(self, mesh):
-        self.reps, self.size = mesh.shape["rep"], mesh.shape["shard"]
+        self.reps, self.size = mesh.shape["cross"] * mesh.shape["core"], mesh.shape["shard"]
         size = self.size
         self.direct = size > RING_MOST or size % 2 == 1
         self.order = list(range(0, size, 2)) + list(range(size - 1, 0, -2))
         self.far = size // 2
         self.near = size - 1 - self.far
-        rep = lax.axis_index("rep")
         shard = lax.axis_index("shard")
-        self.core = rep % 2
+        self.core = lax.axis_index("core")
         self.sign = 1 - 2 * self.core
         self.place = jnp.where(shard % 2 == 0, shard // 2, size - 1 - shard // 2)
 
@@ -577,14 +594,25 @@
         return assemble(arrays, moves, places, self.size * rows)
 
     def gather_quarters(self, values):
-        rows = values.shape[0] // self.reps
-        mine = lax.dynamic_slice_in_dim(values, lax.axis_index("rep") * rows, rows, axis=0)
-        return lax.all_gather(mine, ("shard", "rep"), axis=0, tiled=True)
+        if self.direct:
+            return lax.all_gather(values, "shard", axis=0, tiled=True)
+        rows = values.shape[0]
+        half, part = rows // 2, rows // 4
+        place = self.core * half + lax.axis_index("cross") * part
+        mine = lax.dynamic_slice_in_dim(values, place, part, axis=0)
+        mine = lax.all_gather(mine, ("shard", "cross"), axis=0, tiled=True)
+        (mine,) = yield [mine]
+        (other,) = yield [self.swap(mine, 1)]
+        moves, places = [], []
+        for shard in range(self.size):
+            moves += [(0, shard * half, half), (1, shard * half, half)]
+            places += [shard * rows + self.core * half, shard * rows + (1 - self.core) * half]
+        return assemble([mine, other], moves, places, self.size * rows)
 
     def reduce_halves(self, values, rounds):
         if self.direct:
             own = lax.psum_scatter(values, "shard", scatter_dimension=0, tiled=True)
-            return lax.psum(own, "rep").astype(FULL)
+            return lax.psum(own, ("cross", "core")).astype(FULL)
         width = values.shape[1]
         half = values.shape[0] // self.size // 2
         split = values.reshape(self.size, 2, half, width)
@@ -592,6 +620,7 @@
         (other,) = yield [other]
         mine = lax.dynamic_index_in_dim(split, self.core, axis=1, keepdims=False)
         total = (mine.astype(FULL) + other.astype(FULL)).astype(LOW).reshape(self.size * half, width)
+        (total,) = yield [total]
         total = lax.psum_scatter(total, "shard", scatter_dimension=0, tiled=True)
         for _ in range(rounds):
             yield []
@@ -609,7 +638,7 @@
     def reduce(self, values):
         if self.direct:
             own = lax.psum_scatter(values, "shard", scatter_dimension=0, tiled=True)
-            return lax.psum(own, "rep").astype(FULL)
+            return lax.psum(own, ("cross", "core")).astype(FULL)
         width = values.shape[1]
         half = values.shape[0] // self.size // 2
         split = values.reshape(self.size, 2, half, width)
@@ -654,8 +683,8 @@
             self.running.pop(name, None)
             self.results[name] = end.value
 
-    def advance(self, *values):
-        running = list(self.running.items())
+    def advance(self, *values, near=None):
+        running = [item for item in self.running.items() if near is None or item[0] in near]
         flat = list(values)
         for _, (_, flight) in running:
             flat += flight
@@ -707,43 +736,48 @@
     room = -(-used // (32 * LANES)) * 32 * LANES
     flow = Flow()
     flow.start("group0", links.gather(own_groups[0]))
-    *vectors, b_inner, own_groups[1], w_inner, w_outer = flow.advance(
-        *vectors, b_inner, own_groups[1], w_inner, w_outer
+    w_inner = flow.advance(w_inner)
+    flow.start("inner", links.gather_quarters(w_inner))
+    own_groups[1], w_outer, *own_vectors = flow.advance(
+        own_groups[1], w_outer, *vectors, b_inner, near=("group0",)
     )
-    whole_inner = links.gather_quarters(w_inner)
-    whole_outer = links.gather_quarters(w_outer)
-    packed = jnp.pad(jnp.concatenate(vectors + [b_inner]), (0, room - used))
+    flow.start("outer", links.gather_quarters(w_outer))
+    flow.start("group1", links.gather(own_groups[1]))
+    packed = jnp.pad(jnp.concatenate(own_vectors), (0, room - used))
     flow.start("small", links.gather_small(packed.reshape(room // LANES, LANES), size * hidden))
-    flow.advance()
-    tokens_turned, own_groups[1] = tie(turn(tokens), own_groups[1])
-    flow.start("group1", links.gather(own_groups[1]))
-    flow.advance()
-    flow.advance()
+    tokens_turned, w_out = flow.advance(turn(tokens), w_out, near=("group0", "group1", "small"))
+    flow.start("out", links.gather(w_out))
+    flow.advance(near=("group0", "group1", "small"))
     whole_groups = [flow.take("group0")]
-    vec, bias_inner, bias_groups = flow.take("small")
 
     projected = []
     attended, lse = None, []
     for g in range(GROUPS):
+        part = project(tokens, whole_groups[g])
+        if g == 0:
+            vec, bias_inner, bias_groups = flow.take("small")
         bias = bias_groups[:, g * 3 * WIDE : (g + 1) * 3 * WIDE]
-        projected.append((project(tokens, whole_groups[g]) + bias).astype(LOW))
+        projected.append((part + bias).astype(LOW))
         if g == 0:
-            projected[g], w_out = flow.advance(projected[g], w_out)
-            flow.start("out", links.gather(w_out))
+            projected[g] = flow.advance(projected[g], near=("group1", "out"))
+            attended, logs = attend(projected[g], g, attended)
+            attended = flow.advance(attended, near=("group1", "out", "inner"))
+            whole_groups.append(flow.take("group1"))
         else:
-            projected[g] = flow.advance(projected[g])
-        attended, logs = attend(projected[g], g, attended)
+            projected[g] = flow.advance(projected[g], near=("inner", "out"))
+            attended, logs = attend(projected[g], g, attended)
+            attended = flow.advance(attended, near=("inner", "out"))
         lse.append(logs)
-        attended = flow.advance(attended)
-        if g == 0:
-            whole_groups.append(flow.take("group1"))
     whole_out = flow.take("out")
+    whole_inner = flow.take("inner")
     unit_one, inverse_one, first_low = out_norm(attended, whole_out, tokens, vec)
+    first_low = flow.advance(first_low, near=("outer",))
     active, slope = inner_gelu(first_low, whole_inner, bias_inner)
+    whole_outer = flow.take("outer")
     output, d_second, d_mid, sums_two = outer_norms(active, whole_outer, unit_one, vec, cotangent)
 
     grad_outer, d_mid = tie(gram(active, d_mid).astype(LOW), d_mid)
-    flow.start("outer_back", links.reduce_halves(grad_outer, 5))
+    flow.start("outer_back", links.reduce_halves(grad_outer, 4))
     d_pre, sum_inner = outer_back(d_mid, whole_outer, slope)
     d_pre = flow.advance(d_pre)
     grad_inner, d_pre = flow.advance(gram(first_low, d_pre).astype(LOW), d_pre)
@@ -816,7 +850,9 @@
 
 
 def solution(mesh):
-    rows = P(("rep", "shard"), None)
+    reps, size = mesh.shape["rep"], mesh.shape["shard"]
+    mesh = jax.sharding.Mesh(mesh.devices.reshape(reps // 2, 2, size), AXES)
+    rows = P(AXES, None)
     matrix = P("shard", None)
     vector = P("shard")
     return jax.shard_map(

time: 561 us -> 578 us (1.030)
  waiting for transfers between devices: 92.4 us -> 105 us
    all_gather x2, waiting for transfers between devices: 0.01 us -> 11.9 us  [gather_quarters(): mine = lax.all_gather(mine, ('shard', 'cross'), axis=0, tiled=True)]
    pallas_call x3 -> x5, Pallas kernels: 12 us -> 16.5 us  [assemble(): pl.pallas_call(functools.partial(assemble_kernel, moves, align), in_specs...]
    ppermute x39 -> x41, waiting for transfers between devices: 23.9 us -> 20.4 us  [swap(): return lax.ppermute(values, AXES, pairs)]
    ppermute x39 -> x41, starting transfers between devices: 15.5 us -> 13.3 us  [swap(): return lax.ppermute(values, AXES, pairs)]
    unnamed x186 -> x234, local copies, waits for them, and re-layouts: 48.4 us -> 50.4 us
  transfers between devices with their start and end apart: 105 -> 107, of which waited for: 25 -> 28; matrix products, arithmetic and copies ran while one was open for 13% -> 11% of each run, Pallas kernels for 33% -> 32%
where the time goes in v5:
time: 578 us; the launch traced here: 568 us
  Pallas kernels  201 us (35%)
  waiting for transfers between devices  105 us (18%)
  starting transfers between devices  86.4 us (15%)
  local copies, waits for them, and re-layouts  68.6 us (12%)
  other arithmetic  54.7 us (9%)
  matrix products  36.6 us (6%)
  between operations  15.7 us (3%)
    ppermute x63, waiting for transfers between devices, hop(): return lax.ppermute(values, AXES, pairs)  73 us
    ppermute x63, starting transfers between devices, hop(): return lax.ppermute(values, AXES, pairs)  72.9 us
    unnamed x234, local copies, waits for them, and re-layouts  50.4 us
    pallas_call x2, Pallas kernels, attend_back(): pl.pallas_call(attend_back_kernel, grid=(count // SEQ, PAIRS), in_specs=t...  36.2 us
    pallas_call x1, Pallas kernels, inner_back(): pl.pallas_call(inner_back_kernel, grid=(hidden // COLUMNS,), in_specs=[co...  31.7 us
    dot_general x3, matrix products, gram(): lax.dot_general(left, right, (((0,), (0,)), ((), ())), preferred_element_...  29.4 us
    pallas_call x2, Pallas kernels, attend(): pl.pallas_call(attend_kernel, grid=(seqs, PAIRS), in_specs=triple() + [pl...  22.6 us
    ppermute x41, waiting for transfers between devices, swap(): return lax.ppermute(values, AXES, pairs)  20.4 us
  transfers between devices with their start and end apart: 107, of which 28 were waited for; matrix products, arithmetic and copies ran while one was open for 11% of the time, Pallas kernels for 32%

profile of v5, /device:TPU:0, one launch (start us, length us, event | category | flops | bytes accessed | tf_op | source)
XLA Modules:
  0.0 568.3 jit_solution(12945737441337485574)
XLA Ops:
  12.7 5.1 collective-permute-done.refs_1_
  40.9 4.3 collective-permute-start.11
  45.2 4.3 turn.1.left_ref
  52.9 4.0 collective-permute-done.21.refs_3_
  63.3 4.3 collective-permute-done.18.refs_6_
  85.7 5.0 assemble.5.w_ref
  95.7 6.5 %collective-permute-done.28.refs_10_ = bf16[64,1536]{1,0:T(8,128)(2,1)S(1)} collective-permute-done((bf16[64,1536]{1,0:T(8,128)(2,1)}, bf16[64,1536]{1,0:T(8,128)(2,1)S(1)}, u32[]{:S(2)}, u32[]{:S(2)}) %collective-permute-start.28) | collective-permute-done | bytes 196640 | tf_op jit(solution)/shard_map/ppermute | solution.py:527
  108.5 11.3 %attend.2 = (bf16[1024,1024]{1,0:T(8,128)(2,1)S(1)}, f32[8,2,512]{2,1,0:T(2,128)S(1)}) custom-call(bf16[1024,1536]{1,0:T(8,128)(2,1)S(1)} %fusion.1.query_ref.key_ref.value_ref, bf16[1024,1536]{1,0:T(8,128)(2,1)S(1)} %fusion.1.query_ref.key_ref.value_ref, bf16[1024,1536]{1,0:T(8,128)(2,1)S(1)} %fusion.1.query_ref.key_ref.value_ref), custom_call_target="tpu_custom_call" | custom-call | tf_op jit(solution)/shard_map/attend/pallas_call | solution.py:119
  128.0 4.0 collective-permute-done.40.refs_14_
  139.7 4.1 assemble.6.w_ref
  149.6 11.3 %attend.3 = (bf16[1024,1024]{1,0:T(8,128)(2,1)S(1)}, f32[8,2,512]{2,1,0:T(2,128)S(1)}) custom-call(bf16[1024,1536]{1,0:T(8,128)(2,1)S(1)} %fusion.2.query_ref.key_ref.value_ref, bf16[1024,1536]{1,0:T(8,128)(2,1)S(1)} %fusion.2.query_ref.key_ref.value_ref, bf16[1024,1536]{1,0:T(8,128)(2,1)S(1)} %fusion.2.query_ref.key_ref.value_ref, ...), custom_call_target="tpu_custom_call", output_to_operand_aliasing={{0}: (3, {})} | custom-call | tf_op jit(solution)/shard_map/attend/pallas_call | solution.py:119
  167.1 7.4 %out_norm.1 = (f32[1024,1024]{1,0:T(8,128)}, f32[1024,128]{1,0:T(8,128)S(1)}, bf16[1024,1024]{1,0:T(8,128)(2,1)S(1)}) custom-call(bf16[1024,1024]{1,0:T(8,128)(2,1)S(1)} %get-tuple-element.229.attended_ref, bf16[1024,1024]{1,0:T(8,128)(2,1)} %copy-done.8, bf16[1024,1024]{1,0:T(8,128)(2,1)} %tokens_ref.1, f32[8,1024]{1,0:T(8,128)S(1)} %copy-done.38), custom_call_target="tpu_custom_call" | custom-call | tf_op jit(solution)/shard_map/out_norm/pallas_call | solution.py:204
  176.6 11.8 %all-gather.5.cloned.1.call-done.refs_0_ = bf16[2048,1024]{1,0:T(8,128)(2,1)} async-done(((bf16[128,1024]{1,0:T(8,128)(2,1)}), bf16[2048,1024]{1,0:T(8,128)(2,1)}) %all-gather.5.cloned.1.call-update) | async-done | bytes 4194320 | tf_op jit(solution)/shard_map/all_gather | solution.py:603
  197.6 19.0 %inner_gelu.1 = (bf16[1024,4096]{1,0:T(8,128)(2,1)}, bf16[1024,4096]{1,0:T(8,128)(2,1)}) custom-call(bf16[1024,1024]{1,0:T(8,128)(2,1)S(1)} %copy-done.29, bf16[1024,4096]{1,0:T(8,128)(2,1)} %copy-done.5, f32[1,4096]{1,0:T(1,128)S(1)} %copy-done.78), custom_call_target="tpu_custom_call" | custom-call | tf_op jit(solution)/shard_map/inner_gelu/pallas_call | solution.py:229
  222.9 18.5 %outer_norms.1 = (bf16[1024,1024]{1,0:T(8,128)(2,1)}, f32[1024,1024]{1,0:T(8,128)}, bf16[1024,1024]{1,0:T(8,128)(2,1)S(1)}, f32[8,1024]{1,0:T(8,128)S(1)}) custom-call(bf16[1024,4096]{1,0:T(8,128)(2,1)} %get-tuple-element.243.active_ref, bf16[4096,1024]{1,0:T(8,128)(2,1)} %copy-done.4, f32[1024,1024]{1,0:T(8,128)} %get-tuple-element.245.unit_ref, ...), custom_call_target="tpu_custom_call" | custom-call | tf_op jit(solution)/shard_map/outer_norms/pallas_call | solution.py:258
  241.4 12.1 %convolution_convert_fusion.1 = bf16[4096,1024]{1,0:T(8,128)(2,1)S(1)} fusion(bf16[1024,4096]{1,0:T(8,128)(2,1)} %get-tuple-element.243.active_ref, bf16[1024,1024]{1,0:T(8,128)(2,1)S(1)} %get-tuple-element.248.d_ref), kind=kOutput, calls=%fused_computation.3 | convolution fusion | flops 8594128896 | bytes 18874368 | tf_op jit(solution)/shard_map/dot_general | solution.py:29
  260.1 15.4 %outer_back.1 = (bf16[1024,4096]{1,0:T(8,128)(2,1)}, f32[1,4096]{1,0:T(1,128)S(1)}) custom-call(bf16[1024,1024]{1,0:T(8,128)(2,1)S(1)} %copy-done.32, bf16[4096,1024]{1,0:T(8,128)(2,1)} %copy-done.4, bf16[1024,4096]{1,0:T(8,128)(2,1)} %get-tuple-element.249.slope_ref), custom_call_target="tpu_custom_call" | custom-call | tf_op jit(solution)/shard_map/outer_back/pallas_call | solution.py:285
  275.6 14.9 %convolution_convert_fusion = bf16[1024,4096]{1,0:T(8,128)(2,1)} fusion(bf16[1024,1024]{1,0:T(8,128)(2,1)S(1)} %copy-done.30, bf16[1024,4096]{1,0:T(8,128)(2,1)} %get-tuple-element.254.d_pre_ref), kind=kOutput, calls=%fused_computation.2 | convolution fusion | flops 8594128896 | bytes 18874368 | tf_op jit(solution)/shard_map/dot_general | solution.py:29
  290.5 6.3 %fusion = bf16[8,256,1024]{2,1,0:T(8,128)(2,1)} fusion(bf16[8,256,1024]{2,1,0:T(8,128)(2,1)} %collective-permute-done.51, bf16[8,2,256,1024]{3,2,1,0:T(8,128)(2,1)S(1)} %bitcast.405, s32[]{:T(128)S(6)} %select_n.586), kind=kLoop, calls=%fused_computation.1 | loop fusion | flops 8388608 | bytes 12582916 | tf_op jit(solution)/shard_map/convert_element_type | solution.py:622
  296.8 4.6 dynamic-slice_bitcast_fusion
  302.5 31.7 %inner_back.1 = (f32[1024,1024]{1,0:T(8,128)}, bf16[1024,1024]{1,0:T(8,128)(2,1)S(1)}, bf16[1024,1024]{1,0:T(8,128)(2,1)S(1)}, f32[8,1024]{1,0:T(8,128)S(1)}) custom-call(bf16[1024,4096]{1,0:T(8,128)(2,1)} %get-tuple-element.254.d_pre_ref, bf16[1024,4096]{1,0:T(8,128)(2,1)} %copy-done.5, f32[1024,1024]{1,0:T(8,128)} %get-tuple-element.255.d_ref, ...), custom_call_target="tpu_custom_call" | custom-call | tf_op jit(solution)/shard_map/inner_back/pallas_call | solution.py:334
  344.8 18.2 %attend_back.2 = (bf16[1024,1536]{1,0:T(8,128)(2,1)S(1)}, f32[8,1536]{1,0:T(8,128)S(1)}) custom-call(bf16[1024,1536]{1,0:T(8,128)(2,1)S(1)} %fusion.1.query_ref.key_ref.value_ref, bf16[1024,1536]{1,0:T(8,128)(2,1)S(1)} %fusion.1.query_ref.key_ref.value_ref, bf16[1024,1536]{1,0:T(8,128)(2,1)S(1)} %fusion.1.query_ref.key_ref.value_ref, ...), custom_call_target="tpu_custom_call" | custom-call | tf_op jit(solution)/shard_map/attend_back/pallas_call | solution.py:136
  371.0 5.2 product.2
  376.2 17.7 %collective-permute-done.57 = bf16[64,1024]{1,0:T(8,128)(2,1)S(1)} collective-permute-done((bf16[64,1024]{1,0:T(8,128)(2,1)S(1)}, bf16[64,1024]{1,0:T(8,128)(2,1)S(1)}, u32[]{:S(2)}, u32[]{:S(2)}) %collective-permute-start.57) | collective-permute-done | bytes 131104 | tf_op jit(solution)/shard_map/ppermute | solution.py:527
  393.9 4.8 collective-permute-done.56
  411.0 18.0 %attend_back.3 = (bf16[1024,1536]{1,0:T(8,128)(2,1)S(1)}, f32[8,1536]{1,0:T(8,128)S(1)}) custom-call(bf16[1024,1536]{1,0:T(8,128)(2,1)S(1)} %copy-done.3, bf16[1024,1536]{1,0:T(8,128)(2,1)S(1)} %copy-done.3, bf16[1024,1536]{1,0:T(8,128)(2,1)S(1)} %copy-done.3, bf16[1024,1024]{1,0:T(8,128)(2,1)S(1)} %copy-done.23, f32[8,2,512]{2,1,0:T(2,128)S(1)} %get-tuple-element.279.lse_ref), custom_call_target="tpu_custom_call" | custom-call | tf_op jit(solution)/shard_map/attend_back/pallas_call | solution.py:136
  445.4 5.2 product.3
  470.5 5.0 collective-permute-done.73
  494.1 8.3 %tokens_back.2.base_ref = f32[1024,1024]{1,0:T(8,128)} custom-call(f32[1024,1024]{1,0:T(8,128)} %get-tuple-element.257.base_ref, bf16[1024,1536]{1,0:T(8,128)(2,1)S(1)} %copy-done.11, bf16[1024,1536]{1,0:T(8,128)(2,1)} %copy-done.9), custom_call_target="tpu_custom_call" | custom-call | tf_op jit(solution)/shard_map/tokens_back/pallas_call | solution.py:365
  515.8 7.6 %tokens_back.3 = bf16[1024,1024]{1,0:T(8,128)(2,1)} custom-call(f32[1024,1024]{1,0:T(8,128)} %tokens_back.2.base_ref, bf16[1024,1536]{1,0:T(8,128)(2,1)S(1)} %copy-done.16, bf16[1024,1536]{1,0:T(8,128)(2,1)} %copy-done.12), custom_call_target="tpu_custom_call" | custom-call | tf_op jit(solution)/shard_map/tokens_back/pallas_call | solution.py:365
  543.5 5.6 collective-permute-done.97
  550.4 6.7 %collective-permute-done.98 = bf16[64,1536]{1,0:T(8,128)(2,1)S(1)} collective-permute-done((bf16[64,1536]{1,0:T(8,128)(2,1)S(1)}, bf16[64,1536]{1,0:T(8,128)(2,1)S(1)}, u32[]{:S(2)}, u32[]{:S(2)}) %collective-permute-start.98) | collective-permute-done | bytes 196640 | tf_op jit(solution)/shard_map/ppermute | solution.py:534
  (520 shorter events, 244.6 us)
Async XLA Ops:
  7.3 117.1 %all-gather.3.cloned.1.call-start = ((), (), s32[]{:S(2)}) async-start(), calls=%async_computation.1 | async-start | bytes 4456448 | tf_op jit(solution)/shard_map/all_gather | solution.py:603
  19.1 169.3 %all-gather.5.cloned.1.call-start = ((), (), s32[]{:S(2)}) async-start(), calls=%async_computation.2 | async-start | bytes 4456448 | tf_op jit(solution)/shard_map/all_gather | solution.py:603
  28.3 426.4 %reduce-scatter.2.cloned.1.call-start = ((), (), s32[]{:S(2)}) async-start(), calls=%async_computation.3 | async-start | bytes 4718592 | tf_op jit(solution)/shard_map/reduce_scatter | solution.py:624
  68.4 22.3 %collective-permute-start.31 = (bf16[64,1024]{1,0:T(8,128)(2,1)}, bf16[64,1024]{1,0:T(8,128)(2,1)S(1)}, u32[]{:S(2)}, u32[]{:S(2)}) collective-permute-start(bf16[64,1024]{1,0:T(8,128)(2,1)} %constant_dynamic-slice_fusion.18), channel_id=1, source_target_pairs={{0,2},{2,4},{4,6},{6,7},{7,5},{5,3},{3,1},{1,0},{8,9},{10,8},{12,1... | collective-permute-start | bytes 393224 | tf_op jit(solution)/shard_map/ppermute | solution.py:527
  79.6 22.6 %collective-permute-start.29 = (bf16[64,1536]{1,0:T(8,128)(2,1)}, bf16[64,1536]{1,0:T(8,128)(2,1)}, u32[]{:S(2)}, u32[]{:S(2)}) collective-permute-start(bf16[64,1536]{1,0:T(8,128)(2,1)} %collective-permute-done.17.refs_5_), channel_id=1, source_target_pairs={{0,8},{1,9},{2,10},{3,11},{4,12},{5,13},{6,14},{7,15},{8,0},{9,1},... | collective-permute-start | bytes 589832 | tf_op jit(solution)/shard_map/ppermute | solution.py:534
  82.5 19.7 %collective-permute-start.28 = (bf16[64,1536]{1,0:T(8,128)(2,1)}, bf16[64,1536]{1,0:T(8,128)(2,1)S(1)}, u32[]{:S(2)}, u32[]{:S(2)}) collective-permute-start(bf16[64,1536]{1,0:T(8,128)(2,1)} %collective-permute-done.18.refs_6_), channel_id=1, source_target_pairs={{0,1},{2,0},{4,2},{6,4},{7,6},{5,7},{3,5},{1,3},{8,10},{10,12},{12... | collective-permute-start | bytes 589832 | tf_op jit(solution)/shard_map/ppermute | solution.py:527
  105.0 18.7 %collective-permute-start.35 = (bf16[64,1536]{1,0:T(8,128)(2,1)S(1)}, bf16[64,1536]{1,0:T(8,128)(2,1)S(1)}, u32[]{:S(2)}, u32[]{:S(2)}) collective-permute-start(bf16[64,1536]{1,0:T(8,128)(2,1)S(1)} %collective-permute-done.28.refs_10_), channel_id=1, source_target_pairs={{0,8},{1,9},{2,10},{3,11},{4,12},{5,13},{6,14},{7,15},{8,0},{9,1},... | collective-permute-start | bytes 589832 | tf_op jit(solution)/shard_map/ppermute | solution.py:534
  124.4 23.2 %collective-permute-start.41 = (bf16[512,4096]{1,0:T(8,128)(2,1)}, bf16[512,4096]{1,0:T(8,128)(2,1)S(1)}, u32[]{:S(2)}, u32[]{:S(2)}) collective-permute-start(bf16[512,4096]{1,0:T(8,128)(2,1)} %all-gather.3.cloned.1.call-done.refs_0_), channel_id=1, source_target_pairs={{0,8},{1,9},{2,10},{3,11},{4,12},{5,13},{6,14},{7,15},{8,0},{9,1},... | collective-permute-start | bytes 12582920 | tf_op jit(solution)/shard_map/ppermute | solution.py:534
  124.9 22.7 %collective-permute-start.42 = (bf16[64,1024]{1,0:T(8,128)(2,1)}, bf16[64,1024]{1,0:T(8,128)(2,1)S(1)}, u32[]{:S(2)}, u32[]{:S(2)}) collective-permute-start(bf16[64,1024]{1,0:T(8,128)(2,1)} %copy-done.64), channel_id=1, source_target_pairs={{0,2},{2,4},{4,6},{6,7},{7,5},{5,3},{3,1},{1,0},{8,9},{10,8},{12,1... | collective-permute-start | bytes 393224 | tf_op jit(solution)/shard_map/ppermute | solution.py:527
  125.9 21.7 %collective-permute-start.44 = (bf16[64,1024]{1,0:T(8,128)(2,1)}, bf16[64,1024]{1,0:T(8,128)(2,1)S(1)}, u32[]{:S(2)}, u32[]{:S(2)}) collective-permute-start(bf16[64,1024]{1,0:T(8,128)(2,1)} %copy-done.64), channel_id=1, source_target_pairs={{0,8},{1,9},{2,10},{3,11},{4,12},{5,13},{6,14},{7,15},{8,0},{9,1},... | collective-permute-start | bytes 393224 | tf_op jit(solution)/shard_map/ppermute | solution.py:534
  126.9 20.7 %collective-permute-start.43 = (bf16[64,1024]{1,0:T(8,128)(2,1)}, bf16[64,1024]{1,0:T(8,128)(2,1)S(1)}, u32[]{:S(2)}, u32[]{:S(2)}) collective-permute-start(bf16[64,1024]{1,0:T(8,128)(2,1)} %copy-done.66), channel_id=1, source_target_pairs={{0,1},{2,0},{4,2},{6,4},{7,6},{5,7},{3,5},{1,3},{8,10},{10,12},{12... | collective-permute-start | bytes 393224 | tf_op jit(solution)/shard_map/ppermute | solution.py:527
  188.5 28.1 %collective-permute-start.50 = (bf16[2048,1024]{1,0:T(8,128)(2,1)}, bf16[2048,1024]{1,0:T(8,128)(2,1)}, u32[]{:S(2)}, u32[]{:S(2)}) collective-permute-start(bf16[2048,1024]{1,0:T(8,128)(2,1)} %all-gather.5.cloned.1.call-done.refs_0_), channel_id=1, source_target_pairs={{0,8},{1,9},{2,10},{3,11},{4,12},{5,13},{6,14},{7,15},{8,0},{9,1},... | collective-permute-start | bytes 12582920 | tf_op jit(solution)/shard_map/ppermute | solution.py:534
  301.4 32.8 %collective-permute-start.52 = (bf16[8,64,4096]{2,1,0:T(8,128)(2,1)}, bf16[8,64,4096]{2,1,0:T(8,128)(2,1)}, u32[]{:S(2)}, u32[]{:S(2)}) collective-permute-start(bf16[8,64,4096]{2,1,0:T(8,128)(2,1)} %dynamic-slice_bitcast_fusion), channel_id=1, source_target_pairs={{0,8},{1,9},{2,10},{3,11},{4,12},{5,13},{6,14},{7,15},{8,0},{9,1},... | collective-permute-start | bytes 12582920 | tf_op jit(solution)/shard_map/ppermute | solution.py:534
  339.0 25.7 %collective-permute-start.54 = (bf16[8,64,1024]{2,1,0:T(8,128)(2,1)}, bf16[8,64,1024]{2,1,0:T(8,128)(2,1)}, u32[]{:S(2)}, u32[]{:S(2)}) collective-permute-start(bf16[8,64,1024]{2,1,0:T(8,128)(2,1)} %dynamic-slice_bitcast_fusion.4), channel_id=1, source_target_pairs={{0,8},{1,9},{2,10},{3,11},{4,12},{5,13},{6,14},{7,15},{8,0},{9,1},... | collective-permute-start | bytes 3145736 | tf_op jit(solution)/shard_map/ppermute | solution.py:534
  341.6 23.0 %collective-permute-start.53 = (bf16[64,4096]{1,0:T(8,128)(2,1)}, bf16[64,4096]{1,0:T(8,128)(2,1)}, u32[]{:S(2)}, u32[]{:S(2)}) collective-permute-start(bf16[64,4096]{1,0:T(8,128)(2,1)} %fusion.17), channel_id=1, source_target_pairs={{0,2},{2,4},{4,6},{6,7},{7,5},{5,3},{3,1},{1,0},{8,9},{10,8},{12,1... | collective-permute-start | bytes 1572872 | tf_op jit(solution)/shard_map/ppermute | solution.py:527
  366.9 27.1 %collective-permute-start.55 = (bf16[64,4096]{1,0:T(8,128)(2,1)S(1)}, bf16[64,4096]{1,0:T(8,128)(2,1)S(1)}, u32[]{:S(2)}, u32[]{:S(2)}) collective-permute-start(bf16[64,4096]{1,0:T(8,128)(2,1)S(1)} %get-tuple-element.338), channel_id=1, source_target_pairs={{0,2},{2,4},{4,6},{6,7},{7,5},{5,3},{3,1},{1,0},{8,9},{10,8},{12,1... | collective-permute-start | bytes 1572872 | tf_op jit(solution)/shard_map/ppermute | solution.py:527
  367.9 30.8 %collective-permute-start.56 = (bf16[64,4096]{1,0:T(8,128)(2,1)S(1)}, bf16[64,4096]{1,0:T(8,128)(2,1)S(1)}, u32[]{:S(2)}, u32[]{:S(2)}) collective-permute-start(bf16[64,4096]{1,0:T(8,128)(2,1)S(1)} %get-tuple-element.337), channel_id=1, source_target_pairs={{0,1},{2,0},{4,2},{6,4},{7,6},{5,7},{3,5},{1,3},{8,10},{10,12},{12... | collective-permute-start | bytes 1572872 | tf_op jit(solution)/shard_map/ppermute | solution.py:527
  369.9 24.0 %collective-permute-start.57 = (bf16[64,1024]{1,0:T(8,128)(2,1)S(1)}, bf16[64,1024]{1,0:T(8,128)(2,1)S(1)}, u32[]{:S(2)}, u32[]{:S(2)}) collective-permute-start(bf16[64,1024]{1,0:T(8,128)(2,1)S(1)} %fusion.62), channel_id=1, source_target_pairs={{0,2},{2,4},{4,6},{6,7},{7,5},{5,3},{3,1},{1,0},{8,9},{10,8},{12,1... | collective-permute-start | bytes 393224 | tf_op jit(solution)/shard_map/ppermute | solution.py:527
  400.0 31.3 %collective-permute-start.62 = (bf16[8,64,1536]{2,1,0:T(8,128)(2,1)}, bf16[8,64,1536]{2,1,0:T(8,128)(2,1)}, u32[]{:S(2)}, u32[]{:S(2)}) collective-permute-start(bf16[8,64,1536]{2,1,0:T(8,128)(2,1)} %dynamic-slice_bitcast_fusion.3), channel_id=1, source_target_pairs={{0,8},{1,9},{2,10},{3,11},{4,12},{5,13},{6,14},{7,15},{8,0},{9,1},... | collective-permute-start | bytes 4718600 | tf_op jit(solution)/shard_map/ppermute | solution.py:534
  403.5 27.8 %collective-permute-start.58 = (bf16[64,4096]{1,0:T(8,128)(2,1)}, bf16[64,4096]{1,0:T(8,128)(2,1)}, u32[]{:S(2)}, u32[]{:S(2)}) collective-permute-start(bf16[64,4096]{1,0:T(8,128)(2,1)} %get-tuple-element.336), channel_id=1, source_target_pairs={{0,2},{2,4},{4,6},{6,7},{7,5},{5,3},{3,1},{1,0},{8,9},{10,8},{12,1... | collective-permute-start | bytes 1572872 | tf_op jit(solution)/shard_map/ppermute | solution.py:527
  403.5 27.8 %collective-permute-start.59 = (bf16[64,4096]{1,0:T(8,128)(2,1)}, bf16[64,4096]{1,0:T(8,128)(2,1)}, u32[]{:S(2)}, u32[]{:S(2)}) collective-permute-start(bf16[64,4096]{1,0:T(8,128)(2,1)} %get-tuple-element.335), channel_id=1, source_target_pairs={{0,1},{2,0},{4,2},{6,4},{7,6},{5,7},{3,5},{1,3},{8,10},{10,12},{12... | collective-permute-start | bytes 1572872 | tf_op jit(solution)/shard_map/ppermute | solution.py:527
  407.4 23.9 %collective-permute-start.60 = (bf16[64,1024]{1,0:T(8,128)(2,1)}, bf16[64,1024]{1,0:T(8,128)(2,1)S(1)}, u32[]{:S(2)}, u32[]{:S(2)}) collective-permute-start(bf16[64,1024]{1,0:T(8,128)(2,1)} %get-tuple-element.356), channel_id=1, source_target_pairs={{0,2},{2,4},{4,6},{6,7},{7,5},{5,3},{3,1},{1,0},{8,9},{10,8},{12,1... | collective-permute-start | bytes 393224 | tf_op jit(solution)/shard_map/ppermute | solution.py:527
  407.4 23.9 %collective-permute-start.61 = (bf16[64,1024]{1,0:T(8,128)(2,1)}, bf16[64,1024]{1,0:T(8,128)(2,1)S(1)}, u32[]{:S(2)}, u32[]{:S(2)}) collective-permute-start(bf16[64,1024]{1,0:T(8,128)(2,1)} %get-tuple-element.355), channel_id=1, source_target_pairs={{0,1},{2,0},{4,2},{6,4},{7,6},{5,7},{3,5},{1,3},{8,10},{10,12},{12... | collective-permute-start | bytes 393224 | tf_op jit(solution)/shard_map/ppermute | solution.py:527
  434.8 19.8 %collective-permute-start.63 = (bf16[64,4096]{1,0:T(8,128)(2,1)}, bf16[64,4096]{1,0:T(8,128)(2,1)S(1)}, u32[]{:S(2)}, u32[]{:S(2)}) collective-permute-start(bf16[64,4096]{1,0:T(8,128)(2,1)} %get-tuple-element.334), channel_id=1, source_target_pairs={{0,2},{2,4},{4,6},{6,7},{7,5},{5,3},{3,1},{1,0},{8,9},{10,8},{12,1... | collective-permute-start | bytes 1572872 | tf_op jit(solution)/shard_map/ppermute | solution.py:527
  434.8 19.8 %collective-permute-start.64 = (bf16[64,4096]{1,0:T(8,128)(2,1)}, bf16[64,4096]{1,0:T(8,128)(2,1)S(1)}, u32[]{:S(2)}, u32[]{:S(2)}) collective-permute-start(bf16[64,4096]{1,0:T(8,128)(2,1)} %get-tuple-element.333), channel_id=1, source_target_pairs={{0,1},{2,0},{4,2},{6,4},{7,6},{5,7},{3,5},{1,3},{8,10},{10,12},{12... | collective-permute-start | bytes 1572872 | tf_op jit(solution)/shard_map/ppermute | solution.py:527
  454.7 20.7 %collective-permute-start.69 = (bf16[256,1024]{1,0:T(8,128)(2,1)}, bf16[256,1024]{1,0:T(8,128)(2,1)S(1)}, u32[]{:S(2)}, u32[]{:S(2)}) collective-permute-start(bf16[256,1024]{1,0:T(8,128)(2,1)} %reduce-scatter.2.cloned.1.call-done), channel_id=1, source_target_pairs={{0,16},{1,17},{2,18},{3,19},{4,20},{5,21},{6,22},{7,23},{8,24},{9,... | collective-permute-start | bytes 1572872 | tf_op jit(solution)/shard_map/ppermute | solution.py:534
  457.3 21.5 %collective-permute-start.76 = (bf16[8,64,1536]{2,1,0:T(8,128)(2,1)S(1)}, bf16[8,64,1536]{2,1,0:T(8,128)(2,1)S(1)}, u32[]{:S(2)}, u32[]{:S(2)}) collective-permute-start(bf16[8,64,1536]{2,1,0:T(8,128)(2,1)S(1)} %dynamic-slice_bitcast_fusion.2), channel_id=1, source_target_pairs={{0,8},{1,9},{2,10},{3,11},{4,12},{5,13},{6,14},{7,15},{8,0},{9,1},... | collective-permute-start | bytes 4718600 | tf_op jit(solution)/shard_map/ppermute | solution.py:534
  458.9 19.8 %collective-permute-start.70 = (bf16[64,4096]{1,0:T(8,128)(2,1)S(1)}, bf16[64,4096]{1,0:T(8,128)(2,1)S(1)}, u32[]{:S(2)}, u32[]{:S(2)}) collective-permute-start(bf16[64,4096]{1,0:T(8,128)(2,1)S(1)} %fusion.5), channel_id=1, source_target_pairs={{0,16},{1,17},{2,18},{3,19},{4,20},{5,21},{6,22},{7,23},{8,24},{9,... | collective-permute-start | bytes 1572872 | tf_op jit(solution)/shard_map/ppermute | solution.py:534
  479.9 22.5 %collective-permute-start.77 = (bf16[256,1024]{1,0:T(8,128)(2,1)}, bf16[256,1024]{1,0:T(8,128)(2,1)}, u32[]{:S(2)}, u32[]{:S(2)}) collective-permute-start(bf16[256,1024]{1,0:T(8,128)(2,1)} %add_convert_fusion.3), channel_id=1, source_target_pairs={{0,8},{1,9},{2,10},{3,11},{4,12},{5,13},{6,14},{7,15},{8,0},{9,1},... | collective-permute-start | bytes 1572872 | tf_op jit(solution)/shard_map/ppermute | solution.py:534
  480.9 21.6 %collective-permute-start.78 = (bf16[64,4096]{1,0:T(8,128)(2,1)}, bf16[64,4096]{1,0:T(8,128)(2,1)}, u32[]{:S(2)}, u32[]{:S(2)}) collective-permute-start(bf16[64,4096]{1,0:T(8,128)(2,1)} %add_convert_fusion.2), channel_id=1, source_target_pairs={{0,8},{1,9},{2,10},{3,11},{4,12},{5,13},{6,14},{7,15},{8,0},{9,1},... | collective-permute-start | bytes 1572872 | tf_op jit(solution)/shard_map/ppermute | solution.py:534
  503.9 21.1 %collective-permute-start.86 = (bf16[64,1536]{1,0:T(8,128)(2,1)S(1)}, bf16[64,1536]{1,0:T(8,128)(2,1)S(1)}, u32[]{:S(2)}, u32[]{:S(2)}) collective-permute-start(bf16[64,1536]{1,0:T(8,128)(2,1)S(1)} %get-tuple-element.346), channel_id=1, source_target_pairs={{0,2},{2,4},{4,6},{6,7},{7,5},{5,3},{3,1},{1,0},{8,9},{10,8},{12,1... | collective-permute-start | bytes 589832 | tf_op jit(solution)/shard_map/ppermute | solution.py:527
  505.0 20.0 %collective-permute-start.87 = (bf16[64,1536]{1,0:T(8,128)(2,1)S(1)}, bf16[64,1536]{1,0:T(8,128)(2,1)S(1)}, u32[]{:S(2)}, u32[]{:S(2)}) collective-permute-start(bf16[64,1536]{1,0:T(8,128)(2,1)S(1)} %get-tuple-element.345), channel_id=1, source_target_pairs={{0,1},{2,0},{4,2},{6,4},{7,6},{5,7},{3,5},{1,3},{8,10},{10,12},{12... | collective-permute-start | bytes 589832 | tf_op jit(solution)/shard_map/ppermute | solution.py:527
  (188 other events, 1817.2 us)
Sparse Core Ops, SparseCore 0:
  19.2 85.3 all-gather.2
  108.0 80.4 all-gather.4
  301.6 97.6 reduce-scatter.1
